TPU v7x, 32 devices: a whole 2x2x4 slice. The times are simulated.
32 devices in a mesh: dp: 16 (over z, y, core), mp: 2 (over x).
Axes of the slice: x: 2, y: 2, z: 4, core: 2. Of those that a mesh axis runs over, the one named last changes fastest.
Arguments:
- inputs: bfloat16 [26624, 1024], P(('dp', 'mp')), may hold values from -6 to 6
- qkv_weight: bfloat16 [1, 3, 1024, 1024], P(None, None, None, 'mp'), may hold values from -0.1875 to 0.1875
- qv_bias: float32 [1, 2, 1024], P(None, None, 'mp'), may hold values from -3 to 3
- out_weight: bfloat16 [1, 1024, 1024], P(None, 'mp'), may hold values from -1.5 to 1.5
- out_bias: float32 [1, 1024], replicated, may hold values from -3 to 3
- norm_gain: float32 [1, 2, 1024], replicated, may hold values from 0.1 to 1.9
- norm_shift: float32 [1, 2, 1024], replicated, may hold values from -3 to 3
- up_weight: bfloat16 [1, 1024, 4096], P(None, None, 'mp'), may hold values from -0.1875 to 0.1875
- up_bias: float32 [1, 4096], P(None, 'mp'), may hold values from -3 to 3
- down_weight: bfloat16 [1, 4096, 1024], P(None, 'mp'), may hold values from -0.09375 to 0.09375
- down_bias: float32 [1, 1024], replicated, may hold values from -3 to 3
- cotangent: bfloat16 [26624, 1024], P(('dp', 'mp')), may hold values from -6 to 6
Outputs:
- output: float32 [26624, 1024], P(('dp', 'mp'))
- input_grad: float32 [26624, 1024], P(('dp', 'mp'))
- qkv_weight_grad: float32 [1, 3, 1024, 1024], P(None, None, None, 'mp')
- qv_bias_grad: float32 [1, 2, 1024], P(None, None, 'mp')
- out_weight_grad: float32 [1, 1024, 1024], P(None, 'mp')
- out_bias_grad: float32 [1, 1024], replicated
- norm_gain_grad: float32 [1, 2, 1024], replicated
- norm_shift_grad: float32 [1, 2, 1024], replicated
- up_weight_grad: float32 [1, 1024, 4096], P(None, None, 'mp')
- up_bias_grad: float32 [1, 4096], P(None, 'mp')
- down_weight_grad: float32 [1, 4096, 1024], P(None, 'mp')
- down_bias_grad: float32 [1, 1024], replicated
All inputs are finite; a program needn't handle non-finite values.
Results may differ from a plain program's by a relative error of at most 0.013.
The roundings to bfloat16 on the way count: a program that leaves them out, or rounds other values in their place, can miss the bound.
Values may be sent and summed in bfloat16 or wider, within the bound.
No kernel may reach another device: no remote copies, remote signals or barrier semaphores. Data moves between devices by JAX's collectives and lax.ppermute only.
A program may use at most 192 MiB of HBM per device.

v0:
```python
import jax
import jax.numpy as jnp
from jax import lax
from jax.sharding import PartitionSpec as P

HEAD = 64
PAGE = 416


EPSILON = 1e-05


def norm_rows(matrix, norm_scale, norm_offset):
    average = jnp.mean(matrix, axis=-1, keepdims=True)
    centered = matrix - average
    variance = jnp.mean(centered * centered, axis=-1, keepdims=True)
    return centered * lax.rsqrt(variance + EPSILON) * norm_scale + norm_offset


def exact_gelu(matrix):
    return jax.nn.gelu(matrix, approximate=False)


def spread_rows(rows_low, project):
    return project(lax.all_gather(rows_low, "mp", axis=0, tiled=True), jnp.int32(0))


def sum_rows(term, shard_rows):
    return lax.psum_scatter(
        term(jnp.int32(0), lax.axis_size("mp") * shard_rows), "mp", scatter_dimension=0, tiled=True
    )


def grad_fold(portion, acts, weight):
    weight_grad = lax.dot_general(
        acts, portion, (((0,), (0,)), ((), ())), preferred_element_type=jnp.float32
    )
    product = lax.dot_general(
        portion, weight, (((1,), (1,)), ((), ())), preferred_element_type=jnp.float32
    )
    return (product, weight_grad)


def spread_grads(grad_low, acts, weight):
    return grad_fold(lax.all_gather(grad_low, "mp", axis=0, tiled=True), acts=acts, weight=weight)


def sum_grads(term, shard_rows):
    return lax.psum_scatter(
        term(jnp.int32(0), lax.axis_size("mp") * shard_rows), "mp", scatter_dimension=0, tiled=True
    )


def page_forward(page_items):
    queries, key_rows, values = page_items
    scores = jnp.einsum("qhd,khd->hqk", queries, key_rows, preferred_element_type=jnp.float32)
    row_max = jnp.max(scores, axis=-1, keepdims=True)
    exponent = jnp.exp(scores - row_max)
    denominator = jnp.sum(exponent, axis=-1, keepdims=True)
    weights_low = (exponent / denominator).astype(jnp.bfloat16)
    log_total = row_max + jnp.log(denominator)
    attended = jnp.einsum("hqk,khd->qhd", weights_low, values, preferred_element_type=jnp.float32)
    return (attended.astype(jnp.bfloat16), log_total)


def page_backward(page_items):
    queries, key_rows, values, log_total, grad_mix = page_items
    scores = jnp.einsum("qhd,khd->hqk", queries, key_rows, preferred_element_type=jnp.float32)
    probability = jnp.exp(scores - log_total)
    weights_low = probability.astype(jnp.bfloat16)
    grad_prob = jnp.einsum("qhd,khd->hqk", grad_mix, values, preferred_element_type=jnp.float32)
    inner_total = jnp.sum(probability * grad_prob, axis=-1, keepdims=True)
    grad_scores = (probability * (grad_prob - inner_total)).astype(jnp.bfloat16)
    grad_q = jnp.einsum("hqk,khd->qhd", grad_scores, key_rows, preferred_element_type=jnp.float32)
    grad_k = jnp.einsum("hqk,qhd->khd", grad_scores, queries, preferred_element_type=jnp.float32)
    grad_v = jnp.einsum("hqk,qhd->khd", weights_low, grad_mix, preferred_element_type=jnp.float32)
    return (grad_q.astype(jnp.bfloat16), grad_k.astype(jnp.bfloat16), grad_v.astype(jnp.bfloat16))


def layer_forward(x_shard, params):
    qkv_w, qv_b, out_w, out_b, gains, shifts, up_w, up_b, down_w, down_b = params
    shard_rows = x_shard.shape[0]

    def project_qkv(portion, offset):
        return (
            jnp.einsum("rd,kde->rke", portion, qkv_w, preferred_element_type=jnp.float32),
            portion,
        )

    qkv_all, x_all = spread_rows(x_shard.astype(jnp.bfloat16), project_qkv)
    token_count = qkv_all.shape[0]
    local_width = qkv_all.shape[2]
    layout = (token_count // PAGE, PAGE, local_width // HEAD, HEAD)
    queries = ((qkv_all[:, 0] + qv_b[0]) * 0.125).astype(jnp.bfloat16).reshape(layout)
    key_rows = qkv_all[:, 1].astype(jnp.bfloat16).reshape(layout)
    values = (qkv_all[:, 2] + qv_b[1]).astype(jnp.bfloat16).reshape(layout)
    attended, log_total = lax.map(jax.checkpoint(page_forward), (queries, key_rows, values))
    attended = attended.reshape(token_count, local_width)

    def project_out(offset, amount):
        return jnp.dot(attended, out_w, preferred_element_type=jnp.float32)

    pre_first = x_shard + sum_rows(project_out, shard_rows) + out_b
    hidden = norm_rows(pre_first, gains[0], shifts[0])

    def project_up(portion, offset):
        return (jnp.dot(portion, up_w, preferred_element_type=jnp.float32), portion)

    pre_gelu, hidden_all = spread_rows(hidden.astype(jnp.bfloat16), project_up)
    pre_gelu = pre_gelu + up_b
    active = exact_gelu(pre_gelu).astype(jnp.bfloat16)

    def project_down(offset, amount):
        return jnp.dot(active, down_w, preferred_element_type=jnp.float32)

    pre_second = hidden + sum_rows(project_down, shard_rows) + down_b
    layer_out = norm_rows(pre_second, gains[1], shifts[1])
    stored = (
        x_shard,
        x_all,
        queries,
        key_rows,
        values,
        log_total,
        attended,
        pre_first,
        hidden_all,
        pre_gelu,
        active,
        pre_second,
        out_w,
    )
    return (layer_out, stored)


def layer_backward(grad_out, stored, params):
    qkv_w, qv_b, out_w, out_b, gains, shifts, up_w, up_b, down_w, down_b = params
    (
        x_shard,
        x_all,
        queries,
        key_rows,
        values,
        log_total,
        attended,
        pre_first,
        hidden_all,
        pre_gelu,
        active,
        pre_second,
        out_full,
    ) = stored
    shard_rows = grad_out.shape[0]
    norm_result, norm_back = jax.vjp(norm_rows, pre_second, gains[1], shifts[1])
    grad_second, gain_two, shift_two = norm_back(grad_out)
    grad_down_bias = jnp.sum(grad_second, axis=0)
    grad_active, grad_down = spread_grads(grad_second.astype(jnp.bfloat16), active, down_w)
    gelu_result, gelu_back = jax.vjp(exact_gelu, pre_gelu)
    grad_pre_low = gelu_back(grad_active)[0].astype(jnp.bfloat16)
    grad_up_bias = jnp.sum(grad_pre_low.astype(jnp.float32), axis=0)
    grad_up = lax.dot_general(
        hidden_all, grad_pre_low, (((0,), (0,)), ((), ())), preferred_element_type=jnp.float32
    )

    def back_up(offset, amount):
        return lax.dot_general(
            grad_pre_low, up_w, (((1,), (1,)), ((), ())), preferred_element_type=jnp.float32
        )

    grad_hidden = grad_second + sum_grads(back_up, shard_rows)
    norm_result, norm_back = jax.vjp(norm_rows, pre_first, gains[0], shifts[0])
    grad_first, gain_one, shift_one = norm_back(grad_hidden)
    grad_out_bias = jnp.sum(grad_first, axis=0)
    grad_first_low = grad_first.astype(jnp.bfloat16)
    grad_attended, grad_out_w = spread_grads(grad_first_low, attended, out_w)
    token_count = grad_attended.shape[0]
    local_width = grad_attended.shape[1]
    grad_mix = grad_attended.astype(jnp.bfloat16).reshape(queries.shape)
    grad_q, grad_k, grad_v = lax.map(
        jax.checkpoint(page_backward), (queries, key_rows, values, log_total, grad_mix)
    )
    flat_q = grad_q.reshape(token_count, local_width) * 0.125
    flat_k = grad_k.reshape(token_count, local_width)
    flat_v = grad_v.reshape(token_count, local_width)
    grad_qkv = jnp.stack([flat_q, flat_k, flat_v], axis=1)
    grad_qv_bias = jnp.stack(
        [jnp.sum(flat_q.astype(jnp.float32), axis=0), jnp.sum(flat_v.astype(jnp.float32), axis=0)]
    )
    grad_qkv_w = jnp.einsum("rd,rke->kde", x_all, grad_qkv, preferred_element_type=jnp.float32)

    def back_qkv(offset, amount):
        return jnp.einsum("rke,kde->rd", grad_qkv, qkv_w, preferred_element_type=jnp.float32)

    grad_x = grad_first + sum_grads(back_qkv, shard_rows)
    split_grads = (grad_qkv_w, grad_qv_bias, grad_out_w, grad_up, grad_up_bias, grad_down)
    shared_grads = (
        grad_out_bias,
        jnp.stack([gain_one, gain_two]),
        jnp.stack([shift_one, shift_two]),
        grad_down_bias,
    )
    return (grad_x, split_grads, shared_grads)


def body(
    inputs,
    qkv_weight,
    qv_bias,
    out_weight,
    out_bias,
    norm_gain,
    norm_shift,
    up_weight,
    up_bias,
    down_weight,
    down_bias,
    cotangent,
):
    layer_total = qkv_weight.shape[0]

    def params_of(layer_number):
        return (
            qkv_weight[layer_number],
            qv_bias[layer_number],
            out_weight[layer_number],
            out_bias[layer_number],
            norm_gain[layer_number],
            norm_shift[layer_number],
            up_weight[layer_number],
            up_bias[layer_number],
            down_weight[layer_number],
            down_bias[layer_number],
        )

    current = inputs.astype(jnp.float32)
    layer_number = 0
    layer_in = current
    current, stored = layer_forward(current, params_of(layer_number))
    kept_list = [layer_in]
    grad_rows = cotangent.astype(jnp.float32)
    split_list = []
    shared_list = []
    for layer_number in reversed(range(layer_total)):
        stored = layer_forward(kept_list[layer_number], params_of(layer_number))[1]
        grad_rows, split_grads, shared_grads = layer_backward(
            grad_rows, stored, params_of(layer_number)
        )
        qkv_part, bias_part, out_part, up_part, upb_part, down_part = split_grads
        split_grads = lax.psum((qkv_part, bias_part, out_part, up_part, upb_part, down_part), "dp")
        outb_part, gain_part, shift_part, downb_part = shared_grads
        shared_grads = lax.psum((outb_part, gain_part, shift_part, downb_part), ("dp", "mp"))
        split_list.insert(0, split_grads)
        shared_list.insert(0, shared_grads)
    split_all = tuple((jnp.stack([entry[member] for entry in split_list]) for member in range(6)))
    shared_all = tuple((jnp.stack([entry[member] for entry in shared_list]) for member in range(4)))
    return (
        current,
        grad_rows,
        split_all[0],
        split_all[1],
        split_all[2],
        shared_all[0],
        shared_all[1],
        shared_all[2],
        split_all[3],
        split_all[4],
        split_all[5],
        shared_all[3],
    )


def solution(mesh):
    placed = (
        P(("dp", "mp"), None),
        P(None, None, None, "mp"),
        P(None, None, "mp"),
        P(None, "mp", None),
        P(),
        P(),
        P(),
        P(None, None, "mp"),
        P(None, "mp"),
        P(None, "mp", None),
        P(),
        P(("dp", "mp"), None),
    )
    return jax.shard_map(
        body,
        mesh=mesh,
        in_specs=placed,
        out_specs=(
            P(("dp", "mp"), None),
            P(("dp", "mp"), None),
            P(None, None, None, "mp"),
            P(None, None, "mp"),
            P(None, "mp", None),
            P(),
            P(),
            P(),
            P(None, None, "mp"),
            P(None, "mp"),
            P(None, "mp", None),
            P(),
        ),
        check_vma=False,
    )
```

profile of v0, /device:TPU:0, one launch (start us, length us, event | category | flops | bytes accessed | tf_op | source)
XLA Modules:
  0.0 1571.4 jit_solution(18243817031159209131)
XLA Ops:
  9.0 51.2 %all-gather.6.cloned.1.call-done = bf16[1664,1024]{1,0:T(8,128)(2,1)} async-done(((bf16[832,1024]{1,0:T(8,128)(2,1)}), bf16[1664,1024]{1,0:T(8,128)(2,1)}) %all-gather.6.cloned.1.call-update) | async-done | bytes 3407888 | tf_op jit(solution)/shard_map/all_gather | solution.py:25
  60.2 7.5 fusion.165
  77.6 6.9 squeeze.71
  93.8 6.9 squeeze.72
  105.2 5.4 reshape.214
  117.2 32.2 %while.36 = (s32[]{:T(128)}, bf16[4,416,8,64]{1,3,2,0:T(8,128)(2,1)}, bf16[4,416,8,64]{1,3,2,0:T(8,128)(2,1)}, bf16[4,416,8,64]{1,3,2,0:T(8,128)(2,1)}, bf16[4,416,8,64]{1,3,2,0:T(8,128)(2,1)}, /*index=5*/s32[]{:T(128)}) while((s32[]{:T(128)}, bf16[4,416,8,64]{1,3,2,0:T(8,128)(2,1)}, bf16[4,416,8,64]{1,3,2,0:T(8,128)(2,1)}, ...), condition=%wide.region_3.4_spmd, body=%wide.region_0.3_spmd.sunk | while | flops 538767424 | bytes 3175493 | solution.py:97
  158.8 6.6 fusion.177
  167.0 28.6 %while.37 = (s32[]{:T(128)}, bf16[4,416,8,64]{1,3,2,0:T(8,128)(2,1)}, f32[4,8,416,1]{2,1,3,0:T(8,128)}, bf16[4,416,8,64]{1,3,2,0:T(8,128)(2,1)}, bf16[4,416,8,64...) while((s32[]{:T(128)}, bf16[4,416,8,64]{1,3,2,0:T(8,128)(2,1)}, ...), condition=%wide.region_13.14_spmd, body=%wide.region_10.13_spmd.sunk | while | flops 362935040 | bytes 18822732 | solution.py:97
  205.1 6.6 fusion.175
  213.6 34.8 %reduce-scatter.7.cloned.1.call-done = f32[832,1024]{1,0:T(8,128)} async-done(((f32[1664,1024]{1,0:T(8,128)}), f32[832,1024]{1,0:T(8,128)}) %reduce-scatter.7.cloned.1.call-update) | async-done | bytes 3407888 | tf_op jit(solution)/shard_map/reduce_scatter | solution.py:29
  251.4 82.7 %reduce-scatter.11.cloned.1.call-done = f32[832,1024]{1,0:T(8,128)} async-done(((f32[1664,1024]{1,0:T(8,128)}), f32[832,1024]{1,0:T(8,128)}) %reduce-scatter.11.cloned.1.call-update) | async-done | bytes 3407888 | tf_op jit(solution)/shard_map/reduce_scatter | solution.py:29
  334.1 5.1 fusion.216
  345.9 47.4 %all-gather.10.cloned.1.call-done = bf16[1664,1024]{1,0:T(8,128)(2,1)} async-done(((bf16[832,1024]{1,0:T(8,128)(2,1)}), bf16[1664,1024]{1,0:T(8,128)(2,1)}) %all-gather.10.cloned.1.call-update) | async-done | bytes 3407888 | tf_op jit(solution)/shard_map/all_gather | solution.py:25
  393.3 40.0 %multiply_convert_fusion.1 = (bf16[1664,2048]{1,0:T(8,128)(2,1)S(1)}, f32[1664,2048]{1,0:T(8,128)}, f32[1664,2048]{1,0:T(8,128)}) fusion(f32[2048]{0:T(1024)S(1)} %bitcast.283, bf16[1664,1024]{1,0:T(8,128)(2,1)} %all-gather.10.cloned.1.call-done, bf16[1,1024,2048]{2,1,0:T(8,128)(2,1)} %param.25), kind=kOutput, calls=%fused_computation.86 | convolution fusion | flops 7204241408 | bytes 41689088 | tf_op jit(solution)/shard_map/dot_general | solution.py:107
  436.0 9.2 fusion.146
  445.3 38.0 %fusion.98.clone.4 = bf16[1664,2048]{1,0:T(8,128)(2,1)S(1)} fusion(bf16[1664,1024]{1,0:T(8,128)(2,1)} %all-gather.8.cloned.1.call-done, f32[2048]{0:T(1024)S(1)} %bitcast.284, bf16[1,1024,2048]{2,1,0:T(8,128)(2,1)} %param.25), kind=kOutput, calls=%fused_computation.82.clone.clone.clone.1 | convolution fusion | flops 7204241408 | bytes 14426112 | tf_op jit(solution)/shard_map/dot_general | solution.py:107
  483.3 9.2 fusion.112
  492.6 36.0 %reduce-scatter.13.cloned.1.call-done = f32[832,1024]{1,0:T(8,128)} async-done(((f32[1664,1024]{1,0:T(8,128)}), f32[832,1024]{1,0:T(8,128)}) %reduce-scatter.13.cloned.1.call-update) | async-done | bytes 3407888 | tf_op jit(solution)/shard_map/reduce_scatter | solution.py:29
  528.7 85.8 %reduce-scatter.9.cloned.1.call-done = f32[832,1024]{1,0:T(8,128)} async-done(((f32[1664,1024]{1,0:T(8,128)}), f32[832,1024]{1,0:T(8,128)}) %reduce-scatter.9.cloned.1.call-update) | async-done | bytes 3407888 | tf_op jit(solution)/shard_map/reduce_scatter | solution.py:29
  614.5 7.1 fusion.214
  632.1 48.0 %all-gather.12.cloned.1.call-done = bf16[1664,1024]{1,0:T(8,128)(2,1)} async-done(((bf16[832,1024]{1,0:T(8,128)(2,1)}), bf16[1664,1024]{1,0:T(8,128)(2,1)}) %all-gather.12.cloned.1.call-update) | async-done | bytes 3407888 | tf_op jit(solution)/shard_map/all_gather | solution.py:45
  680.1 23.2 %convert_reduce_fusion = (f32[2048]{0:T(1024)}, bf16[1664,2048]{1,0:T(8,128)(2,1)}) fusion(f32[1664,2048]{1,0:T(8,128)} %get-tuple-element.257, bf16[1664,1024]{1,0:T(8,128)(2,1)} %all-gather.12.cloned.1.call-done, bf16[1,2048,1024]{2,1,0:T(8,128)(2,1)} %param.27, f32[1664,2048]{1,0:T(8,128)} %get-tuple-element.282, f32[2048]{0:T(1024)S(1)} %bitcast.285), kind=kOutput, calls=%fused_computation.84 | convolution fusion | flops 7037253632 | bytes 41697280 | tf_op jit(solution)/shard_map/dot_general | solution.py:38
  703.3 12.4 fusion.151
  715.8 82.9 %reduce-scatter.15.cloned.1.call-done = f32[832,1024]{1,0:T(8,128)} async-done(((f32[1664,1024]{1,0:T(8,128)}), f32[832,1024]{1,0:T(8,128)}) %reduce-scatter.15.cloned.1.call-update) | async-done | bytes 3407888 | tf_op jit(solution)/shard_map/reduce_scatter | solution.py:49
  798.6 6.1 multiply_reduce_fusion.1
  809.7 13.4 convolution_bitcast_fusion.2
  823.1 12.2 convolution_bitcast_fusion
  835.3 22.3 %all-gather.14.cloned.1.call-done = bf16[1664,1024]{1,0:T(8,128)(2,1)} async-done(((bf16[832,1024]{1,0:T(8,128)(2,1)}), bf16[1664,1024]{1,0:T(8,128)(2,1)}) %all-gather.14.cloned.1.call-update) | async-done | bytes 3407888 | tf_op jit(solution)/shard_map/all_gather | solution.py:45
  857.7 5.4 convolution_convert_fusion.2
  863.1 5.4 reshape.210
  868.5 5.0 copy.59
  878.2 83.8 %while.38 = (s32[]{:T(128)}, bf16[4,416,8,64]{1,3,2,0:T(8,128)(2,1)}, bf16[4,416,8,64]{1,3,2,0:T(8,128)(2,1)}, bf16[4,416,8,64]{1,3,2,0:T(8,128)(2,1)}, bf16[4,4...) while((s32[]{:T(128)}, ...), condition=%wide.region_27.28_spmd, body=%wide.region_25.27_spmd.sunk | while | flops 899142400 | bytes 56252548 | solution.py:179
  881.6 5.4 multiply_reduce_fusion.8
  902.5 5.4 multiply_reduce_fusion.8
  923.4 5.4 multiply_reduce_fusion.8
  944.3 5.4 multiply_reduce_fusion.8
  969.9 5.7 reshape.211
  983.2 5.7 reshape.212
  993.7 5.9 reshape.213
  1008.2 7.9 fusion.170
  1016.1 10.0 convolution_bitcast_fusion.1
  1026.9 42.1 %all-reduce = (f32[1,1024]{1,0:T(1,128)}, f32[1,2,1024]{2,1,0:T(2,128)}, f32[1,2,1024]{2,1,0:T(2,128)}, f32[1,1024]{1,0:T(1,128)}) all-reduce(f32[1,1024]{1,0:T(1,128)S(1)} %bitcast.279, f32[1,2,1024]{2,1,0:T(2,128)S(1)} %maximum_bitcast_fusion, ...), channel_id=1, replica_groups=mesh['dp'=16,'mp'=2] {'dp','mp'}, use_global_device_ids=true, to_apply=%region_35.36 | all-reduce | flops 6144 | bytes 49152 | tf_op jit(solution)/shard_map/psum | solution.py:251
  1073.4 63.5 %all-reduce.1 = (f32[1,2,512]{2,1,0:T(2,128)}, f32[1,2048]{1,0:T(1,128)}) all-reduce(f32[1,2,512]{2,1,0:T(2,128)S(1)} %maximum_bitcast_fusion.2, f32[1,2048]{1,0:T(1,128)S(1)} %bitcast.281), channel_id=1, replica_groups=mesh['dp'=16,'mp'=2] {'dp'}, use_global_device_ids=true, to_apply=%region_32.33 | all-reduce | flops 3072 | bytes 24576 | tf_op jit(solution)/shard_map/psum | solution.py:249
  1136.9 323.8 %all-reduce.5.cloned.1.call-done = (f32[1,3,1024,512]{2,3,1,0:T(8,128)}, f32[1,512,1024]{2,1,0:T(8,128)}, f32[1,1024,2048]{2,1,0:T(8,128)}, f32[1,2048,1024]{2,1,0:T(8,128)}) async-done(((f32[1,3,1024,512]{2,3,1,0:T(8,128)}, f32[1,512,1024]{2,1,0:T(8,128)}, f32[1,1024,2048]{2,1,0:T(8,128)}, f32[1,2048,1024]{2,1,0:T(8,128)}), (f32[1,3,1024,512]{2,3,1,0:T(8,128)}, f32[1,512,1024]{2,1,0:T(8,128)}, ...) | async-done | bytes 25165840 | tf_op jit(solution)/shard_map/psum | solution.py:249
  1460.7 6.6 copy.68
  1467.3 78.2 %reduce-scatter.17.cloned.1.call-done = f32[832,1024]{1,0:T(8,128)} async-done(((f32[1664,1024]{1,0:T(8,128)}), f32[832,1024]{1,0:T(8,128)}) %reduce-scatter.17.cloned.1.call-update) | async-done | bytes 3407888 | tf_op jit(solution)/shard_map/reduce_scatter | solution.py:49
  1545.5 5.3 add_add_fusion.4
  1552.1 8.6 copy.127
  (246 shorter events, 247.9 us)
Async XLA Ops:
  7.2 53.0 %copy-start = (bf16[1,3,1024,512]{3,2,1,0:T(8,128)(2,1)S(1)}, bf16[1,3,1024,512]{3,2,1,0:T(8,128)(2,1)}, u32[]{:S(2)}) copy-start(bf16[1,3,1024,512]{3,2,1,0:T(8,128)(2,1)} %param.19) | copy-start | bytes 9437188
  7.2 53.0 %all-gather.6.cloned.1.call-start = ((), (), s32[]{:S(2)}) async-start(), calls=%async_computation.6 | async-start | bytes 5111808 | tf_op jit(solution)/shard_map/all_gather | solution.py:25
  7.9 240.4 %reduce-scatter.7.cloned.1.call-start = ((), (), s32[]{:S(2)}) async-start(), calls=%async_computation.7 | async-start | bytes 10223616 | tf_op jit(solution)/shard_map/reduce_scatter | solution.py:29
  165.4 168.7 %reduce-scatter.11.cloned.1.call-start = ((), (), s32[]{:S(2)}) async-start(), calls=%async_computation.10 | async-start | bytes 10223616 | tf_op jit(solution)/shard_map/reduce_scatter | solution.py:29
  211.6 36.7 %copy-start.19 = (f32[1,1024]{1,0:T(1,128)S(1)}, f32[1,1024]{1,0:T(1,128)}, u32[]{:S(2)}) copy-start(f32[1,1024]{1,0:T(1,128)} %param.22) | copy-start | bytes 12292
  211.7 181.6 %all-gather.10.cloned.1.call-start = ((), (), s32[]{:S(2)}) async-start(), calls=%async_computation.11 | async-start | bytes 5111808 | tf_op jit(solution)/shard_map/all_gather | solution.py:25
  212.9 127.4 %copy-start.17 = (f32[1,1,1024]{2,1,0:T(1,128)}, f32[1,1,1024]{2,1,0:T(1,128)S(1)}, u32[]{:S(2)}) copy-start(f32[1,1,1024]{2,1,0:T(1,128)S(1)} %get-tuple-element.278) | copy-start | bytes 12292
  213.6 126.8 %copy-start.25 = (f32[1,1,1024]{2,1,0:T(1,128)}, f32[1,1,1024]{2,1,0:T(1,128)S(1)}, u32[]{:S(2)}) copy-start(f32[1,1,1024]{2,1,0:T(1,128)S(1)} %get-tuple-element.280) | copy-start | bytes 12292
  251.4 89.0 %copy-start.21 = (f32[832]{0:T(1024)}, f32[832]{0:T(1024)S(1)}, u32[]{:S(2)}) copy-start(f32[832]{0:T(1024)S(1)} %broadcast_multiply_fusion.4) | copy-start | bytes 9988
  334.1 6.3 copy-start.4
  339.2 6.0 copy-start.1
  339.2 3.2 copy-start.3
  339.2 5.9 copy-start.13
  339.2 5.9 copy-start.27
  340.4 4.8 copy-start.15
  345.2 48.1 %copy-start.48 = (f32[1,2048]{1,0:T(1,128)S(1)}, f32[1,2048]{1,0:T(1,128)}, u32[]{:S(2)}) copy-start(f32[1,2048]{1,0:T(1,128)} %param.26) | copy-start | bytes 24580
  345.2 100.0 %all-gather.8.cloned.1.call-start = ((), (), s32[]{:S(2)}) async-start(), calls=%async_computation.8 | async-start | bytes 5111808 | tf_op jit(solution)/shard_map/all_gather | solution.py:25
  345.8 182.9 %reduce-scatter.13.cloned.1.call-start = ((), (), s32[]{:S(2)}) async-start(), calls=%async_computation.12 | async-start | bytes 10223616 | tf_op jit(solution)/shard_map/reduce_scatter | solution.py:29
  393.3 42.7 %copy-start.43 = (bf16[1,2048,1024]{2,1,0:T(8,128)(2,1)S(1)}, bf16[1,2048,1024]{2,1,0:T(8,128)(2,1)}, u32[]{:S(2)}) copy-start(bf16[1,2048,1024]{2,1,0:T(8,128)(2,1)} %param.27) | copy-start | bytes 12582916
  445.2 169.3 %reduce-scatter.9.cloned.1.call-start = ((), (), s32[]{:S(2)}) async-start(), calls=%async_computation.9 | async-start | bytes 10223616 | tf_op jit(solution)/shard_map/reduce_scatter | solution.py:29
  445.3 38.1 %copy-start.44 = (bf16[1,2048,1024]{2,1,0:T(8,128)(2,1)S(1)}, bf16[1,2048,1024]{2,1,0:T(8,128)(2,1)}, u32[]{:S(2)}) copy-start(bf16[1,2048,1024]{2,1,0:T(8,128)(2,1)} %param.27) | copy-start | bytes 12582916
  492.5 121.9 %copy-start.14 = (f32[832]{0:T(1024)S(1)}, f32[832]{0:T(1024)}, u32[]{:S(2)}) copy-start(f32[832]{0:T(1024)} %copy-done.13) | copy-start | bytes 9988
  492.5 121.9 %copy-start.16 = (f32[832]{0:T(1024)S(1)}, f32[832]{0:T(1024)}, u32[]{:S(2)}) copy-start(f32[832]{0:T(1024)} %copy-done.15) | copy-start | bytes 9988
  492.5 121.9 %copy-start.18 = (f32[1,1,1024]{2,1,0:T(1,128)S(1)}, f32[1,1,1024]{2,1,0:T(1,128)}, u32[]{:S(2)}) copy-start(f32[1,1,1024]{2,1,0:T(1,128)} %copy-done.17) | copy-start | bytes 12292
  492.5 121.9 %copy-start.20 = (f32[1,1024]{1,0:T(1,128)S(1)}, f32[1,1024]{1,0:T(1,128)}, u32[]{:S(2)}) copy-start(f32[1,1024]{1,0:T(1,128)} %param.22) | copy-start | bytes 12292
  492.5 121.9 %copy-start.22 = (f32[832]{0:T(1024)S(1)}, f32[832]{0:T(1024)}, u32[]{:S(2)}) copy-start(f32[832]{0:T(1024)} %copy-done.21) | copy-start | bytes 9988
  492.5 121.9 %copy-start.26 = (f32[1,1,1024]{2,1,0:T(1,128)S(1)}, f32[1,1,1024]{2,1,0:T(1,128)}, u32[]{:S(2)}) copy-start(f32[1,1,1024]{2,1,0:T(1,128)} %copy-done.25) | copy-start | bytes 12292
  492.5 121.9 %copy-start.28 = (f32[832]{0:T(1024)S(1)}, f32[832]{0:T(1024)}, u32[]{:S(2)}) copy-start(f32[832]{0:T(1024)} %copy-done.27) | copy-start | bytes 9988
  492.6 121.9 %copy-start.42 = (f32[1,1024]{1,0:T(1,128)S(1)}, f32[1,1024]{1,0:T(1,128)}, u32[]{:S(2)}) copy-start(f32[1,1024]{1,0:T(1,128)} %param.28) | copy-start | bytes 12292
  492.6 187.5 %all-gather.12.cloned.1.call-start = ((), (), s32[]{:S(2)}) async-start(), calls=%async_computation.13 | async-start | bytes 5111808 | tf_op jit(solution)/shard_map/all_gather | solution.py:45
  632.1 166.5 %reduce-scatter.15.cloned.1.call-start = ((), (), s32[]{:S(2)}) async-start(), calls=%async_computation.14 | async-start | bytes 10223616 | tf_op jit(solution)/shard_map/reduce_scatter | solution.py:49
  715.7 89.1 %copy-start.30 = (f32[832]{0:T(1024)S(1)}, f32[832]{0:T(1024)}, u32[]{:S(2)}) copy-start(f32[832]{0:T(1024)} %copy-done.29) | copy-start | bytes 9988
  715.7 142.0 %all-gather.14.cloned.1.call-start = ((), (), s32[]{:S(2)}) async-start(), calls=%async_computation.15 | async-start | bytes 5111808 | tf_op jit(solution)/shard_map/all_gather | solution.py:45
  798.6 6.2 copy-start.2
  805.8 3.8 copy-start.23
  809.7 651.0 %all-reduce.5.cloned.1.call-start = ((), (), s32[]{:S(2)}) async-start(), calls=%async_computation.17 | async-start | bytes 50331648 | tf_op jit(solution)/shard_map/psum | solution.py:249
  809.7 13.4 copy-start.47
  878.4 3.2 copy-start.7
  999.7 4.2 copy-start.11
  999.7 4.2 copy-start.46
  1003.9 3.5 copy-start.12
  1003.9 4.3 copy-start.45
  1016.1 529.4 %reduce-scatter.17.cloned.1.call-start = ((), (), s32[]{:S(2)}) async-start(), calls=%async_computation.16 | async-start | bytes 10223616 | tf_op jit(solution)/shard_map/reduce_scatter | solution.py:49
  1026.2 47.2 %copy-start.39 = (f32[2048]{0:T(1024)S(1)}, f32[2048]{0:T(1024)}, u32[]{:S(2)}) copy-start(f32[2048]{0:T(1024)} %get-tuple-element.283) | copy-start | bytes 24580
  1460.7 84.8 %copy-start.24 = (f32[832]{0:T(1024)S(1)}, f32[832]{0:T(1024)}, u32[]{:S(2)}) copy-start(f32[832]{0:T(1024)} %copy-done.23) | copy-start | bytes 9988
  1545.5 5.3 copy-start.10
  1550.8 9.9 slice-start
  1552.1 8.6 slice-start.1
  (19 other events, 30.9 us)
Sparse Core Ops, SparseCore 0:
  9.6 50.5 all-gather.5
  165.5 82.7 reduce-scatter.6
  251.3 82.7 reduce-scatter.10
  345.4 47.8 all-gather.9
  395.2 47.8 all-gather.7
  445.9 82.7 reduce-scatter.12
  531.7 82.7 reduce-scatter.8
  632.2 47.8 all-gather.11
  715.8 82.7 reduce-scatter.14
  809.8 47.8 all-gather.13
  1016.2 444.4 all-reduce.4
  1463.0 82.4 reduce-scatter.16
where the time goes:
time: 1580 us; the launch traced here: 1570 us
  waiting for transfers between devices  895 us (57%)
  matrix products  320 us (20%)
  local copies, waits for them, and re-layouts  155 us (10%)
  blocking collectives  106 us (7%)
  other arithmetic  80.2 us (5%)
    psum x1, waiting for transfers between devices, body(): lax.psum((qkv_part, bias_part, out_part, up_part, upb_part, down_part), '...  324 us
    reduce_scatter x4, waiting for transfers between devices, sum_rows(): lax.psum_scatter(term(jnp.int32(0), lax.axis_size('mp') * shard_rows), 'm...  239 us
    reduce_scatter x2, waiting for transfers between devices, sum_grads(): lax.psum_scatter(term(jnp.int32(0), lax.axis_size('mp') * shard_rows), 'm...  161 us
    all_gather x3, waiting for transfers between devices, spread_rows(): lax.all_gather(rows_low, 'mp', axis=0, tiled=True)  98.6 us
    dot_general x2, matrix products, project_up(): return (jnp.dot(portion, up_w, preferred_element_type=jnp.float32), portion)  78 us
    all_gather x2, waiting for transfers between devices, spread_grads(): lax.all_gather(grad_low, 'mp', axis=0, tiled=True)  70.3 us
    psum x1, blocking collectives, body(): lax.psum((qkv_part, bias_part, out_part, up_part, upb_part, down_part), '...  63.5 us
    psum x1, blocking collectives, body(): lax.psum((outb_part, gain_part, shift_part, downb_part), ('dp', 'mp'))  42.1 us
  transfers between devices with their start and end apart: 12, of which 11 were waited for; matrix products, arithmetic and copies ran while one was open for 12% of the time, Pallas kernels for 0%

commit v1 on v0

--- a/solution.py
+++ b/solution.py
@@ -1,14 +1,17 @@
 import jax
 import jax.numpy as jnp
 from jax import lax
+from jax.experimental import pallas as pl
+from jax.experimental.pallas import tpu as pltpu
 from jax.sharding import PartitionSpec as P
 
 HEAD = 64
 PAGE = 416
-
+LANES = 128
 
 EPSILON = 1e-05
-
+F32 = jnp.float32
+LOW = jnp.bfloat16
 
 def norm_rows(matrix, norm_scale, norm_offset):
     average = jnp.mean(matrix, axis=-1, keepdims=True)
@@ -202,7 +205,7 @@
     return (grad_x, split_grads, shared_grads)
 
 
-def body(
+def spread_body(
     inputs,
     qkv_weight,
     qv_bias,
@@ -269,6 +272,430 @@
     )
 
 
+RATE = 0.42
+POLY = (
+    0.23672758308126046,
+    0.24094666497815675,
+    0.18682847081810067,
+    0.2932523313321973,
+    -0.17452300094788806,
+    0.4864472432641871,
+    -0.34587320596419,
+    0.0761939461469462,
+)
+
+
+def gelu_pair(u):
+    magnitude = jnp.abs(u)
+    t = 1.0 / (1.0 + (RATE * 0.5**0.5) * magnitude)
+    total = jnp.full_like(u, 0.5 * POLY[-1])
+    for factor in POLY[-2::-1]:
+        total = total * t + 0.5 * factor
+    bell = jnp.exp(u * u * -0.5)
+    tail = total * t * bell
+    below = jnp.where(u >= 0, 1.0 - tail, tail)
+    return u * below, below + u * bell * 0.3989422804014327
+
+
+def matmul(left, right, left_dim=1, right_dim=0):
+    return lax.dot_general(
+        left, right, (((left_dim,), (right_dim,)), ((), ())), preferred_element_type=F32
+    )
+
+
+def head_mask(which):
+    lane = lax.broadcasted_iota(jnp.int32, (1, LANES), 1)
+    return (lane // HEAD) == which
+
+
+def attend_kernel(q_ref, k_ref, v_ref, o_ref, lse_ref):
+    queries, key_rows, values = q_ref[...], k_ref[...], v_ref[...]
+    values_t = values.T
+    columns = []
+    for which in range(LANES // HEAD):
+        keys_one = jnp.where(head_mask(which), key_rows, jnp.zeros_like(key_rows))
+        scores = matmul(keys_one, queries, 1, 1)
+        peak = jnp.max(scores, axis=0, keepdims=True)
+        exponent = jnp.exp(scores - peak)
+        denominator = jnp.sum(exponent, axis=0, keepdims=True)
+        weights_low = (exponent * (1.0 / denominator)).astype(LOW)
+        columns.append(matmul(values_t[which * HEAD : (which + 1) * HEAD], weights_low))
+        lse_ref[0, 0, which : which + 1, :] = peak + jnp.log(denominator)
+    o_ref[...] = jnp.concatenate(columns, axis=0).T.astype(LOW)
+
+
+def attend_back_kernel(q_ref, k_ref, v_ref, lse_ref, g_ref, dq_ref, dk_ref, dv_ref):
+    queries, key_rows, values, grads = q_ref[...], k_ref[...], v_ref[...], g_ref[...]
+    keys_t = key_rows.T
+    columns, dk_parts, dv_parts = [], [], []
+    for which in range(LANES // HEAD):
+        mask = head_mask(which)
+        keys_one = jnp.where(mask, key_rows, jnp.zeros_like(key_rows))
+        scores = matmul(keys_one, queries, 1, 1)
+        probability = jnp.exp(scores - lse_ref[0, 0, which : which + 1, :])
+        values_one = jnp.where(mask, values, jnp.zeros_like(values))
+        grad_prob = matmul(values_one, grads, 1, 1)
+        inner = jnp.sum(probability * grad_prob, axis=0, keepdims=True)
+        grad_scores = (probability * (grad_prob - inner)).astype(LOW)
+        dv_parts.append(matmul(probability.astype(LOW), grads))
+        dk_parts.append(matmul(grad_scores, queries))
+        columns.append(matmul(keys_t[which * HEAD : (which + 1) * HEAD], grad_scores))
+    first = head_mask(0)
+    dv_ref[...] = jnp.where(first, dv_parts[0], dv_parts[1]).astype(LOW)
+    dk_ref[...] = jnp.where(first, dk_parts[0], dk_parts[1]).astype(LOW)
+    grad_q = jnp.concatenate(columns, axis=0).T.astype(LOW)
+    dq_ref[...] = (grad_q.astype(F32) * 0.125).astype(LOW)
+
+
+def head_specs(count):
+    return [pl.BlockSpec((PAGE, LANES), lambda page, pair: (page, pair)) for _ in range(count)]
+
+
+def lse_spec():
+    return pl.BlockSpec((1, 1, LANES // HEAD, PAGE), lambda page, pair: (page, pair, 0, 0))
+
+
+def attend(queries, key_rows, values):
+    rows, width = queries.shape
+    pages, pairs = rows // PAGE, width // LANES
+    area = rows * PAGE * width
+    return pl.pallas_call(
+        attend_kernel,
+        grid=(pages, pairs),
+        in_specs=head_specs(3),
+        out_specs=head_specs(1) + [lse_spec()],
+        out_shape=[
+            jax.ShapeDtypeStruct((rows, width), LOW),
+            jax.ShapeDtypeStruct((pages, pairs, LANES // HEAD, PAGE), F32),
+        ],
+        compiler_params=pltpu.CompilerParams(vmem_limit_bytes=48 * 2**20),
+        cost_estimate=pl.CostEstimate(
+            flops=16 * area, bytes_accessed=8 * rows * width, transcendentals=area // HEAD
+        ),
+        name="attend",
+    )(queries, key_rows, values)
+
+
+def attend_back(queries, key_rows, values, lse, grads):
+    rows, width = queries.shape
+    pages, pairs = rows // PAGE, width // LANES
+    area = rows * PAGE * width
+    return pl.pallas_call(
+        attend_back_kernel,
+        grid=(pages, pairs),
+        in_specs=head_specs(3) + [lse_spec()] + head_specs(1),
+        out_specs=head_specs(3),
+        out_shape=[jax.ShapeDtypeStruct((rows, width), LOW)] * 3,
+        compiler_params=pltpu.CompilerParams(vmem_limit_bytes=48 * 2**20),
+        cost_estimate=pl.CostEstimate(
+            flops=40 * area, bytes_accessed=14 * rows * width, transcendentals=area // HEAD
+        ),
+        name="attend_back",
+    )(queries, key_rows, values, lse, grads)
+
+
+UNITS = 512
+
+
+def expand_kernel(h_ref, w_ref, b_ref, active_ref, slope_ref):
+    rows = h_ref.shape[0] // 4
+    for part in range(4):
+        span = slice(part * rows, (part + 1) * rows)
+        value, slope = gelu_pair(matmul(h_ref[span, :], w_ref[...]) + b_ref[...])
+        active_ref[span, :] = value.astype(LOW)
+        slope_ref[span, :] = slope.astype(LOW)
+
+
+def expand(hidden_low, weight, bias):
+    rows, depth = hidden_low.shape
+    units = weight.shape[1]
+    column = pl.BlockSpec((rows, UNITS), lambda step: (0, step))
+    return pl.pallas_call(
+        expand_kernel,
+        grid=(units // UNITS,),
+        in_specs=[
+            pl.BlockSpec((rows, depth), lambda step: (0, 0)),
+            pl.BlockSpec((depth, UNITS), lambda step: (0, step)),
+            pl.BlockSpec((1, UNITS), lambda step: (0, step)),
+        ],
+        out_specs=[column, column],
+        out_shape=[jax.ShapeDtypeStruct((rows, units), LOW)] * 2,
+        compiler_params=pltpu.CompilerParams(vmem_limit_bytes=48 * 2**20),
+        cost_estimate=pl.CostEstimate(
+            flops=4 * rows * depth * units,
+            bytes_accessed=2 * depth * units + 4 * rows * units,
+            transcendentals=2 * rows * units,
+        ),
+        name="expand",
+    )(hidden_low, weight, bias)
+
+
+def contract_back_kernel(g_ref, w_ref, slope_ref, out_ref, bias_ref):
+    rows = g_ref.shape[0] // 4
+    total = jnp.zeros(bias_ref.shape, F32)
+    for part in range(4):
+        span = slice(part * rows, (part + 1) * rows)
+        grad = matmul(g_ref[span, :], w_ref[...], 1, 1) * slope_ref[span, :].astype(F32)
+        grad_low = grad.astype(LOW)
+        out_ref[span, :] = grad_low
+        total = total + jnp.sum(grad_low.astype(F32), axis=0, keepdims=True)
+    bias_ref[...] = total
+
+
+def contract_back(grad_low, weight, slope):
+    rows, depth = grad_low.shape
+    units = weight.shape[0]
+    column = pl.BlockSpec((rows, UNITS), lambda step: (0, step))
+    return pl.pallas_call(
+        contract_back_kernel,
+        grid=(units // UNITS,),
+        in_specs=[
+            pl.BlockSpec((rows, depth), lambda step: (0, 0)),
+            pl.BlockSpec((UNITS, depth), lambda step: (step, 0)),
+            column,
+        ],
+        out_specs=[column, pl.BlockSpec((1, UNITS), lambda step: (0, step))],
+        out_shape=[
+            jax.ShapeDtypeStruct((rows, units), LOW),
+            jax.ShapeDtypeStruct((1, units), F32),
+        ],
+        compiler_params=pltpu.CompilerParams(vmem_limit_bytes=48 * 2**20),
+        cost_estimate=pl.CostEstimate(
+            flops=2 * rows * depth * units,
+            bytes_accessed=2 * depth * units + 4 * rows * units,
+            transcendentals=0,
+        ),
+        name="contract_back",
+    )(grad_low, weight, slope)
+
+
+def swap(value, distance, axis="dp"):
+    count = lax.axis_size(axis)
+    return lax.ppermute(value, axis, [(place, place ^ distance) for place in range(count)])
+
+
+def bit_of(place, distance):
+    return (place // distance) % 2
+
+
+def cut(value, number, count, axis):
+    size = value.shape[axis] // count
+    return lax.dynamic_slice_in_dim(value, number * size, size, axis)
+
+
+def ordered(bit, mine, theirs, axis):
+    return jnp.where(
+        bit == 0,
+        jnp.concatenate([mine, theirs], axis),
+        jnp.concatenate([theirs, mine], axis),
+    )
+
+
+SHARERS = (1, 2, 4)
+
+
+def fetch_other(weight, axis):
+    place = lax.axis_index("dp")
+    number = place % 8
+    piece = swap(cut(weight, number, 8, axis), 1, "mp")
+    beside = swap(piece, 2)
+    above = swap(piece, 4)
+    half = piece.shape[axis] // 2
+    low_part = swap(lax.slice_in_dim(beside, 0, half, axis=axis), 4)
+    high_part = swap(lax.slice_in_dim(above, half, 2 * half, axis=axis), 2)
+    across = jnp.concatenate([low_part, high_part], axis)
+    mine = jnp.concatenate([piece, beside, above, across], axis)
+    both = jnp.concatenate([mine, swap(mine, 1)], axis)
+    whole = both
+    size = piece.shape[axis]
+    for slot, relative in enumerate((0, 2, 4, 6, 1, 3, 5, 7)):
+        whole = lax.dynamic_update_slice_in_dim(
+            whole,
+            lax.slice_in_dim(both, slot * size, (slot + 1) * size, axis=axis),
+            (number ^ relative) * size,
+            axis,
+        )
+    return whole
+
+
+def reduce_gradient(own_keep, own_send, other_keep, other_send):
+    place = lax.axis_index("dp")
+    count = lax.axis_size("dp")
+    from_other = swap(other_send.astype(LOW), 1)
+    from_own = swap(own_send.astype(LOW), 1)
+    crossing = swap((other_keep + from_other.astype(F32)).astype(LOW), 1, "mp")
+    total = (own_keep + from_own.astype(F32) + crossing.astype(F32)).astype(LOW)
+    distances = []
+    distance = 2
+    while distance < count:
+        distances.append(distance)
+        distance *= 2
+    for distance in distances:
+        bit = bit_of(place, distance)
+        received = swap(cut(total, 1 - bit, 2, 0), distance)
+        total = (cut(total, bit, 2, 0).astype(F32) + received.astype(F32)).astype(LOW)
+    for distance in reversed(distances):
+        total = ordered(bit_of(place, distance), total, swap(total, distance), 0)
+    return total, swap(total, 1)
+
+
+def whole_page_body(
+    inputs,
+    qkv_weight,
+    qv_bias,
+    out_weight,
+    out_bias,
+    norm_gain,
+    norm_shift,
+    up_weight,
+    up_bias,
+    down_weight,
+    down_bias,
+    cotangent,
+):
+    place = lax.axis_index("dp")
+    column = lax.axis_index("mp")
+    core = bit_of(place, 1)
+
+    qkv_own, out_own, up_own, down_own = qkv_weight[0], out_weight[0], up_weight[0], down_weight[0]
+    qkv_w = (qkv_own, fetch_other(qkv_own, 1))
+    out_w = (out_own, fetch_other(out_own, 0))
+    up_w = (up_own, fetch_other(up_own, 0))
+    down_w = (down_own, fetch_other(down_own, 0))
+    biases = jnp.concatenate([qv_bias[0].reshape(-1), up_bias[0]])
+    biases = (biases, swap(biases, 1, "mp"))
+    width = qv_bias.shape[2]
+    q_b = [entry[:width] for entry in biases]
+    v_b = [entry[width : 2 * width] for entry in biases]
+    up_b = [entry[2 * width :].reshape(1, -1) for entry in biases]
+    gains, shifts = norm_gain[0], norm_shift[0]
+
+    x_low = inputs
+    x_shard = inputs.astype(F32)
+    heads = []
+    for half in range(2):
+        weight = qkv_w[half]
+        queries = ((matmul(x_low, weight[0]) + q_b[half]) * 0.125).astype(LOW)
+        key_rows = matmul(x_low, weight[1]).astype(LOW)
+        values = (matmul(x_low, weight[2]) + v_b[half]).astype(LOW)
+        attended, lse = attend(queries, key_rows, values)
+        heads.append((queries, key_rows, values, lse, attended))
+    pre_first = x_shard + out_bias[0]
+    for half in range(2):
+        pre_first = pre_first + matmul(heads[half][4], out_w[half])
+    hidden = norm_rows(pre_first, gains[0], shifts[0])
+    hidden_low = hidden.astype(LOW)
+    units = [expand(hidden_low, up_w[half], up_b[half]) for half in range(2)]
+    pre_second = hidden + down_bias[0]
+    for half in range(2):
+        pre_second = pre_second + matmul(units[half][0], down_w[half])
+    layer_out, norm_back = jax.vjp(norm_rows, pre_second, gains[1], shifts[1])
+    grad_second, gain_two, shift_two = norm_back(cotangent.astype(F32))
+
+    def weight_gradient(left, right, axis):
+        if axis == 0:
+            return [matmul(part, right, 0, 0) for part in left]
+        return [matmul(left, part, 0, 0) for part in right]
+
+    def by_core(rows):
+        return (cut(rows, core, 2, 1), cut(rows, 1 - core, 2, 1))
+
+    grad_second_low = grad_second.astype(LOW)
+    second_parts = by_core(grad_second_low)
+    hidden_parts = by_core(hidden_low)
+    input_parts = by_core(x_low)
+
+    down_parts = [weight_gradient(units[half][0], second_parts, 1) for half in range(2)]
+    down_sum = reduce_gradient(*down_parts[0], *down_parts[1])
+    grad_down = ordered(core, down_sum[0], down_sum[1], 1).astype(F32)
+
+    back = [contract_back(grad_second_low, down_w[half], units[half][1]) for half in range(2)]
+    up_parts = [weight_gradient(hidden_parts, back[half][0], 0) for half in range(2)]
+    up_sum = reduce_gradient(*up_parts[0], *up_parts[1])
+    grad_up = ordered(core, up_sum[0], up_sum[1], 0).astype(F32)
+
+    grad_hidden = grad_second
+    for half in range(2):
+        grad_hidden = grad_hidden + matmul(back[half][0], up_w[half], 1, 1)
+    norm_result, norm_back = jax.vjp(norm_rows, pre_first, gains[0], shifts[0])
+    grad_first, gain_one, shift_one = norm_back(grad_hidden)
+    grad_first_low = grad_first.astype(LOW)
+    first_parts = by_core(grad_first_low)
+    out_parts = [weight_gradient(heads[half][4], first_parts, 1) for half in range(2)]
+    out_sum = reduce_gradient(*out_parts[0], *out_parts[1])
+    grad_out_w = ordered(core, out_sum[0], out_sum[1], 1).astype(F32)
+
+    grad_x = grad_first
+    qkv_parts = []
+    qv_sums = []
+    for half in (1, 0):
+        queries, key_rows, values, lse, attended = heads[half]
+        grad_mix = matmul(grad_first_low, out_w[half], 1, 1).astype(LOW)
+        three = attend_back(queries, key_rows, values, lse, grad_mix)
+        keep, send = (
+            jnp.concatenate([matmul(part, entry, 0, 0) for entry in three])
+            for part in input_parts
+        )
+        qkv_parts = [keep, send] + qkv_parts
+        for member in range(3):
+            grad_x = grad_x + matmul(three[member], qkv_w[half][member], 1, 1)
+        qv_sums.insert(0, [jnp.sum(three[member].astype(F32), axis=0) for member in (0, 2)])
+    qkv_sum = reduce_gradient(*qkv_parts)
+    depth = qkv_own.shape[1] // 2
+    grad_qkv = ordered(
+        core,
+        qkv_sum[0].reshape(3, depth, width),
+        qkv_sum[1].reshape(3, depth, width),
+        1,
+    ).astype(F32)
+
+    split_small = [
+        jnp.concatenate(qv_sums[half] + [back[half][1].reshape(-1)]) for half in range(2)
+    ]
+    shared_small = jnp.concatenate(
+        [
+            jnp.sum(grad_first, axis=0),
+            gain_one,
+            gain_two,
+            shift_one,
+            shift_two,
+            jnp.sum(grad_second, axis=0),
+        ]
+    )
+    crossing = swap(jnp.concatenate([split_small[1], shared_small]), 1, "mp")
+    small = jnp.concatenate([split_small[0], shared_small]) + crossing
+    distance = 1
+    while distance < lax.axis_size("dp"):
+        small = small + swap(small, distance)
+        distance *= 2
+    split_width = split_small[0].shape[0]
+    grad_qv_bias = small[: 2 * width].reshape(1, 2, width)
+    grad_up_bias = small[2 * width : split_width].reshape(1, -1)
+    shared = small[split_width:].reshape(6, -1)
+    return (
+        layer_out,
+        grad_x,
+        grad_qkv[None],
+        grad_qv_bias,
+        grad_out_w[None],
+        shared[0:1],
+        shared[1:3][None],
+        shared[3:5][None],
+        grad_up[None],
+        grad_up_bias,
+        grad_down[None],
+        shared[5:6],
+    )
+
+
+def body(inputs, *others):
+    rows = inputs.shape[0]
+    shared = lax.axis_size("mp") == 2 and lax.axis_size("dp") in (8, 16, 32, 64)
+    if rows % PAGE == 0 and shared:
+        return whole_page_body(inputs, *others)
+    return spread_body(inputs, *others)
+
+
 def solution(mesh):
     placed = (
         P(("dp", "mp"), None),

time: 1580 us -> 673 us (0.43)
  waiting for transfers between devices: 895 us -> 272 us
  matrix products: 320 us -> 124 us
  blocking collectives: 106 us -> 0 us
  local copies, waits for them, and re-layouts: 155 us -> 57.8 us
  Pallas kernels: 0 us -> 92.1 us
  starting transfers between devices: 0.49 us -> 66.7 us
  other arithmetic: 80.2 us -> 52.8 us
    reduce_scatter x6 -> x0, waiting for transfers between devices: 400 us -> none  [the longest x4 239 us: sum_rows(): lax.psum_scatter(term(jnp.int32(0), lax.axis_size('mp') * shard_rows), 'm...]
    psum x1 -> x0, waiting for transfers between devices: 324 us -> none  [body(): lax.psum((qkv_part, bias_part, out_part, up_part, upb_part, down_part), '...]
    ppermute x0 -> x70, waiting for transfers between devices: none -> 272 us  [swap(): lax.ppermute(value, axis, [(place, place ^ distance) for place in range(c...]
    dot_general x47 -> x44, matrix products: 307 us -> 124 us  [matmul(): lax.dot_general(left, right, (((left_dim,), (right_dim,)), ((), ())), pre...]
    all_gather x5 -> x0, waiting for transfers between devices: 169 us -> none  [the longest x3 98.6 us: spread_rows(): lax.all_gather(rows_low, 'mp', axis=0, tiled=True)]
    psum x2 -> x0, blocking collectives: 106 us -> none  [the longest x1 63.5 us: body(): lax.psum((qkv_part, bias_part, out_part, up_part, upb_part, down_part), '...]
    pallas_call x0 -> x8, Pallas kernels: none -> 92.1 us  [the longest x2 27 us: attend_back(): pl.pallas_call(attend_back_kernel, grid=(pages, pairs), in_specs=head_spe...]
    ppermute x0 -> x70, starting transfers between devices: none -> 66.7 us  [swap(): lax.ppermute(value, axis, [(place, place ^ distance) for place in range(c...]
  transfers between devices with their start and end apart: 12 -> 70, of which waited for: 11 -> 29; matrix products, arithmetic and copies ran while one was open for 12% -> 18% of each run, Pallas kernels for 0% -> 7%
where the time goes in v1:
time: 673 us; the launch traced here: 669 us
  waiting for transfers between devices  272 us (40%)
  matrix products  124 us (18%)
  Pallas kernels  92.1 us (14%)
  starting transfers between devices  66.7 us (10%)
  local copies, waits for them, and re-layouts  57.8 us (9%)
  other arithmetic  52.8 us (8%)
    ppermute x70, waiting for transfers between devices, swap(): lax.ppermute(value, axis, [(place, place ^ distance) for place in range(c...  272 us
    dot_general x44, matrix products, matmul(): lax.dot_general(left, right, (((left_dim,), (right_dim,)), ((), ())), pre...  124 us
    ppermute x70, starting transfers between devices, swap(): lax.ppermute(value, axis, [(place, place ^ distance) for place in range(c...  66.7 us
    pallas_call x2, Pallas kernels, attend_back(): pl.pallas_call(attend_back_kernel, grid=(pages, pairs), in_specs=head_spe...  27 us
    pallas_call x2, Pallas kernels, expand(): pl.pallas_call(expand_kernel, grid=(units // UNITS,), in_specs=[pl.BlockS...  26.9 us
    unnamed x192, local copies, waits for them, and re-layouts  22.4 us
    pallas_call x2, Pallas kernels, attend(): pl.pallas_call(attend_kernel, grid=(pages, pairs), in_specs=head_specs(3)...  20.5 us
    dynamic_update_slice x28, local copies, waits for them, and re-layouts, fetch_other(): lax.dynamic_update_slice_in_dim(whole, lax.slice_in_dim(both, slot * size...  18.3 us
  transfers between devices with their start and end apart: 70, of which 29 were waited for; matrix products, arithmetic and copies ran while one was open for 18% of the time, Pallas kernels for 7%

profile of v1, /device:TPU:0, one launch (start us, length us, event | category | flops | bytes accessed | tf_op | source)
XLA Modules:
  0.0 668.8 jit_solution(8500573980582523755)
XLA Ops:
  19.3 10.3 %attend.2 = (bf16[832,512]{1,0:T(8,128)(2,1)S(1)}, f32[2,4,2,416]{3,2,1,0:T(2,128)S(1)}) custom-call(bf16[832,512]{1,0:T(8,128)(2,1)S(1)} %multiply_convert_fusion.1.q_ref, bf16[832,512]{1,0:T(8,128)(2,1)S(1)} %convolution_convert_fusion.7.k_ref, bf16[832,512]{1,0:T(8,128)(2,1)S(1)} %add_convert_fusion.9.v_ref), custom_call_target="tpu_custom_call" | custom-call | flops 2835349504 | bytes 3407872 | tf_op jit(solution)/shard_map/attend/pallas_call | solution.py:362
  53.8 3.1 collective-permute-done.1
  60.3 23.4 %collective-permute-done.3 = bf16[3,64,512]{2,1,0:T(8,128)(2,1)S(1)} collective-permute-done((bf16[3,64,512]{2,1,0:T(8,128)(2,1)S(1)}, bf16[3,64,512]{2,1,0:T(8,128)(2,1)S(1)}, u32[]{:S(2)}, u32[]{:S(2)}) %collective-permute-start.3) | collective-permute-done | bytes 196640 | tf_op jit(solution)/shard_map/ppermute | solution.py:474
  84.9 5.0 collective-permute-done.4
  101.3 3.2 collective-permute-done.22
  112.5 10.1 %attend.3 = (bf16[832,512]{1,0:T(8,128)(2,1)S(1)}, f32[2,4,2,416]{3,2,1,0:T(2,128)S(1)}) custom-call(bf16[832,512]{1,0:T(8,128)(2,1)S(1)} %fusion.11.q_ref, bf16[832,512]{1,0:T(8,128)(2,1)S(1)} %fusion.13.k_ref, bf16[832,512]{1,0:T(8,128)(2,1)S(1)} %fusion.12.v_ref), custom_call_target="tpu_custom_call" | custom-call | flops 2835349504 | bytes 3407872 | tf_op jit(solution)/shard_map/attend/pallas_call | solution.py:362
  126.5 13.6 %expand.2 = (bf16[832,2048]{1,0:T(8,128)(2,1)S(1)}, bf16[832,2048]{1,0:T(8,128)(2,1)}) custom-call(bf16[832,1024]{1,0:T(8,128)(2,1)S(1)} %fusion.10.h_ref, bf16[1024,2048]{1,0:T(8,128)(2,1)} %bitcast.133, f32[1,2048]{1,0:T(1,128)S(1)} %copy-done.6), custom_call_target="tpu_custom_call" | custom-call | flops 6979321856 | bytes 11010048 | tf_op jit(solution)/shard_map/expand/pallas_call | solution.py:413
  140.2 8.9 %fusion.97 = f32[832,1024]{1,0:T(8,128)} fusion(bf16[832,2048]{1,0:T(8,128)(2,1)S(1)} %get-tuple-element.32, bf16[1,2048,1024]{2,1,0:T(8,128)(2,1)} %param.21), kind=kOutput, calls=%fused_computation.298 | convolution fusion | flops 3489660928 | bytes 11010048 | tf_op jit(solution)/shard_map/dot_general | solution.py:301
  158.7 13.2 %expand.3 = (bf16[832,2048]{1,0:T(8,128)(2,1)S(1)}, bf16[832,2048]{1,0:T(8,128)(2,1)}) custom-call(bf16[832,1024]{1,0:T(8,128)(2,1)S(1)} %fusion.10.h_ref, bf16[1024,2048]{1,0:T(8,128)(2,1)} %copy-done.72, f32[1,2048]{1,0:T(1,128)S(1)} %bitcast.126), custom_call_target="tpu_custom_call" | custom-call | flops 6979321856 | bytes 11010048 | tf_op jit(solution)/shard_map/expand/pallas_call | solution.py:413
  171.9 4.3 constant_dynamic-update-slice_fusion.38
  188.1 6.3 fusion.110
  197.2 3.1 fusion.102
  202.1 8.1 %contract_back.3 = (bf16[832,2048]{1,0:T(8,128)(2,1)S(1)}, f32[1,2048]{1,0:T(1,128)S(1)}) custom-call(bf16[832,1024]{1,0:T(8,128)(2,1)S(1)} %get-tuple-element.60.g_ref, bf16[2048,1024]{1,0:T(8,128)(2,1)} %slice_dynamic-update-slice_fusion.w_ref, bf16[832,2048]{1,0:T(8,128)(2,1)} %get-tuple-element.36.slope_ref), custom_call_target="tpu_custom_call" | custom-call | flops 3489660928 | bytes 11010048 | tf_op jit(solution)/shard_map/contract_back/pallas_call | solution.py:449
  210.2 9.6 %contract_back.2 = (bf16[832,2048]{1,0:T(8,128)(2,1)S(1)}, f32[1,2048]{1,0:T(1,128)S(1)}) custom-call(bf16[832,1024]{1,0:T(8,128)(2,1)S(1)} %get-tuple-element.60.g_ref, bf16[2048,1024]{1,0:T(8,128)(2,1)} %bitcast.132, bf16[832,2048]{1,0:T(8,128)(2,1)} %get-tuple-element.34.slope_ref), custom_call_target="tpu_custom_call" | custom-call | flops 3489660928 | bytes 11010048 | tf_op jit(solution)/shard_map/contract_back/pallas_call | solution.py:449
  219.8 7.8 %fusion.99 = f32[832,1024]{1,0:T(8,128)} fusion(bf16[832,2048]{1,0:T(8,128)(2,1)S(1)} %get-tuple-element.35, bf16[1,1024,2048]{2,1,0:T(8,128)(2,1)} %param.19), kind=kOutput, calls=%fused_computation.300 | convolution fusion | flops 3489660928 | bytes 11010048 | tf_op jit(solution)/shard_map/dot_general | solution.py:301
  227.6 9.6 %multiply_reduce_fusion = (f32[1024]{0:T(1024)S(1)}, f32[832]{0:T(1024)S(1)}, f32[1024]{0:T(1024)S(1)}, f32[832,1024]{1,0:T(8,128)}) fusion(f32[832,1024]{1,0:T(8,128)S(1)} %copy-done.29, f32[832]{0:T(1024)S(1)} %fusion.95, f32[832]{0:T(1024)S(1)} %broadcast_multiply_fusion.1, f32[1024]{0:T(1024)S(1)} %bitcast.138, ...), kind=kOutput, calls=%fused_computation.17 | convolution fusion | flops 3499029760 | bytes 21259264 | tf_op jit(solution)/shard_map/dot_general | solution.py:301
  244.8 13.3 %attend_back.3 = (bf16[832,512]{1,0:T(8,128)(2,1)S(1)}, bf16[832,512]{1,0:T(8,128)(2,1)S(1)}, bf16[832,512]{1,0:T(8,128)(2,1)S(1)}) custom-call(bf16[832,512]{1,0:T(8,128)(2,1)S(1)} %copy-done.21, bf16[832,512]{1,0:T(8,128)(2,1)S(1)} %copy-done.16, bf16[832,512]{1,0:T(8,128)(2,1)S(1)} %copy-done.23, f32[2,4,2,416]{3,2,1,0:T(2,128)S(1)} %get-tuple-element.42.lse_ref, ...), custom_call_target="tpu_custom_call" | custom-call | flops 7088373760 | bytes 5963776 | tf_op jit(solution)/shard_map/attend_back/pallas_call | solution.py:383
  258.1 4.7 fusion.18
  262.8 4.2 fusion.21
  270.5 13.7 %attend_back.2 = (bf16[832,512]{1,0:T(8,128)(2,1)S(1)}, bf16[832,512]{1,0:T(8,128)(2,1)S(1)}, bf16[832,512]{1,0:T(8,128)(2,1)S(1)}) custom-call(bf16[832,512]{1,0:T(8,128)(2,1)S(1)} %copy-done.25, bf16[832,512]{1,0:T(8,128)(2,1)S(1)} %copy-done.18, bf16[832,512]{1,0:T(8,128)(2,1)S(1)} %copy-done.27, f32[2,4,2,416]{3,2,1,0:T(2,128)S(1)} %get-tuple-element.38.lse_ref, ...), custom_call_target="tpu_custom_call" | custom-call | flops 7088373760 | bytes 5963776 | tf_op jit(solution)/shard_map/attend_back/pallas_call | solution.py:383
  285.1 3.1 fusion.59
  296.7 3.8 convolution_convert_fusion.2
  302.9 3.7 convolution_convert_fusion.3
  306.6 3.9 convolution_convert_fusion
  310.6 3.7 convolution_convert_fusion.1
  327.5 9.5 %collective-permute-done.42 = bf16[512,512]{1,0:T(8,128)(2,1)S(1)} collective-permute-done((bf16[512,512]{1,0:T(8,128)(2,1)S(1)}, bf16[512,512]{1,0:T(8,128)(2,1)S(1)}, u32[]{:S(2)}, u32[]{:S(2)}) %collective-permute-start.42) | collective-permute-done | bytes 524320 | tf_op jit(solution)/shard_map/ppermute | solution.py:474
  347.9 3.9 add_convert_fusion.3
  353.4 5.6 add_convert_fusion.1
  359.9 19.3 %collective-permute-done.27 = bf16[1536,512]{1,0:T(8,128)(2,1)S(1)} collective-permute-done((bf16[1536,512]{1,0:T(8,128)(2,1)S(1)}, bf16[1536,512]{1,0:T(8,128)(2,1)S(1)}, u32[]{:S(2)}, u32[]{:S(2)}) %collective-permute-start.27) | collective-permute-done | bytes 1572896 | tf_op jit(solution)/shard_map/ppermute | solution.py:474
  385.3 4.1 fusion.28
  391.8 11.3 %collective-permute-done.28 = bf16[768,512]{1,0:T(8,128)(2,1)S(1)} collective-permute-done((bf16[768,512]{1,0:T(8,128)(2,1)S(1)}, bf16[768,512]{1,0:T(8,128)(2,1)S(1)}, u32[]{:S(2)}, u32[]{:S(2)}) %collective-permute-start.28) | collective-permute-done | bytes 786464 | tf_op jit(solution)/shard_map/ppermute | solution.py:474
  405.5 23.7 %collective-permute-done.52 = bf16[512,2048]{1,0:T(8,128)(2,1)S(1)} collective-permute-done((bf16[512,2048]{1,0:T(8,128)(2,1)}, bf16[512,2048]{1,0:T(8,128)(2,1)S(1)}, u32[]{:S(2)}, u32[]{:S(2)}) %collective-permute-start.52) | collective-permute-done | bytes 2097184 | tf_op jit(solution)/shard_map/ppermute | solution.py:474
  432.5 40.0 %collective-permute-done.62 = bf16[2048,512]{1,0:T(8,128)(2,1)} collective-permute-done((bf16[2048,512]{1,0:T(8,128)(2,1)}, bf16[2048,512]{1,0:T(8,128)(2,1)}, u32[]{:S(2)}, u32[]{:S(2)}) %collective-permute-start.62) | collective-permute-done | bytes 2097184 | tf_op jit(solution)/shard_map/ppermute | solution.py:474
  480.2 6.1 collective-permute-done.30
  487.6 11.4 %collective-permute-done.63 = bf16[1024,512]{1,0:T(8,128)(2,1)S(1)} collective-permute-done((bf16[1024,512]{1,0:T(8,128)(2,1)S(1)}, bf16[1024,512]{1,0:T(8,128)(2,1)S(1)}, u32[]{:S(2)}, u32[]{:S(2)}) %collective-permute-start.63) | collective-permute-done | bytes 1048608 | tf_op jit(solution)/shard_map/ppermute | solution.py:474
  503.2 13.2 %collective-permute-done.64 = bf16[512,512]{1,0:T(8,128)(2,1)S(1)} collective-permute-done((bf16[512,512]{1,0:T(8,128)(2,1)S(1)}, bf16[512,512]{1,0:T(8,128)(2,1)S(1)}, u32[]{:S(2)}, u32[]{:S(2)}) %collective-permute-start.64) | collective-permute-done | bytes 524320 | tf_op jit(solution)/shard_map/ppermute | solution.py:474
  520.6 14.8 %collective-permute-done.65 = bf16[256,512]{1,0:T(8,128)(2,1)S(1)} collective-permute-done((bf16[256,512]{1,0:T(8,128)(2,1)S(1)}, bf16[256,512]{1,0:T(8,128)(2,1)S(1)}, u32[]{:S(2)}, u32[]{:S(2)}) %collective-permute-start.65) | collective-permute-done | bytes 262176 | tf_op jit(solution)/shard_map/ppermute | solution.py:474
  535.6 11.1 %collective-permute-done.56 = bf16[64,2048]{1,0:T(8,128)(2,1)S(1)} collective-permute-done((bf16[64,2048]{1,0:T(8,128)(2,1)S(1)}, bf16[64,2048]{1,0:T(8,128)(2,1)S(1)}, u32[]{:S(2)}, u32[]{:S(2)}) %collective-permute-start.56) | collective-permute-done | bytes 262176 | tf_op jit(solution)/shard_map/ppermute | solution.py:474
  549.1 3.3 collective-permute-done.66
  552.7 7.9 %collective-permute-done.45 = bf16[64,512]{1,0:T(8,128)(2,1)S(1)} collective-permute-done((bf16[64,512]{1,0:T(8,128)(2,1)S(1)}, bf16[64,512]{1,0:T(8,128)(2,1)S(1)}, u32[]{:S(2)}, u32[]{:S(2)}) %collective-permute-start.45) | collective-permute-done | bytes 65568 | tf_op jit(solution)/shard_map/ppermute | solution.py:474
  560.6 3.4 collective-permute-start.46
  566.8 5.6 collective-permute-done.46
  580.9 4.2 fusion.27
  585.7 46.6 %collective-permute-done.48 = bf16[256,512]{1,0:T(8,128)(2,1)S(1)} collective-permute-done((bf16[256,512]{1,0:T(8,128)(2,1)S(1)}, bf16[256,512]{1,0:T(8,128)(2,1)S(1)}, u32[]{:S(2)}, u32[]{:S(2)}) %collective-permute-start.48) | collective-permute-done | bytes 262176 | tf_op jit(solution)/shard_map/ppermute | solution.py:474
  638.7 6.2 add_add_fusion.2
  649.6 5.1 fusion.9
  654.7 6.0 fusion
  660.7 7.9 %fusion.1 = f32[1,2048,1024]{2,1,0:T(8,128)} fusion(bf16[1,2048,512]{2,1,0:T(8,128)(2,1)} %bitcast.37, bf16[1,2048,512]{2,1,0:T(8,128)(2,1)} %bitcast.36, pred[]{:T(512)S(6)} %eq.54), kind=kLoop, calls=%fused_computation.8 | loop fusion | flops 20971520 | bytes 12582913 | tf_op jit(solution)/shard_map/convert_element_type | solution.py:610
  (472 shorter events, 201.6 us)
Async XLA Ops:
  2.6 42.0 %collective-permute-start = (bf16[3,128,512]{2,1,0:T(8,128)(2,1)}, bf16[3,128,512]{2,1,0:T(8,128)(2,1)}, u32[]{:S(2)}, u32[]{:S(2)}) collective-permute-start(bf16[3,128,512]{2,1,0:T(8,128)(2,1)} %dynamic-slice_bitcast_fusion.2), channel_id=1, source_target_pairs={{0,1},{1,0},{2,3},{3,2},{4,5},{5,4},{6,7},{7,6},{8,9},{9,8},{10,11... | collective-permute-start | bytes 1179656 | tf_op jit(solution)/shard_map/ppermute | solution.py:474
  7.0 27.6 %collective-permute-start.6 = (f32[3072]{0:T(1024)S(1)}, f32[3072]{0:T(1024)S(1)}, u32[]{:S(2)}, u32[]{:S(2)}) collective-permute-start(f32[3072]{0:T(1024)S(1)} %pad_maximum_fusion.2), channel_id=1, source_target_pairs={{0,1},{1,0},{2,3},{3,2},{4,5},{5,4},{6,7},{7,6},{8,9},{9,8},{10,11... | collective-permute-start | bytes 36872 | tf_op jit(solution)/shard_map/ppermute | solution.py:474
  7.6 25.4 %collective-permute-start.7 = (bf16[64,1024]{1,0:T(8,128)(2,1)}, bf16[64,1024]{1,0:T(8,128)(2,1)S(1)}, u32[]{:S(2)}, u32[]{:S(2)}) collective-permute-start(bf16[64,1024]{1,0:T(8,128)(2,1)} %dynamic-slice_bitcast_fusion.3), channel_id=1, source_target_pairs={{0,1},{1,0},{2,3},{3,2},{4,5},{5,4},{6,7},{7,6},{8,9},{9,8},{10,11... | collective-permute-start | bytes 393224 | tf_op jit(solution)/shard_map/ppermute | solution.py:474
  10.7 36.7 %collective-permute-start.13 = (bf16[128,2048]{1,0:T(8,128)(2,1)S(1)}, bf16[128,2048]{1,0:T(8,128)(2,1)}, u32[]{:S(2)}, u32[]{:S(2)}) collective-permute-start(bf16[128,2048]{1,0:T(8,128)(2,1)S(1)} %dynamic-slice_bitcast_fusion.1), channel_id=1, source_target_pairs={{0,1},{1,0},{2,3},{3,2},{4,5},{5,4},{6,7},{7,6},{8,9},{9,8},{10,11... | collective-permute-start | bytes 1572872 | tf_op jit(solution)/shard_map/ppermute | solution.py:474
  12.7 36.8 %collective-permute-start.19 = (bf16[256,1024]{1,0:T(8,128)(2,1)}, bf16[256,1024]{1,0:T(8,128)(2,1)}, u32[]{:S(2)}, u32[]{:S(2)}) collective-permute-start(bf16[256,1024]{1,0:T(8,128)(2,1)} %dynamic-slice_bitcast_fusion), channel_id=1, source_target_pairs={{0,1},{1,0},{2,3},{3,2},{4,5},{5,4},{6,7},{7,6},{8,9},{9,8},{10,11... | collective-permute-start | bytes 1572872 | tf_op jit(solution)/shard_map/ppermute | solution.py:474
  47.5 42.5 %collective-permute-start.14 = (bf16[128,2048]{1,0:T(8,128)(2,1)}, bf16[128,2048]{1,0:T(8,128)(2,1)S(1)}, u32[]{:S(2)}, u32[]{:S(2)}) collective-permute-start(bf16[128,2048]{1,0:T(8,128)(2,1)} %collective-permute-done.13), channel_id=1, source_target_pairs={{0,4},{2,6},{4,0},{6,2},{8,12},{10,14},{12,8},{14,10},{16,20},{18,... | collective-permute-start | bytes 1572872 | tf_op jit(solution)/shard_map/ppermute | solution.py:474
  49.5 41.8 %collective-permute-start.15 = (bf16[128,2048]{1,0:T(8,128)(2,1)}, bf16[128,2048]{1,0:T(8,128)(2,1)S(1)}, u32[]{:S(2)}, u32[]{:S(2)}) collective-permute-start(bf16[128,2048]{1,0:T(8,128)(2,1)} %collective-permute-done.13), channel_id=1, source_target_pairs={{0,8},{2,10},{4,12},{6,14},{8,0},{10,2},{12,4},{14,6},{16,24},{18,... | collective-permute-start | bytes 1572872 | tf_op jit(solution)/shard_map/ppermute | solution.py:474
  56.8 36.0 %collective-permute-start.20 = (bf16[256,1024]{1,0:T(8,128)(2,1)}, bf16[256,1024]{1,0:T(8,128)(2,1)S(1)}, u32[]{:S(2)}, u32[]{:S(2)}) collective-permute-start(bf16[256,1024]{1,0:T(8,128)(2,1)} %collective-permute-done.19), channel_id=1, source_target_pairs={{0,4},{2,6},{4,0},{6,2},{8,12},{10,14},{12,8},{14,10},{16,20},{18,... | collective-permute-start | bytes 1572872 | tf_op jit(solution)/shard_map/ppermute | solution.py:474
  57.8 35.6 %collective-permute-start.21 = (bf16[256,1024]{1,0:T(8,128)(2,1)}, bf16[256,1024]{1,0:T(8,128)(2,1)S(1)}, u32[]{:S(2)}, u32[]{:S(2)}) collective-permute-start(bf16[256,1024]{1,0:T(8,128)(2,1)} %collective-permute-done.19), channel_id=1, source_target_pairs={{0,8},{2,10},{4,12},{6,14},{8,0},{10,2},{12,4},{14,6},{16,24},{18,... | collective-permute-start | bytes 1572872 | tf_op jit(solution)/shard_map/ppermute | solution.py:474
  58.7 25.0 %collective-permute-start.3 = (bf16[3,64,512]{2,1,0:T(8,128)(2,1)S(1)}, bf16[3,64,512]{2,1,0:T(8,128)(2,1)S(1)}, u32[]{:S(2)}, u32[]{:S(2)}) collective-permute-start(bf16[3,64,512]{2,1,0:T(8,128)(2,1)S(1)} %slice.222), channel_id=1, source_target_pairs={{0,8},{2,10},{4,12},{6,14},{8,0},{10,2},{12,4},{14,6},{16,24},{18,... | collective-permute-start | bytes 589832 | tf_op jit(solution)/shard_map/ppermute | solution.py:474
  89.9 16.3 %collective-permute-start.5 = (bf16[3,512,512]{2,1,0:T(8,128)(2,1)S(1)}, bf16[3,512,512]{2,1,0:T(8,128)(2,1)S(1)}, u32[]{:S(2)}, u32[]{:S(2)}) collective-permute-start(bf16[3,512,512]{2,1,0:T(8,128)(2,1)S(1)} %get-tuple-element.89), channel_id=1, source_target_pairs={{0,2},{2,0},{4,6},{6,4},{8,10},{10,8},{12,14},{14,12},{16,18},{18,... | collective-permute-start | bytes 4718600 | tf_op jit(solution)/shard_map/ppermute | solution.py:474
  101.3 47.8 %collective-permute-start.18 = (bf16[512,2048]{1,0:T(8,128)(2,1)}, bf16[512,2048]{1,0:T(8,128)(2,1)}, u32[]{:S(2)}, u32[]{:S(2)}) collective-permute-start(bf16[512,2048]{1,0:T(8,128)(2,1)} %get-tuple-element.85), channel_id=1, source_target_pairs={{0,2},{2,0},{4,6},{6,4},{8,10},{10,8},{12,14},{14,12},{16,18},{18,... | collective-permute-start | bytes 6291464 | tf_op jit(solution)/shard_map/ppermute | solution.py:474
  106.2 65.8 %collective-permute-start.24 = (bf16[1024,1024]{1,0:T(8,128)(2,1)}, bf16[1024,1024]{1,0:T(8,128)(2,1)}, u32[]{:S(2)}, u32[]{:S(2)}) collective-permute-start(bf16[1024,1024]{1,0:T(8,128)(2,1)} %get-tuple-element.81), channel_id=1, source_target_pairs={{0,2},{2,0},{4,6},{6,4},{8,10},{10,8},{12,14},{14,12},{16,18},{18,... | collective-permute-start | bytes 6291464 | tf_op jit(solution)/shard_map/ppermute | solution.py:474
  315.2 22.1 %collective-permute-start.26 = (bf16[1536,512]{1,0:T(8,128)(2,1)S(1)}, bf16[1536,512]{1,0:T(8,128)(2,1)S(1)}, u32[]{:S(2)}, u32[]{:S(2)}) collective-permute-start(bf16[1536,512]{1,0:T(8,128)(2,1)S(1)} %pad_maximum_fusion.1), channel_id=1, source_target_pairs={{0,2},{2,0},{4,6},{6,4},{8,10},{10,8},{12,14},{14,12},{16,18},{18,... | collective-permute-start | bytes 4718600 | tf_op jit(solution)/shard_map/ppermute | solution.py:474
  316.5 30.8 %collective-permute-start.51 = (bf16[512,2048]{1,0:T(8,128)(2,1)}, bf16[512,2048]{1,0:T(8,128)(2,1)S(1)}, u32[]{:S(2)}, u32[]{:S(2)}) collective-permute-start(bf16[512,2048]{1,0:T(8,128)(2,1)} %convolution_convert_fusion.2), channel_id=1, source_target_pairs={{0,2},{2,0},{4,6},{6,4},{8,10},{10,8},{12,14},{14,12},{16,18},{18,... | collective-permute-start | bytes 6291464 | tf_op jit(solution)/shard_map/ppermute | solution.py:474
  326.8 32.1 %collective-permute-start.25 = (bf16[1536,512]{1,0:T(8,128)(2,1)}, bf16[1536,512]{1,0:T(8,128)(2,1)S(1)}, u32[]{:S(2)}, u32[]{:S(2)}) collective-permute-start(bf16[1536,512]{1,0:T(8,128)(2,1)} %pad_maximum_fusion), channel_id=1, source_target_pairs={{0,2},{2,0},{4,6},{6,4},{8,10},{10,8},{12,14},{14,12},{16,18},{18,... | collective-permute-start | bytes 4718600 | tf_op jit(solution)/shard_map/ppermute | solution.py:474
  327.0 24.8 %collective-permute-start.61 = (bf16[2048,512]{1,0:T(8,128)(2,1)}, bf16[2048,512]{1,0:T(8,128)(2,1)}, u32[]{:S(2)}, u32[]{:S(2)}) collective-permute-start(bf16[2048,512]{1,0:T(8,128)(2,1)} %convolution_convert_fusion), channel_id=1, source_target_pairs={{0,2},{2,0},{4,6},{6,4},{8,10},{10,8},{12,14},{14,12},{16,18},{18,... | collective-permute-start | bytes 6291464 | tf_op jit(solution)/shard_map/ppermute | solution.py:474
  342.6 36.6 %collective-permute-start.27 = (bf16[1536,512]{1,0:T(8,128)(2,1)S(1)}, bf16[1536,512]{1,0:T(8,128)(2,1)S(1)}, u32[]{:S(2)}, u32[]{:S(2)}) collective-permute-start(bf16[1536,512]{1,0:T(8,128)(2,1)S(1)} %fusion.8), channel_id=1, source_target_pairs={{0,1},{1,0},{2,3},{3,2},{4,5},{5,4},{6,7},{7,6},{8,9},{9,8},{10,11... | collective-permute-start | bytes 4718600 | tf_op jit(solution)/shard_map/ppermute | solution.py:474
  347.2 57.2 %collective-permute-start.50 = (bf16[512,2048]{1,0:T(8,128)(2,1)}, bf16[512,2048]{1,0:T(8,128)(2,1)}, u32[]{:S(2)}, u32[]{:S(2)}) collective-permute-start(bf16[512,2048]{1,0:T(8,128)(2,1)} %convolution_convert_fusion.3), channel_id=1, source_target_pairs={{0,2},{2,0},{4,6},{6,4},{8,10},{10,8},{12,14},{14,12},{16,18},{18,... | collective-permute-start | bytes 6291464 | tf_op jit(solution)/shard_map/ppermute | solution.py:474
  347.3 85.2 %collective-permute-start.60 = (bf16[2048,512]{1,0:T(8,128)(2,1)}, bf16[2048,512]{1,0:T(8,128)(2,1)S(1)}, u32[]{:S(2)}, u32[]{:S(2)}) collective-permute-start(bf16[2048,512]{1,0:T(8,128)(2,1)} %convolution_convert_fusion.1), channel_id=1, source_target_pairs={{0,2},{2,0},{4,6},{6,4},{8,10},{10,8},{12,14},{14,12},{16,18},{18,... | collective-permute-start | bytes 6291464 | tf_op jit(solution)/shard_map/ppermute | solution.py:474
  351.8 32.4 %collective-permute-start.37 = (f32[9216]{0:T(1024)S(1)}, f32[9216]{0:T(1024)S(1)}, u32[]{:S(2)}, u32[]{:S(2)}) collective-permute-start(f32[9216]{0:T(1024)S(1)} %add.502), channel_id=1, source_target_pairs={{0,4},{2,6},{4,0},{6,2},{8,12},{10,14},{12,8},{14,10},{16,20},{18,... | collective-permute-start | bytes 110600 | tf_op jit(solution)/shard_map/ppermute | solution.py:474
  359.0 25.8 %collective-permute-start.44 = (bf16[128,512]{1,0:T(8,128)(2,1)S(1)}, bf16[128,512]{1,0:T(8,128)(2,1)S(1)}, u32[]{:S(2)}, u32[]{:S(2)}) collective-permute-start(bf16[128,512]{1,0:T(8,128)(2,1)S(1)} %constant_dynamic-slice_fusion.7), channel_id=1, source_target_pairs={{0,8},{2,10},{4,12},{6,14},{8,0},{10,2},{12,4},{14,6},{16,24},{18,... | collective-permute-start | bytes 393224 | tf_op jit(solution)/shard_map/ppermute | solution.py:474
  380.3 48.8 %collective-permute-start.52 = (bf16[512,2048]{1,0:T(8,128)(2,1)}, bf16[512,2048]{1,0:T(8,128)(2,1)S(1)}, u32[]{:S(2)}, u32[]{:S(2)}) collective-permute-start(bf16[512,2048]{1,0:T(8,128)(2,1)} %add_convert_fusion.3), channel_id=1, source_target_pairs={{0,1},{1,0},{2,3},{3,2},{4,5},{5,4},{6,7},{7,6},{8,9},{9,8},{10,11... | collective-permute-start | bytes 6291464 | tf_op jit(solution)/shard_map/ppermute | solution.py:474
  384.2 88.4 %collective-permute-start.62 = (bf16[2048,512]{1,0:T(8,128)(2,1)}, bf16[2048,512]{1,0:T(8,128)(2,1)}, u32[]{:S(2)}, u32[]{:S(2)}) collective-permute-start(bf16[2048,512]{1,0:T(8,128)(2,1)} %add_convert_fusion.1), channel_id=1, source_target_pairs={{0,1},{1,0},{2,3},{3,2},{4,5},{5,4},{6,7},{7,6},{8,9},{9,8},{10,11... | collective-permute-start | bytes 6291464 | tf_op jit(solution)/shard_map/ppermute | solution.py:474
  384.8 18.3 %collective-permute-start.28 = (bf16[768,512]{1,0:T(8,128)(2,1)S(1)}, bf16[768,512]{1,0:T(8,128)(2,1)S(1)}, u32[]{:S(2)}, u32[]{:S(2)}) collective-permute-start(bf16[768,512]{1,0:T(8,128)(2,1)S(1)} %constant_dynamic-slice_fusion.11), channel_id=1, source_target_pairs={{0,4},{2,6},{4,0},{6,2},{8,12},{10,14},{12,8},{14,10},{16,20},{18,... | collective-permute-start | bytes 2359304 | tf_op jit(solution)/shard_map/ppermute | solution.py:474
  403.1 182.0 %collective-permute-start.38 = (f32[9216]{0:T(1024)S(1)}, f32[9216]{0:T(1024)S(1)}, u32[]{:S(2)}, u32[]{:S(2)}) collective-permute-start(f32[9216]{0:T(1024)S(1)} %add.503), channel_id=1, source_target_pairs={{0,8},{2,10},{4,12},{6,14},{8,0},{10,2},{12,4},{14,6},{16,24},{18,... | collective-permute-start | bytes 110600 | tf_op jit(solution)/shard_map/ppermute | solution.py:474
  404.3 71.6 %collective-permute-start.29 = (bf16[384,512]{1,0:T(8,128)(2,1)S(1)}, bf16[384,512]{1,0:T(8,128)(2,1)S(1)}, u32[]{:S(2)}, u32[]{:S(2)}) collective-permute-start(bf16[384,512]{1,0:T(8,128)(2,1)S(1)} %constant_dynamic-slice_fusion.10), channel_id=1, source_target_pairs={{0,8},{2,10},{4,12},{6,14},{8,0},{10,2},{12,4},{14,6},{16,24},{18,... | collective-permute-start | bytes 1179656 | tf_op jit(solution)/shard_map/ppermute | solution.py:474
  432.0 46.8 %collective-permute-start.53 = (bf16[256,2048]{1,0:T(8,128)(2,1)S(1)}, bf16[256,2048]{1,0:T(8,128)(2,1)S(1)}, u32[]{:S(2)}, u32[]{:S(2)}) collective-permute-start(bf16[256,2048]{1,0:T(8,128)(2,1)S(1)} %constant_dynamic-slice_fusion.5), channel_id=1, source_target_pairs={{0,4},{2,6},{4,0},{6,2},{8,12},{10,14},{12,8},{14,10},{16,20},{18,... | collective-permute-start | bytes 3145736 | tf_op jit(solution)/shard_map/ppermute | solution.py:474
  475.4 23.6 %collective-permute-start.63 = (bf16[1024,512]{1,0:T(8,128)(2,1)S(1)}, bf16[1024,512]{1,0:T(8,128)(2,1)S(1)}, u32[]{:S(2)}, u32[]{:S(2)}) collective-permute-start(bf16[1024,512]{1,0:T(8,128)(2,1)S(1)} %constant_dynamic-slice_fusion.2), channel_id=1, source_target_pairs={{0,4},{2,6},{4,0},{6,2},{8,12},{10,14},{12,8},{14,10},{16,20},{18,... | collective-permute-start | bytes 3145736 | tf_op jit(solution)/shard_map/ppermute | solution.py:474
  479.2 21.2 %collective-permute-start.54 = (bf16[128,2048]{1,0:T(8,128)(2,1)S(1)}, bf16[128,2048]{1,0:T(8,128)(2,1)S(1)}, u32[]{:S(2)}, u32[]{:S(2)}) collective-permute-start(bf16[128,2048]{1,0:T(8,128)(2,1)S(1)} %constant_dynamic-slice_fusion.4), channel_id=1, source_target_pairs={{0,8},{2,10},{4,12},{6,14},{8,0},{10,2},{12,4},{14,6},{16,24},{18,... | collective-permute-start | bytes 1572872 | tf_op jit(solution)/shard_map/ppermute | solution.py:474
  486.4 33.3 %collective-permute-start.31 = (bf16[192,512]{1,0:T(8,128)(2,1)S(1)}, bf16[192,512]{1,0:T(8,128)(2,1)S(1)}, u32[]{:S(2)}, u32[]{:S(2)}) collective-permute-start(bf16[192,512]{1,0:T(8,128)(2,1)S(1)} %add_convert_fusion.19), channel_id=1, source_target_pairs={{0,16},{2,18},{4,20},{6,22},{8,24},{10,26},{12,28},{14,30},{16,0},... | collective-permute-start | bytes 589832 | tf_op jit(solution)/shard_map/ppermute | solution.py:474
  499.3 17.1 %collective-permute-start.64 = (bf16[512,512]{1,0:T(8,128)(2,1)S(1)}, bf16[512,512]{1,0:T(8,128)(2,1)S(1)}, u32[]{:S(2)}, u32[]{:S(2)}) collective-permute-start(bf16[512,512]{1,0:T(8,128)(2,1)S(1)} %constant_dynamic-slice_fusion.1), channel_id=1, source_target_pairs={{0,8},{2,10},{4,12},{6,14},{8,0},{10,2},{12,4},{14,6},{16,24},{18,... | collective-permute-start | bytes 1572872 | tf_op jit(solution)/shard_map/ppermute | solution.py:474
  500.6 17.2 %collective-permute-start.55 = (bf16[64,2048]{1,0:T(8,128)(2,1)S(1)}, bf16[64,2048]{1,0:T(8,128)(2,1)S(1)}, u32[]{:S(2)}, u32[]{:S(2)}) collective-permute-start(bf16[64,2048]{1,0:T(8,128)(2,1)S(1)} %constant_dynamic-slice_fusion.3), channel_id=1, source_target_pairs={{0,16},{2,18},{4,20},{6,22},{8,24},{10,26},{12,28},{14,30},{16,0},... | collective-permute-start | bytes 786440 | tf_op jit(solution)/shard_map/ppermute | solution.py:474
  516.6 18.8 %collective-permute-start.65 = (bf16[256,512]{1,0:T(8,128)(2,1)S(1)}, bf16[256,512]{1,0:T(8,128)(2,1)S(1)}, u32[]{:S(2)}, u32[]{:S(2)}) collective-permute-start(bf16[256,512]{1,0:T(8,128)(2,1)S(1)} %constant_dynamic-slice_fusion), channel_id=1, source_target_pairs={{0,16},{2,18},{4,20},{6,22},{8,24},{10,26},{12,28},{14,30},{16,0},... | collective-permute-start | bytes 786440 | tf_op jit(solution)/shard_map/ppermute | solution.py:474
  517.8 28.8 %collective-permute-start.56 = (bf16[64,2048]{1,0:T(8,128)(2,1)S(1)}, bf16[64,2048]{1,0:T(8,128)(2,1)S(1)}, u32[]{:S(2)}, u32[]{:S(2)}) collective-permute-start(bf16[64,2048]{1,0:T(8,128)(2,1)S(1)} %add_convert_fusion.17), channel_id=1, source_target_pairs={{0,16},{2,18},{4,20},{6,22},{8,24},{10,26},{12,28},{14,30},{16,0},... | collective-permute-start | bytes 786440 | tf_op jit(solution)/shard_map/ppermute | solution.py:474
  519.9 44.2 %collective-permute-start.32 = (bf16[384,512]{1,0:T(8,128)(2,1)S(1)}, bf16[384,512]{1,0:T(8,128)(2,1)S(1)}, u32[]{:S(2)}, u32[]{:S(2)}) collective-permute-start(bf16[384,512]{1,0:T(8,128)(2,1)S(1)} %maximum_select_fusion.13), channel_id=1, source_target_pairs={{0,8},{2,10},{4,12},{6,14},{8,0},{10,2},{12,4},{14,6},{16,24},{18,... | collective-permute-start | bytes 1179656 | tf_op jit(solution)/shard_map/ppermute | solution.py:474
  535.5 16.9 %collective-permute-start.66 = (bf16[256,512]{1,0:T(8,128)(2,1)S(1)}, bf16[256,512]{1,0:T(8,128)(2,1)S(1)}, u32[]{:S(2)}, u32[]{:S(2)}) collective-permute-start(bf16[256,512]{1,0:T(8,128)(2,1)S(1)} %add_convert_fusion.16), channel_id=1, source_target_pairs={{0,16},{2,18},{4,20},{6,22},{8,24},{10,26},{12,28},{14,30},{16,0},... | collective-permute-start | bytes 786440 | tf_op jit(solution)/shard_map/ppermute | solution.py:474
  546.8 18.8 %collective-permute-start.57 = (bf16[128,2048]{1,0:T(8,128)(2,1)S(1)}, bf16[128,2048]{1,0:T(8,128)(2,1)S(1)}, u32[]{:S(2)}, u32[]{:S(2)}) collective-permute-start(bf16[128,2048]{1,0:T(8,128)(2,1)S(1)} %maximum_select_fusion.11), channel_id=1, source_target_pairs={{0,8},{2,10},{4,12},{6,14},{8,0},{10,2},{12,4},{14,6},{16,24},{18,... | collective-permute-start | bytes 1572872 | tf_op jit(solution)/shard_map/ppermute | solution.py:474
  552.6 24.9 %collective-permute-start.67 = (bf16[512,512]{1,0:T(8,128)(2,1)S(1)}, bf16[512,512]{1,0:T(8,128)(2,1)S(1)}, u32[]{:S(2)}, u32[]{:S(2)}) collective-permute-start(bf16[512,512]{1,0:T(8,128)(2,1)S(1)} %maximum_select_fusion.12), channel_id=1, source_target_pairs={{0,8},{2,10},{4,12},{6,14},{8,0},{10,2},{12,4},{14,6},{16,24},{18,... | collective-permute-start | bytes 1572872 | tf_op jit(solution)/shard_map/ppermute | solution.py:474
  564.3 68.3 %collective-permute-start.33 = (bf16[768,512]{1,0:T(8,128)(2,1)S(1)}, bf16[768,512]{1,0:T(8,128)(2,1)S(1)}, u32[]{:S(2)}, u32[]{:S(2)}) collective-permute-start(bf16[768,512]{1,0:T(8,128)(2,1)S(1)} %maximum_select_fusion.9), channel_id=1, source_target_pairs={{0,4},{2,6},{4,0},{6,2},{8,12},{10,14},{12,8},{14,10},{16,20},{18,... | collective-permute-start | bytes 2359304 | tf_op jit(solution)/shard_map/ppermute | solution.py:474
  565.9 69.1 %collective-permute-start.58 = (bf16[256,2048]{1,0:T(8,128)(2,1)S(1)}, bf16[256,2048]{1,0:T(8,128)(2,1)S(1)}, u32[]{:S(2)}, u32[]{:S(2)}) collective-permute-start(bf16[256,2048]{1,0:T(8,128)(2,1)S(1)} %maximum_select_fusion.7), channel_id=1, source_target_pairs={{0,4},{2,6},{4,0},{6,2},{8,12},{10,14},{12,8},{14,10},{16,20},{18,... | collective-permute-start | bytes 3145736 | tf_op jit(solution)/shard_map/ppermute | solution.py:474
  578.0 58.0 %collective-permute-start.68 = (bf16[1024,512]{1,0:T(8,128)(2,1)S(1)}, bf16[1024,512]{1,0:T(8,128)(2,1)S(1)}, u32[]{:S(2)}, u32[]{:S(2)}) collective-permute-start(bf16[1024,512]{1,0:T(8,128)(2,1)S(1)} %maximum_select_fusion.8), channel_id=1, source_target_pairs={{0,4},{2,6},{4,0},{6,2},{8,12},{10,14},{12,8},{14,10},{16,20},{18,... | collective-permute-start | bytes 3145736 | tf_op jit(solution)/shard_map/ppermute | solution.py:474
  580.3 52.0 %collective-permute-start.48 = (bf16[256,512]{1,0:T(8,128)(2,1)S(1)}, bf16[256,512]{1,0:T(8,128)(2,1)S(1)}, u32[]{:S(2)}, u32[]{:S(2)}) collective-permute-start(bf16[256,512]{1,0:T(8,128)(2,1)S(1)} %maximum_select_fusion.14), channel_id=1, source_target_pairs={{0,4},{2,6},{4,0},{6,2},{8,12},{10,14},{12,8},{14,10},{16,20},{18,... | collective-permute-start | bytes 786440 | tf_op jit(solution)/shard_map/ppermute | solution.py:474
  585.1 59.8 %collective-permute-start.39 = (f32[9216]{0:T(1024)S(1)}, f32[9216]{0:T(1024)S(1)}, u32[]{:S(2)}, u32[]{:S(2)}) collective-permute-start(f32[9216]{0:T(1024)S(1)} %add.504), channel_id=1, source_target_pairs={{0,16},{2,18},{4,20},{6,22},{8,24},{10,26},{12,28},{14,30},{16,0},... | collective-permute-start | bytes 110600 | tf_op jit(solution)/shard_map/ppermute | solution.py:474
  632.5 15.4 %collective-permute-start.49 = (bf16[512,512]{1,0:T(8,128)(2,1)S(1)}, bf16[512,512]{1,0:T(8,128)(2,1)S(1)}, u32[]{:S(2)}, u32[]{:S(2)}) collective-permute-start(bf16[512,512]{1,0:T(8,128)(2,1)S(1)} %maximum_select_fusion.10), channel_id=1, source_target_pairs={{0,2},{2,0},{4,6},{6,4},{8,10},{10,8},{12,14},{14,12},{16,18},{18,... | collective-permute-start | bytes 1572872 | tf_op jit(solution)/shard_map/ppermute | solution.py:474
  634.5 15.1 %collective-permute-start.34 = (bf16[1536,512]{1,0:T(8,128)(2,1)}, bf16[1536,512]{1,0:T(8,128)(2,1)}, u32[]{:S(2)}, u32[]{:S(2)}) collective-permute-start(bf16[1536,512]{1,0:T(8,128)(2,1)} %maximum_select_fusion.5), channel_id=1, source_target_pairs={{0,2},{2,0},{4,6},{6,4},{8,10},{10,8},{12,14},{14,12},{16,18},{18,... | collective-permute-start | bytes 4718600 | tf_op jit(solution)/shard_map/ppermute | solution.py:474
  635.9 18.8 %collective-permute-start.59 = (bf16[512,2048]{1,0:T(8,128)(2,1)S(1)}, bf16[512,2048]{1,0:T(8,128)(2,1)}, u32[]{:S(2)}, u32[]{:S(2)}) collective-permute-start(bf16[512,2048]{1,0:T(8,128)(2,1)S(1)} %maximum_select_fusion.3), channel_id=1, source_target_pairs={{0,2},{2,0},{4,6},{6,4},{8,10},{10,8},{12,14},{14,12},{16,18},{18,... | collective-permute-start | bytes 6291464 | tf_op jit(solution)/shard_map/ppermute | solution.py:474
  638.1 22.6 %collective-permute-start.69 = (bf16[2048,512]{1,0:T(8,128)(2,1)}, bf16[2048,512]{1,0:T(8,128)(2,1)}, u32[]{:S(2)}, u32[]{:S(2)}) collective-permute-start(bf16[2048,512]{1,0:T(8,128)(2,1)} %maximum_select_fusion.4), channel_id=1, source_target_pairs={{0,2},{2,0},{4,6},{6,4},{8,10},{10,8},{12,14},{14,12},{16,18},{18,... | collective-permute-start | bytes 6291464 | tf_op jit(solution)/shard_map/ppermute | solution.py:474
  (104 other events, 816.6 us)

commit v2 on v0

--- a/solution.py
+++ b/solution.py
@@ -1,14 +1,17 @@
 import jax
 import jax.numpy as jnp
 from jax import lax
+from jax.experimental import pallas as pl
+from jax.experimental.pallas import tpu as pltpu
 from jax.sharding import PartitionSpec as P
 
 HEAD = 64
 PAGE = 416
-
+LANES = 128
 
 EPSILON = 1e-05
-
+F32 = jnp.float32
+LOW = jnp.bfloat16
 
 def norm_rows(matrix, norm_scale, norm_offset):
     average = jnp.mean(matrix, axis=-1, keepdims=True)
@@ -202,7 +205,7 @@
     return (grad_x, split_grads, shared_grads)
 
 
-def body(
+def spread_body(
     inputs,
     qkv_weight,
     qv_bias,
@@ -269,6 +272,1255 @@
     )
 
 
+RATE = 0.42
+POLY = (
+    0.23672758308126046,
+    0.24094666497815675,
+    0.18682847081810067,
+    0.2932523313321973,
+    -0.17452300094788806,
+    0.4864472432641871,
+    -0.34587320596419,
+    0.0761939461469462,
+)
+LARGE = 58 * 2**20
+SPEED = 30 * 1.1e9
+HEAVY = 1
+UNITS = 512
+GROUP = 256
+
+
+def gelu_pair(u):
+    t = 1.0 / (1.0 + (RATE * 0.5**0.5) * jnp.abs(u))
+    total = 0.5 * POLY[-1] * t + 0.5 * POLY[-2]
+    for factor in POLY[-3::-1]:
+        total = total * t + 0.5 * factor
+    bell = jnp.exp(u * u * -0.5)
+    tail = total * t * bell
+    below = jnp.where(u >= 0, 1.0 - tail, tail)
+    return u * below, below + u * bell * 0.3989422804014327
+
+
+def matmul(left, right, left_dim=1, right_dim=0):
+    return lax.dot_general(
+        left, right, (((left_dim,), (right_dim,)), ((), ())), preferred_element_type=F32
+    )
+
+
+def head_mask(which):
+    lane = lax.broadcasted_iota(jnp.int32, (1, LANES), 1)
+    return (lane // HEAD) == which
+
+
+def shaped(*dims, kind=F32):
+    return jax.ShapeDtypeStruct(dims, kind)
+
+
+def held(dims):
+    return pl.BlockSpec(dims, lambda *place: (0,) * len(dims), pipeline_mode=pl.Buffered(1))
+
+
+def scalar_spec():
+    return pl.BlockSpec(memory_space=pltpu.SMEM)
+
+
+TIMES = {
+    "heads": 8,
+    "heads_back": 26,
+    "units": 20,
+    "units_back": 22,
+    "project": 7,
+    "turn": 9,
+    "first_back": 10,
+    "combine": 2,
+    "join_rows": 2,
+    "take_blocks": 3,
+    "split_blocks": 2,
+    "join_depth": 3,
+    "finish": 6,
+}
+
+
+def cost_of(name):
+    return pl.CostEstimate(
+        flops=int((TIMES[name] if TIMES[name] < 5 else TIMES[name] * HEAVY) * SPEED), bytes_accessed=1, transcendentals=0
+    )
+
+
+def run(kernel, name, grid, in_specs, out_specs, out_shape, operands, scratch=()):
+    return pl.pallas_call(
+        kernel,
+        grid=grid,
+        in_specs=in_specs,
+        out_specs=out_specs,
+        out_shape=out_shape,
+        scratch_shapes=list(scratch),
+        compiler_params=pltpu.CompilerParams(vmem_limit_bytes=LARGE),
+        cost_estimate=cost_of(name),
+        name=name,
+    )(*operands)
+
+
+def spans(pair):
+    return [
+        slice(start * GROUP + pair * LANES, start * GROUP + (pair + 1) * LANES)
+        for start in range(3)
+    ]
+
+
+def gather_depth(order_ref, refs, target, by_column):
+    for relative, ref in enumerate(refs):
+        span = pl.ds(pl.multiple_of((order_ref[0] ^ relative) * QUARTER, QUARTER), QUARTER)
+        if by_column:
+            target[:, span] = ref[0]
+        else:
+            for member in range(3):
+                target[span, member * GROUP : (member + 1) * GROUP] = ref[0, member]
+
+
+QUARTER = 256
+
+
+def qkv_specs(quarters, part):
+    shape = (1, 3, QUARTER, GROUP)
+    if len(quarters) == 1:
+        return [
+            pl.BlockSpec(
+                shape,
+                lambda page, number=number: (0, 0, number, part),
+                pipeline_mode=pl.Buffered(1),
+            )
+            for number in range(4)
+        ]
+    return [held(shape)] * 4
+
+
+def four_times(quarters):
+    return list(quarters) * (4 // len(quarters))
+
+
+def heads_kernel(order_ref, w0_ref, w1_ref, w2_ref, w3_ref, x_ref, b_ref, *refs):
+    three_ref, o_ref, lse_ref, weight = refs[-4:]
+
+    @pl.when(pl.program_id(0) == 0)
+    def _():
+        gather_depth(order_ref, (w0_ref, w1_ref, w2_ref, w3_ref), weight, False)
+
+    scaled = matmul(x_ref[...], weight[...]) + b_ref[...]
+    three_ref[:, :GROUP] = (scaled[:, :GROUP] * 0.125).astype(LOW)
+    three_ref[:, GROUP:] = scaled[:, GROUP:].astype(LOW)
+    for pair in range(GROUP // LANES):
+        queries, key_rows, values = (three_ref[:, entry] for entry in spans(pair))
+        values_t = values.T
+        columns = []
+        for which in range(LANES // HEAD):
+            head = pair * (LANES // HEAD) + which
+            keys_one = jnp.where(head_mask(which), key_rows, jnp.zeros_like(key_rows))
+            scores = matmul(keys_one, queries, 1, 1)
+            peak = jnp.max(scores, axis=0, keepdims=True)
+            exponent = jnp.exp(scores - peak)
+            denominator = jnp.sum(exponent, axis=0, keepdims=True)
+            weights_low = (exponent * (1.0 / denominator)).astype(LOW)
+            columns.append(matmul(values_t[which * HEAD : (which + 1) * HEAD], weights_low))
+            lse_ref[0, 0, head : head + 1, :] = peak + jnp.log(denominator)
+        o_ref[:, pair * LANES : (pair + 1) * LANES] = (
+            jnp.concatenate(columns, axis=0).T.astype(LOW)
+        )
+
+
+def heads_forward(order, quarters, x_low, bias, part, parts, before=()):
+    rows, depth = x_low.shape
+    width = 3 * GROUP
+    pages = rows // PAGE
+    count = GROUP // HEAD
+    return pl.pallas_call(
+        heads_kernel,
+        grid=(pages,),
+        in_specs=[scalar_spec()]
+        + qkv_specs(quarters, part)
+        + [pl.BlockSpec((PAGE, depth), lambda page: (page, 0)), held((1, width))]
+        + [pl.BlockSpec(memory_space=pl.ANY)] * len(before),
+        out_specs=[
+            pl.BlockSpec((PAGE, width), lambda page: (page, part)),
+            pl.BlockSpec((PAGE, GROUP), lambda page: (page, part)),
+            pl.BlockSpec((1, 1, count, PAGE), lambda page: (part, page, 0, 0)),
+        ],
+        out_shape=[
+            shaped(rows, parts * width, kind=LOW),
+            shaped(rows, parts * GROUP, kind=LOW),
+            shaped(parts, pages, count, PAGE),
+        ],
+        scratch_shapes=[pltpu.VMEM((depth, width), LOW)],
+        input_output_aliases={7 + number: number for number in range(len(before))},
+        compiler_params=pltpu.CompilerParams(vmem_limit_bytes=LARGE),
+        cost_estimate=cost_of("heads"),
+        name="heads",
+    )(order, *four_times(quarters), x_low, bias, *before)
+
+
+def heads_back_kernel(core_ref, order_ref, x_ref, g_ref, before_ref, *refs):
+    keep_ref, send_ref, gx_ref, sum_ref = refs[22:26]
+    qkv_total, out_total, weight, out_weight = refs[26:]
+    side, page = pl.program_id(0), pl.program_id(1)
+    pages = pl.num_programs(1)
+    core = core_ref[0]
+    half = x_ref.shape[1] // 2
+
+    def work(order, first_side, three_ref, lse_ref, att_ref, *weights):
+        @pl.when(page == 0)
+        def _():
+            gather_depth(order, weights[:4], weight, False)
+            gather_depth(order, weights[4:], out_weight, True)
+
+        mix = matmul(g_ref[...], out_weight[...], 1, 1).astype(LOW)
+        grads_three = [None] * (3 * (GROUP // LANES))
+        for pair in range(GROUP // LANES):
+            queries, key_rows, values = (three_ref[:, entry] for entry in spans(pair))
+            grads = mix[:, pair * LANES : (pair + 1) * LANES]
+            keys_t = key_rows.T
+            columns, dk_parts, dv_parts = [], [], []
+            for which in range(LANES // HEAD):
+                head = pair * (LANES // HEAD) + which
+                mask = head_mask(which)
+                keys_one = jnp.where(mask, key_rows, jnp.zeros_like(key_rows))
+                scores = matmul(keys_one, queries, 1, 1)
+                probability = jnp.exp(scores - lse_ref[0, 0, head : head + 1, :])
+                values_one = jnp.where(mask, values, jnp.zeros_like(values))
+                grad_prob = matmul(values_one, grads, 1, 1)
+                inner = jnp.sum(probability * grad_prob, axis=0, keepdims=True)
+                grad_scores = (probability * (grad_prob - inner)).astype(LOW)
+                dv_parts.append(matmul(probability.astype(LOW), grads))
+                dk_parts.append(matmul(grad_scores, queries))
+                columns.append(matmul(keys_t[which * HEAD : (which + 1) * HEAD], grad_scores))
+            first = head_mask(0)
+            grad_q = jnp.concatenate(columns, axis=0).T.astype(LOW)
+            grads_three[pair] = (grad_q.astype(F32) * 0.125).astype(LOW)
+            grads_three[2 + pair] = jnp.where(first, dk_parts[0], dk_parts[1]).astype(LOW)
+            grads_three[4 + pair] = jnp.where(first, dv_parts[0], dv_parts[1]).astype(LOW)
+        three = jnp.concatenate(grads_three, axis=1)
+        start = page == 0
+        sums = jnp.sum(three.astype(F32), axis=0, keepdims=True)
+        sum_ref[0] = jnp.where(start, 0.0, sum_ref[0]) + sums
+        product = matmul(x_ref[...], three, 0, 0)
+        qkv_total[...] = jnp.where(start, 0.0, qkv_total[...]) + product
+        product = matmul(att_ref[...], g_ref[...], 0, 0)
+        out_total[...] = jnp.where(start, 0.0, out_total[...]) + product
+        rows = pl.ds(pl.multiple_of(page * PAGE, PAGE), PAGE)
+        before = before_ref[...] if first_side else gx_ref[rows, :]
+        gx_ref[rows, :] = before + matmul(three, weight[...], 1, 1)
+
+    @pl.when(side == 0)
+    def _():
+        work((0,), True, *refs[:11])
+
+    @pl.when(side == 1)
+    def _():
+        work(order_ref, False, *refs[11:22])
+
+    @pl.when(page == pages - 1)
+    def _():
+        for ref, number in ((keep_ref, core), (send_ref, 1 - core)):
+            start = pl.multiple_of(number * half, half)
+            for member in range(3):
+                span = slice(member * GROUP, (member + 1) * GROUP)
+                ref[member] = qkv_total[pl.ds(start, half), span].astype(LOW)
+            for member in range(2):
+                column = pl.ds(pl.multiple_of(number * half + member * GROUP, GROUP), GROUP)
+                ref[3, member * GROUP : (member + 1) * GROUP, :] = out_total[:, column].astype(LOW)
+
+
+def heads_back(core, order, saved, part, x_low, grad_low, qkv, out, before):
+    rows, depth = x_low.shape
+    width = 3 * GROUP
+    pages = rows // PAGE
+    count = GROUP // HEAD
+    half = depth // 2
+    block = pl.BlockSpec((4, half, GROUP), lambda side, page: (side, 0, 0))
+    line = pl.BlockSpec((PAGE, depth), lambda side, page: (page, 0))
+    once = pl.BlockSpec(
+        (PAGE, depth), lambda side, page: (jnp.where(side == 0, page, pages - 1), 0)
+    )
+    in_specs, operands = [], []
+    for number, side in enumerate(("own", "other")):
+
+        def page_of(side, page, number=number):
+            return jnp.where(side == number, page, 0 if number else pages - 1)
+
+        def beside(side, page, page_of=page_of):
+            return (page_of(side, page), part)
+
+        def above(side, page, page_of=page_of):
+            return (part, page_of(side, page), 0, 0)
+
+        in_specs += [
+            pl.BlockSpec((PAGE, width), beside),
+            pl.BlockSpec((1, 1, count, PAGE), above),
+            pl.BlockSpec((PAGE, GROUP), beside),
+        ]
+        for quarter in range(4):
+            fixed = (0, 0, quarter, part) if side == "own" else (0, 0, 0, 0)
+            in_specs.append(
+                pl.BlockSpec(
+                    (1, 3, QUARTER, GROUP),
+                    lambda side, page, fixed=fixed: fixed,
+                    pipeline_mode=pl.Buffered(1),
+                )
+            )
+        for quarter in range(4):
+            fixed = (0, part, quarter if side == "own" else 0)
+            in_specs.append(
+                pl.BlockSpec(
+                    (1, GROUP, QUARTER),
+                    lambda side, page, fixed=fixed: fixed,
+                    pipeline_mode=pl.Buffered(1),
+                )
+            )
+        three, attended, lse = saved[side]
+        operands += [three, lse, attended, *four_times(qkv[side]), *four_times(out[side])]
+    return run(
+        heads_back_kernel,
+        "heads_back",
+        (2, pages),
+        [scalar_spec(), scalar_spec(), line, line, once] + in_specs,
+        [
+            block,
+            block,
+            held((rows, depth)),
+            pl.BlockSpec((1, 1, width), lambda side, page: (side, 0, 0)),
+        ],
+        [
+            shaped(8, half, GROUP, kind=LOW),
+            shaped(8, half, GROUP, kind=LOW),
+            shaped(rows, depth),
+            shaped(2, 1, width),
+        ],
+        (core, order, x_low, grad_low, before, *operands),
+        [
+            pltpu.VMEM((depth, width), F32),
+            pltpu.VMEM((GROUP, depth), F32),
+            pltpu.VMEM((depth, width), LOW),
+            pltpu.VMEM((GROUP, depth), LOW),
+        ],
+    )
+
+
+ROW_STEPS = 4
+
+
+def pair_specs(pair, shape, axis, first=0):
+    def place(step, number):
+        return (0, number, step + first) if axis == 1 else (0, step + first, number)
+
+    if len(pair) == 1:
+        return [
+            pl.BlockSpec((1,) + shape, lambda step, number=number: place(step, number))
+            for number in range(2)
+        ]
+    return [pl.BlockSpec((1,) + shape, lambda step: place(step, 0)) for _ in range(2)]
+
+
+def twice(pair):
+    return list(pair) * (2 // len(pair))
+
+
+def depth_spans(order_ref, half):
+    return [
+        pl.ds(pl.multiple_of((order_ref[0] ^ relative) * half, half), half)
+        for relative in range(2)
+    ]
+
+
+def units_kernel(order_ref, h_ref, up_a, up_b, b_ref, down_a, down_b, *outs):
+    active_ref, slope_ref, total_ref = outs
+    rows = h_ref.shape[0] // ROW_STEPS
+    first, second = depth_spans(order_ref, h_ref.shape[1] // 2)
+    for part in range(ROW_STEPS):
+        span = slice(part * rows, (part + 1) * rows)
+        pre = matmul(h_ref[span, first], up_a[0]) + matmul(h_ref[span, second], up_b[0])
+        value, slope = gelu_pair(pre + b_ref[...])
+        value = value.astype(LOW)
+        active_ref[span, :] = value
+        slope_ref[span, :] = slope.astype(LOW)
+        for place, weight in ((first, down_a), (second, down_b)):
+            before = jnp.where(pl.program_id(0) == 0, 0.0, total_ref[span, place])
+            total_ref[span, place] = before + matmul(value, weight[0])
+
+
+def units_forward(order, hidden_low, up, bias, down):
+    rows, depth = hidden_low.shape
+    units = bias.shape[1]
+    half = depth // 2
+    column = pl.BlockSpec((rows, UNITS), lambda step: (0, step))
+    return run(
+        units_kernel,
+        "units",
+        (units // UNITS,),
+        [scalar_spec(), held((rows, depth))]
+        + pair_specs(up, (half, UNITS), 1)
+        + [pl.BlockSpec((1, UNITS), lambda step: (0, step))]
+        + pair_specs(down, (UNITS, half), 2),
+        [column, column, held((rows, depth))],
+        [shaped(rows, units, kind=LOW), shaped(rows, units, kind=LOW), shaped(rows, depth)],
+        (order, hidden_low, *twice(up), bias, *twice(down)),
+    )
+
+
+def units_back_kernel(core_ref, order_ref, g_ref, h_ref, *refs):
+    keep_ref, send_ref, total_ref, sum_ref = refs[-4:]
+    core = core_ref[0]
+    half = g_ref.shape[1] // 2
+    step = pl.program_id(0)
+    steps = pl.num_programs(0) // 2
+
+    def work(order, active_ref, slope_ref, up_a, up_b, down_a, down_b):
+        first, second = depth_spans(order, half)
+        grad = matmul(g_ref[:, first], down_a[0], 1, 1)
+        grad = grad + matmul(g_ref[:, second], down_b[0], 1, 1)
+        grad_low = (grad * slope_ref[...].astype(F32)).astype(LOW)
+        sum_ref[0] = jnp.sum(grad_low.astype(F32), axis=0, keepdims=True)
+        for place, weight in ((first, up_a), (second, up_b)):
+            before = jnp.where(step == 0, 0.0, total_ref[:, place])
+            total_ref[:, place] = before + matmul(grad_low, weight[0], 1, 1)
+        for ref, number in ((keep_ref, core), (send_ref, 1 - core)):
+            span = pl.ds(pl.multiple_of(number * half, half), half)
+            ref[0] = matmul(active_ref[...], g_ref[:, span], 0, 0).astype(LOW)
+            ref[1] = matmul(h_ref[:, span], grad_low, 0, 0).astype(LOW)
+
+    @pl.when(step < steps)
+    def _():
+        work((0,), *refs[:6])
+
+    @pl.when(step >= steps)
+    def _():
+        work(order_ref, *refs[6:12])
+
+
+def units_back(core, order, grad_low, hidden_low, units, up, down, part, parts):
+    rows, depth = hidden_low.shape
+    here = units["own"][0].shape[1] // parts
+    half = depth // 2
+    steps = here // UNITS
+    first = part * steps
+    in_specs, operands = [], []
+    for side, least in (("own", 0), ("other", steps)):
+
+        def number(step, least=least):
+            return first + jnp.clip(step - least, 0, steps - 1)
+
+        column = pl.BlockSpec((rows, UNITS), lambda step, number=number: (0, number(step)))
+        in_specs += [column, column]
+        for axis, pair, shape in ((1, up, (half, UNITS)), (2, down, (UNITS, half))):
+            for which in range(2):
+                fixed = which if side == "own" else 0
+
+                def place(step, axis=axis, fixed=fixed, number=number):
+                    moving = number(step)
+                    return (0, fixed, moving) if axis == 1 else (0, moving, fixed)
+
+                in_specs.append(pl.BlockSpec((1,) + shape, place))
+        operands += [*units[side][:2], *twice(up[side]), *twice(down[side])]
+    block = pl.BlockSpec((2, half, UNITS), lambda step: (step, 0, 0))
+    return run(
+        units_back_kernel,
+        "units_back",
+        (2 * steps,),
+        [scalar_spec(), scalar_spec(), held((rows, depth)), held((rows, depth))] + in_specs,
+        [
+            block,
+            block,
+            held((rows, depth)),
+            pl.BlockSpec((1, 1, UNITS), lambda step: (step, 0, 0)),
+        ],
+        [
+            shaped(4 * steps, half, UNITS, kind=LOW),
+            shaped(4 * steps, half, UNITS, kind=LOW),
+            shaped(rows, depth),
+            shaped(2 * steps, 1, UNITS),
+        ],
+        (core, order, grad_low, hidden_low, *operands),
+    )
+
+
+def normal_rows(matrix):
+    average = jnp.mean(matrix, axis=-1, keepdims=True)
+    centered = matrix - average
+    variance = jnp.mean(centered * centered, axis=-1, keepdims=True)
+    scale = lax.rsqrt(variance + EPSILON)
+    return centered * scale, scale
+
+
+def normal_back(normal, scale, gain, grad):
+    scaled = gain * grad
+    level = jnp.mean(scaled, axis=-1, keepdims=True)
+    along = jnp.mean(scaled * normal, axis=-1, keepdims=True)
+    return scale * (scaled - level - normal * along)
+
+
+def add_rows(ref, matrix):
+    total = jnp.sum(matrix, axis=0, keepdims=True)
+    before = jnp.where(pl.program_id(0) == 0, 0.0, ref[...])
+    ref[...] = before + total
+
+
+STRIP = 208
+
+
+def strip(columns):
+    return pl.BlockSpec((STRIP, columns), lambda step: (step, 0))
+
+
+def project_kernel(order_ref, a_ref, b_ref, wa_ref, w0, w1, w2, w3, x_ref, *refs):
+    bias_ref, g_ref, s_ref, first_ref, hidden_ref, low_ref = refs
+    first_ref[...] = x_ref[...].astype(F32) + bias_ref[...] + matmul(a_ref[...], wa_ref[0])
+    for relative, weight in enumerate((w0, w1, w2, w3)):
+        span = pl.ds(pl.multiple_of((order_ref[0] ^ relative) * QUARTER, QUARTER), QUARTER)
+        first_ref[:, span] += matmul(b_ref[...], weight[0])
+    hidden = normal_rows(first_ref[...])[0] * g_ref[...] + s_ref[...]
+    hidden_ref[...] = hidden
+    low_ref[...] = hidden.astype(LOW)
+
+
+def project(order, sides, own, quarters, x_low, bias, gain, shift):
+    rows, depth = x_low.shape
+    line = held((1, depth))
+    page = pl.BlockSpec((PAGE, depth), lambda step: (step, 0))
+    side = pl.BlockSpec((PAGE, sides[0].shape[1]), lambda step: (step, 0))
+    return run(
+        project_kernel,
+        "project",
+        (rows // PAGE,),
+        [scalar_spec(), side, side, held(own.shape)]
+        + [held(entry.shape) for entry in quarters]
+        + [page, line, line, line],
+        [page] * 3,
+        [shaped(rows, depth), shaped(rows, depth), shaped(rows, depth, kind=LOW)],
+        (order, *sides, own, *quarters, x_low, bias, gain, shift),
+    )
+
+
+def turn_kernel(a_ref, b_ref, h_ref, c_ref, bias_ref, g_ref, s_ref, *outs):
+    out_ref, grad_ref, low_ref, gain_ref, shift_ref, sum_ref = outs
+    normal, scale = normal_rows(h_ref[...] + (a_ref[...] + b_ref[...]) + bias_ref[...])
+    out_ref[...] = normal * g_ref[...] + s_ref[...]
+    grad_out = c_ref[...].astype(F32)
+    grad = normal_back(normal, scale, g_ref[...], grad_out)
+    grad_ref[...] = grad
+    low_ref[...] = grad.astype(LOW)
+    add_rows(gain_ref, grad_out * normal)
+    add_rows(shift_ref, grad_out)
+    add_rows(sum_ref, grad)
+
+
+def turn(sides, hidden, cotangent, bias, gain, shift):
+    rows, depth = hidden.shape
+    line = pl.BlockSpec((1, depth), lambda step: (0, 0))
+    return run(
+        turn_kernel,
+        "turn",
+        (rows // STRIP,),
+        [strip(depth)] * 4 + [line] * 3,
+        [strip(depth)] * 3 + [line] * 3,
+        [shaped(rows, depth), shaped(rows, depth), shaped(rows, depth, kind=LOW)]
+        + [shaped(1, depth)] * 3,
+        (*sides, hidden, cotangent, bias, gain, shift),
+    )
+
+
+def first_back_kernel(*refs):
+    *sides, second_ref, first_ref, g_ref = refs[:-5]
+    grad_ref, low_ref, gain_ref, shift_ref, sum_ref = refs[-5:]
+    total = second_ref[...]
+    for side in sides:
+        total = total + side[...]
+    normal, scale = normal_rows(first_ref[...])
+    grad = normal_back(normal, scale, g_ref[...], total)
+    grad_ref[...] = grad
+    low_ref[...] = grad.astype(LOW)
+    add_rows(gain_ref, total * normal)
+    add_rows(shift_ref, total)
+    add_rows(sum_ref, grad)
+
+
+def first_back(sides, grad_second, pre_first, gain):
+    rows, depth = pre_first.shape
+    line = pl.BlockSpec((1, depth), lambda step: (0, 0))
+    return run(
+        first_back_kernel,
+        "first_back",
+        (rows // STRIP,),
+        [strip(depth)] * (len(sides) + 2) + [line],
+        [strip(depth)] * 2 + [line] * 3,
+        [shaped(rows, depth), shaped(rows, depth, kind=LOW)] + [shaped(1, depth)] * 3,
+        (*sides, grad_second, pre_first, gain),
+    )
+
+
+def swap(value, distance, axis="dp"):
+    count = lax.axis_size(axis)
+    return lax.ppermute(value, axis, [(place, place ^ distance) for place in range(count)])
+
+
+def bit_of(place, distance):
+    return jnp.minimum(jnp.bitwise_and(place, distance), 1).astype(jnp.int32)
+
+
+def cut(value, number, count, axis):
+    size = value.shape[axis] // count
+    return lax.dynamic_slice_in_dim(value, number * size, size, axis)
+
+
+def ordered(bit, mine, theirs, axis):
+    return jnp.where(
+        bit == 0,
+        jnp.concatenate([mine, theirs], axis),
+        jnp.concatenate([theirs, mine], axis),
+    )
+
+
+def hold(value, *tokens):
+    return lax.optimization_barrier((value,) + tokens)[0] if tokens else value
+
+
+def take_blocks(words, sources):
+    count = len(sources)
+
+    def kernel(word_ref, *refs):
+        for source, target in zip(refs[:count], refs[count:]):
+            target[...] = source[...]
+
+    return pl.pallas_call(
+        kernel,
+        grid_spec=pltpu.PrefetchScalarGridSpec(
+            num_scalar_prefetch=1,
+            grid=(1,),
+            in_specs=[
+                pl.BlockSpec(shape, lambda step, word, index=index: index(word))
+                for _, shape, index in sources
+            ],
+            out_specs=[
+                pl.BlockSpec(shape, lambda step, word, shape=shape: (0,) * len(shape))
+                for _, shape, _ in sources
+            ],
+        ),
+        out_shape=[shaped(*shape, kind=LOW) for _, shape, _ in sources],
+        compiler_params=pltpu.CompilerParams(vmem_limit_bytes=LARGE),
+        cost_estimate=cost_of("take_blocks"),
+        name="take_blocks",
+    )(words, *[array for array, _, _ in sources])
+
+
+def split_blocks(first, second, axis):
+    half = first.shape[axis] // 2
+    shape = first.shape[:axis] + (half,) + first.shape[axis + 1 :]
+
+    def kernel(first_ref, second_ref, low_ref, high_ref):
+        if axis == 2:
+            low_ref[...] = first_ref[:, :, :half]
+            high_ref[...] = second_ref[:, :, half:]
+        else:
+            low_ref[...] = first_ref[:, :half]
+            high_ref[...] = second_ref[:, half:]
+
+    return run(
+        kernel,
+        "split_blocks",
+        (1,),
+        [held(first.shape), held(second.shape)],
+        [held(shape), held(shape)],
+        [shaped(*shape, kind=first.dtype)] * 2,
+        (first, second),
+    )
+
+
+def join_depth(words, piece, beside, above, low_part, high_part, axis):
+    size = piece.shape[axis]
+    shape = piece.shape[:axis] + (4 * size,) + piece.shape[axis + 1 :]
+    half = low_part.shape[3 - axis]
+
+    def kernel(word_ref, piece_ref, beside_ref, above_ref, low_ref, high_ref, target):
+        place = word_ref[2] % 4
+
+        def span(number):
+            return pl.ds(pl.multiple_of(number * size, size), size)
+
+        for ref, number in ((piece_ref, place), (beside_ref, place ^ 2), (above_ref, place ^ 1)):
+            if axis == 1:
+                target[:, span(number)] = ref[...]
+            else:
+                target[:, :, span(number)] = ref[...]
+        last = span(place ^ 3)
+        if axis == 1:
+            target[:, last, :half] = low_ref[...]
+            target[:, last, half:] = high_ref[...]
+        else:
+            target[:, :half, last] = low_ref[...]
+            target[:, half:, last] = high_ref[...]
+
+    entries = [piece, beside, above, low_part, high_part]
+    return run(
+        kernel,
+        "join_depth",
+        (1,),
+        [scalar_spec()] + [held(entry.shape) for entry in entries],
+        held(shape),
+        shaped(*shape, kind=piece.dtype),
+        (words, *entries),
+    )
+
+
+class FetchQuarters:
+    def __init__(self, clock, piece):
+        self.clock = clock
+        self.piece = swap(piece, 1, "mp")
+        self.stages = [self.share, self.last]
+
+    def step(self):
+        self.stages.pop(0)()
+
+    def share(self):
+        self.piece = self.clock.hold(self.piece)
+        self.clock.tick(self.piece)
+        self.beside = swap(self.piece, 2)
+        self.core_piece = swap(self.piece, 1)
+
+    def last(self):
+        self.beside = self.clock.hold(self.beside)
+        self.clock.tick(self.beside)
+        self.parts = (self.piece, self.beside, self.core_piece, swap(self.beside, 1))
+
+
+class FetchHalves:
+    def __init__(self, clock, words, piece, axis):
+        self.clock, self.words, self.axis = clock, words, axis
+        self.piece = swap(piece, 1, "mp")
+        self.stages = [self.share, self.cross, self.join]
+
+    def step(self):
+        self.stages.pop(0)()
+
+    def share(self):
+        self.piece = self.clock.hold(self.piece)
+        self.clock.tick(self.piece)
+        self.near = [swap(self.piece, distance) for distance in (2, 4)]
+
+    def cross(self):
+        beside, above = self.near
+        low_part, high_part = split_blocks(self.clock.hold(beside), above, 3 - self.axis)
+        self.clock.tick(low_part, high_part)
+        self.far = [swap(low_part, 4), swap(high_part, 2)]
+
+    def join(self):
+        beside, above = self.near
+        mine = join_depth(
+            self.words, self.clock.hold(self.piece), beside, above, *self.far, self.axis
+        )
+        self.clock.tick(mine)
+        self.parts = (mine, swap(mine, 1))
+
+
+class Clock:
+    def __init__(self):
+        self.tokens = ()
+
+    def hold(self, value):
+        return hold(value, *self.tokens)
+
+    def tick(self, *values):
+        self.tokens = values
+
+
+def combine(words, sides, count, cut_by):
+    terms = [term for side in sides for term in side]
+    _, rows, columns = terms[0][0].shape
+    ways = 2 if cut_by else 1
+    size = rows // ways
+
+    def kernel(word_ref, *refs):
+        sources, targets = list(refs[: len(terms)]), list(refs[len(terms) :])
+        leaving = [targets.pop(0) for _ in range(ways - 1)]
+        place = (word_ref[0] // cut_by) % 2 if cut_by else 0
+        for number, side in enumerate(sides):
+            mine = [sources.pop(0) for _ in side]
+
+            def total(relative):
+                span = slice(None)
+                if ways > 1:
+                    span = pl.ds(pl.multiple_of((place ^ relative) * size, size), size)
+                values = [ref[:, span, :].astype(F32) for ref in mine]
+                return sum(values[1:], values[0]).astype(LOW)
+
+            targets[number][...] = total(0)
+            for relative, target in enumerate(leaving, 1):
+                target[number * count : (number + 1) * count] = total(relative)
+
+    def block(number):
+        return pl.BlockSpec((count, rows, columns), lambda step: (number, 0, 0))
+
+    shapes = [(count * len(sides), size, columns)] * (ways - 1) + [(count, size, columns)] * len(sides)
+    return run(
+        kernel,
+        "combine",
+        (1,),
+        [scalar_spec()] + [block(number) for _, number in terms],
+        [held(shape) for shape in shapes],
+        [shaped(*shape, kind=LOW) for shape in shapes],
+        (words, *[array for array, _ in terms]),
+    )
+
+
+def join_rows(words, entries, distance):
+    ways = len(entries)
+    count, size, columns = entries[0].shape
+    shape = (count, ways * size, columns)
+
+    def kernel(word_ref, *refs):
+        target = refs[-1]
+        place = (word_ref[0] // distance) % 2
+        for relative, ref in enumerate(refs[:-1]):
+            target[:, pl.ds(pl.multiple_of((place ^ relative) * size, size), size), :] = ref[...]
+
+    return run(
+        kernel,
+        "join_rows",
+        (1,),
+        [scalar_spec()] + [held(entry.shape) for entry in entries],
+        held(shape),
+        shaped(*shape, kind=LOW),
+        (words, *entries),
+    )
+
+
+class Piece:
+    def __init__(self, clock, words, order, source, count):
+        self.clock, self.words = clock, words
+        self.order = list(order)
+        self.back = [ways for ways in reversed(order) if ways != "x"]
+        self.source = source
+        self.count = count
+        self.flight = None
+        self.kept = None
+        self.complete = False
+
+    def add(self, sides):
+        array, number = sides[0][0]
+        sides[0][0] = (self.clock.hold(array), number)
+        ways = self.order[0] if self.order else None
+        sums = combine(self.words, sides, self.count, None if ways == "x" else ways)
+        self.clock.tick(sums[0])
+        if ways == "x":
+            self.flight = [swap(sums[-1], 1, "mp")]
+            self.kept = [[(entry, 0)] for entry in sums[:-1]]
+        elif ways:
+            self.flight = [swap(sums[0], ways)]
+            self.kept = [[(entry, 0)] for entry in sums[1:]]
+        else:
+            self.total = sums[0]
+            self.gather()
+
+    def gather(self):
+        self.flight = [swap(self.total, self.back[0] if self.back else 1)]
+
+    def step(self):
+        if self.flight is None:
+            first = [(1,), (0, 1)][self.order[0] != "x"]
+            self.add([self.source(side) for side in first])
+            return
+        if self.order:
+            self.order.pop(0)
+            sides = self.kept or [self.source(0)]
+            for number, side in enumerate(sides):
+                side += [(array, number) for array in self.flight]
+            self.add(sides)
+            return
+        if not self.back:
+            self.flight = [self.clock.hold(self.flight[0])]
+            self.clock.tick(self.flight[0])
+            self.complete = True
+            return
+        distance = self.back.pop(0)
+        entries = [self.clock.hold(self.total)] + self.flight
+        self.total = join_rows(self.words, entries, distance)
+        self.clock.tick(self.total)
+        self.gather()
+
+
+def finish_units(core, ends):
+    count, half, units = ends[0].shape
+    entries = count // 2
+    parts = len(ends) // 2
+
+    def kernel(core_ref, *refs):
+        down_ref, up_ref = refs[-2:]
+        for part in range(parts):
+
+            @pl.when(pl.program_id(0) // entries == part)
+            def _():
+                for ref, number in ((refs[2 * part], core_ref[0]), (refs[2 * part + 1], 1 - core_ref[0])):
+                    span = pl.ds(pl.multiple_of(number * half, half), half)
+                    down_ref[:, span] = ref[0].astype(F32)
+                    up_ref[span, :] = ref[1].astype(F32)
+
+    def block(part):
+        return pl.BlockSpec(
+            (2, half, units), lambda step: (jnp.clip(step - part * entries, 0, entries - 1), 0, 0)
+        )
+
+    total = entries * parts * units
+    return run(
+        kernel,
+        "finish",
+        (entries * parts,),
+        [scalar_spec()] + [block(number // 2) for number in range(len(ends))],
+        [
+            pl.BlockSpec((half, 2 * half), lambda step: (step, 0)),
+            pl.BlockSpec((2 * half, units), lambda step: (0, step)),
+        ],
+        [shaped(total, 2 * half), shaped(2 * half, total)],
+        (core, *ends),
+    )
+
+
+def finish_heads(core, ends):
+    _, half, group = ends[0].shape
+    parts = len(ends) // 2
+
+    def kernel(core_ref, *refs):
+        qkv_ref, out_ref = refs[-2:]
+        for part in range(parts):
+
+            @pl.when(pl.program_id(0) == part)
+            def _():
+                for ref, number in ((refs[2 * part], core_ref[0]), (refs[2 * part + 1], 1 - core_ref[0])):
+                    span = pl.ds(pl.multiple_of(number * half, half), half)
+                    for member in range(3):
+                        qkv_ref[member, span, :] = ref[member].astype(F32)
+                    for member in range(half // group):
+                        start = pl.multiple_of(number * half + member * group, group)
+                        rows = slice(member * group, (member + 1) * group)
+                        out_ref[:, pl.ds(start, group)] = ref[3, rows, :].astype(F32)
+
+    return run(
+        kernel,
+        "finish",
+        (parts,),
+        [scalar_spec()] + [held(entry.shape) for entry in ends],
+        [
+            pl.BlockSpec((3, 2 * half, group), lambda step: (0, 0, step)),
+            pl.BlockSpec((group, 2 * half), lambda step: (step, 0)),
+        ],
+        [shaped(3, 2 * half, parts * group), shaped(parts * group, 2 * half)],
+        (core, *ends),
+    )
+
+
+MLP_ORDERS = (("x", 2, 4, 8), (2, "x", 4, 8))
+HEAD_ORDERS = ((2, "x", 4, 8), (2, "x", 4, 8))
+FORWARD = (
+    ("own", 0),
+    "a",
+    ("own", 1),
+    "b",
+    "a",
+    "out",
+    "up",
+    ("other", 0),
+    "b",
+    "out",
+    "down",
+    ("other", 1),
+    "up",
+    "project",
+    "down",
+    "up",
+    "units",
+    "down",
+)
+BACKWARD = (
+    ("ub", 0),
+    ("ub", 1),
+    ("m", 0),
+    ("fb",),
+    ("m", 1),
+    ("hb", 0),
+    ("hb", 1),
+    ("m", 0),
+    ("m", 1),
+    ("h", 0),
+    ("h", 1),
+    ("m", 0),
+    ("m", 1),
+    ("m", 0),
+    ("h", 0),
+    ("m", 1),
+    ("m", 0),
+    ("h", 1),
+    ("h", 0),
+    ("m", 1),
+    ("m", 0),
+    ("h", 1),
+    ("h", 0),
+    ("m", 1),
+    ("m", 0),
+    ("h", 1),
+    ("h", 0),
+    ("m", 1),
+    ("h", 1),
+    ("m", 0),
+    ("h", 0),
+    ("h", 1),
+    ("m", 0),
+    ("h", 0),
+    ("m", 1),
+    ("h", 1),
+    ("m", 1),
+    ("h", 0),
+    ("h", 1),
+    ("h", 0),
+    ("h", 1),
+)
+
+
+def whole_page_body(
+    inputs,
+    qkv_weight,
+    qv_bias,
+    out_weight,
+    out_bias,
+    norm_gain,
+    norm_shift,
+    up_weight,
+    up_bias,
+    down_weight,
+    down_bias,
+    cotangent,
+):
+    place = lax.axis_index("dp")
+    core, beside, above = (bit_of(place, distance) for distance in (1, 2, 4))
+    words = jnp.stack([place, core * 2 + beside, core * 4 + beside * 2 + above, core])
+    words = words.astype(jnp.int32)
+    core_word, quarter_word = words[3:4], words[1:2]
+    nothing = jnp.zeros((1,), jnp.int32)
+    quarter_order = {"own": nothing, "other": quarter_word}
+    half_order = {"own": nothing, "other": core_word}
+    width = qv_bias.shape[2]
+    parts = width // GROUP
+    rows, depth = inputs.shape
+    units_here = up_bias.shape[1]
+    clock = Clock()
+
+    def qkv_block(part):
+        return (qkv_weight, (1, 3, QUARTER, GROUP), lambda word: (0, 0, word[1], part))
+
+    pieces_now = take_blocks(words, [qkv_block(0), qkv_block(1)])
+    clock.tick(pieces_now[0])
+    fetch = {name: FetchQuarters(clock, piece) for name, piece in zip("ab", pieces_now)}
+    pieces_now = take_blocks(
+        words,
+        [
+            (clock.hold(out_weight), (1, width, QUARTER), lambda word: (0, 0, word[1])),
+            (up_weight, (1, depth // 8, units_here), lambda word: (0, word[2], 0)),
+            (down_weight, (1, units_here, depth // 8), lambda word: (0, 0, word[2])),
+        ],
+    )
+    clock.tick(pieces_now[0])
+    fetch["out"] = FetchQuarters(clock, pieces_now[0])
+    fetch["up"] = FetchHalves(clock, words, pieces_now[1], 1)
+    fetch["down"] = FetchHalves(clock, words, pieces_now[2], 2)
+    biases = jnp.concatenate([qv_bias[0].reshape(-1), up_bias[0]])
+    biases = {"own": biases, "other": swap(biases, 1, "mp")}
+    gains, shifts = norm_gain[0], norm_shift[0]
+    saved = {"own": (), "other": ()}
+    qkv_w = {("own", part): (qkv_weight,) for part in range(parts)}
+    up_w, down_w, out_w = {"own": (up_weight,)}, {"own": (down_weight,)}, {"own": (out_weight,)}
+    units = {}
+
+    def run_heads(side, part):
+        values = biases[side] if side == "own" else clock.hold(biases[side])
+        span = slice(part * GROUP, (part + 1) * GROUP)
+        bias = jnp.concatenate(
+            [values[:width][span], jnp.zeros((GROUP,), F32), values[width : 2 * width][span]]
+        )
+        if side == "other":
+            qkv_w[side, part] = fetch["ab"[part]].parts
+        saved[side] = heads_forward(
+            quarter_order[side],
+            qkv_w[side, part],
+            clock.hold(inputs),
+            bias[None],
+            part,
+            parts,
+            saved[side],
+        )
+        clock.tick(saved[side][1])
+
+    def run_units(side):
+        bias = up_bias if side == "own" else clock.hold(biases[side])[None, 2 * width :]
+        units[side] = units_forward(
+            half_order[side], clock.hold(hidden_low), up_w[side], bias, down_w[side]
+        )
+        clock.tick(units[side][2])
+
+    for action in FORWARD:
+        if action == "project":
+            out_w["other"] = fetch["out"].parts
+            pre_first, hidden, hidden_low = project(
+                quarter_word,
+                (saved["own"][1], saved["other"][1]),
+                out_weight,
+                out_w["other"],
+                clock.hold(inputs),
+                out_bias,
+                gains[0:1],
+                shifts[0:1],
+            )
+            clock.tick(hidden_low)
+        elif action == "units":
+            run_units("own")
+        elif isinstance(action, tuple):
+            run_heads(*action)
+        else:
+            fetch[action].step()
+    up_w["other"], down_w["other"] = fetch["up"].parts, fetch["down"].parts
+    run_units("other")
+    layer_out, grad_second, second_low, gain_two, shift_two, down_sum = turn(
+        (units["own"][2], units["other"][2]),
+        hidden,
+        cotangent,
+        down_bias,
+        gains[1:2],
+        shifts[1:2],
+    )
+    clock.tick(second_low)
+    keep, received, totals, up_sums, head_sums = {}, {}, [], {}, {}
+    state = {}
+
+    def run_units_back(part):
+        kept, sent, total, up_sums[part] = units_back(
+            core_word,
+            core_word,
+            clock.hold(second_low),
+            hidden_low,
+            units,
+            up_w,
+            down_w,
+            part,
+            2,
+        )
+        keep["m", part], received["m", part] = kept, swap(sent, 1)
+        totals.append(total)
+        clock.tick(total)
+
+    def run_first_back():
+        state["first"] = first_back(totals, clock.hold(grad_second), pre_first, gains[0:1])
+        state["grad_x"] = state["first"][0]
+        clock.tick(state["first"][1])
+
+    def run_heads_back(part):
+        kept, sent, grad_x, head_sums[part] = heads_back(
+            core_word,
+            quarter_word,
+            saved,
+            part,
+            inputs,
+            clock.hold(state["first"][1]),
+            {side: qkv_w[side, part] for side in ("own", "other")},
+            out_w,
+            state["grad_x"],
+        )
+        keep["h", part], received["h", part] = kept, swap(sent, 1)
+        state["grad_x"] = grad_x
+        clock.tick(grad_x)
+
+    pieces = {}
+    outcome = {}
+
+    def run_piece(kind, number):
+        key = (kind, number)
+        if key not in pieces:
+            orders = MLP_ORDERS if kind == "m" else HEAD_ORDERS
+
+            def source(side):
+                return [(keep[key], side), (received[key], side)]
+
+            pieces[key] = Piece(clock, words, orders[number], source, 4)
+        pieces[key].step()
+        both = [pieces.get((kind, other)) for other in range(2)]
+        if kind not in outcome and all(piece and piece.complete for piece in both):
+            ends = [array for piece in both for array in (piece.total, piece.flight[0])]
+            ends[0] = clock.hold(ends[0])
+            outcome[kind] = finish_units(core_word, ends) if kind == "m" else finish_heads(core_word, ends)
+            clock.tick(outcome[kind][0])
+
+    for action in BACKWARD:
+        name, *rest = action
+        if name == "ub":
+            run_units_back(*rest)
+        elif name == "fb":
+            run_first_back()
+        elif name == "hb":
+            run_heads_back(*rest)
+        else:
+            run_piece(*action)
+    for kind in "mh":
+        while kind not in outcome:
+            for number in range(2):
+                if not pieces[kind, number].complete:
+                    run_piece(kind, number)
+    grad_x = state["grad_x"]
+    gain_one, shift_one, out_sum = state["first"][2:]
+    grad_down, grad_up = outcome["m"]
+    grad_qkv, grad_out_w = outcome["h"]
+
+    def small_of(side):
+        sums = [head_sums[part][side, 0] for part in range(parts)]
+        entries = [entry[:GROUP] for entry in sums] + [entry[2 * GROUP :] for entry in sums]
+        for part in range(2):
+            steps = up_sums[part].shape[0] // 2
+            entries.append(up_sums[part][side * steps : (side + 1) * steps].reshape(-1))
+        return jnp.concatenate(entries)
+
+    shared_small = jnp.concatenate(
+        [entry[0] for entry in (out_sum, gain_one, gain_two, shift_one, shift_two, down_sum)]
+    )
+    own_small, other_small = small_of(0), small_of(1)
+    split_width = own_small.shape[0]
+    every = lax.all_gather(
+        jnp.concatenate([own_small, other_small, shared_small]), ("dp", "mp"), axis=0
+    ).reshape(lax.axis_size("dp"), 2, -1)
+    same = jnp.sum(every, axis=0)
+    column = lax.axis_index("mp")
+    straight = same[0, :split_width] + same[1, split_width : 2 * split_width]
+    turned = same[1, :split_width] + same[0, split_width : 2 * split_width]
+    split_sum = jnp.where(column == 0, straight, turned)
+    grad_qv_bias = split_sum[: 2 * width].reshape(1, 2, width)
+    grad_up_bias = split_sum[2 * width :].reshape(1, -1)
+    small = same[0] + same[1]
+    split_width = 2 * split_width
+    shared = small[split_width:].reshape(6, -1)
+    return (
+        layer_out,
+        grad_x,
+        grad_qkv[None],
+        grad_qv_bias,
+        grad_out_w[None],
+        shared[0:1],
+        shared[1:3][None],
+        shared[3:5][None],
+        grad_up[None],
+        grad_up_bias,
+        grad_down[None],
+        shared[5:6],
+    )
+
+
+def body(inputs, *others):
+    rows = inputs.shape[0]
+    shared = lax.axis_size("mp") == 2 and lax.axis_size("dp") == 16
+    if rows % PAGE == 0 and shared:
+        return whole_page_body(inputs, *others)
+    return spread_body(inputs, *others)
+
+
 def solution(mesh):
     placed = (
         P(("dp", "mp"), None),

time: 1580 us -> 550 us (0.35)
  waiting for transfers between devices: 895 us -> 121 us
  matrix products: 320 us -> 0 us
  Pallas kernels: 0 us -> 317 us
  local copies, waits for them, and re-layouts: 155 us -> 28.7 us
  blocking collectives: 106 us -> 0 us
  other arithmetic: 80.2 us -> 2.49 us
  starting transfers between devices: 0.49 us -> 55.4 us
    reduce_scatter x6 -> x0, waiting for transfers between devices: 400 us -> none  [the longest x4 239 us: sum_rows(): lax.psum_scatter(term(jnp.int32(0), lax.axis_size('mp') * shard_rows), 'm...]
    psum x1 -> x0, waiting for transfers between devices: 324 us -> none  [body(): lax.psum((qkv_part, bias_part, out_part, up_part, upb_part, down_part), '...]
    pallas_call x0 -> x53, Pallas kernels: none -> 317 us  [the longest x47 278 us: run(): pl.pallas_call(kernel, grid=grid, in_specs=in_specs, out_specs=out_specs,...]
    dot_general x47 -> x0, matrix products: 307 us -> none  [the longest x2 78 us: project_up(): return (jnp.dot(portion, up_w, preferred_element_type=jnp.float32), portion)]
    all_gather x5 -> x1, waiting for transfers between devices: 169 us -> 35.7 us  [whole_page_body(): lax.all_gather(jnp.concatenate([own_small, other_small, shared_small]), (...]
    psum x2 -> x0, blocking collectives: 106 us -> none  [the longest x1 63.5 us: body(): lax.psum((qkv_part, bias_part, out_part, up_part, upb_part, down_part), '...]
    ppermute x0 -> x61, waiting for transfers between devices: none -> 85.7 us  [swap(): lax.ppermute(value, axis, [(place, place ^ distance) for place in range(c...]
    ppermute x0 -> x61, starting transfers between devices: none -> 55.3 us  [swap(): lax.ppermute(value, axis, [(place, place ^ distance) for place in range(c...]
  transfers between devices with their start and end apart: 12 -> 62, of which waited for: 11 -> 21; matrix products, arithmetic and copies ran while one was open for 12% -> 3% of each run, Pallas kernels for 0% -> 47%
where the time goes in v2:
time: 550 us; the launch traced here: 540 us
  Pallas kernels  317 us (58%)
  waiting for transfers between devices  121 us (22%)
  starting transfers between devices  55.4 us (10%)
  local copies, waits for them, and re-layouts  28.7 us (5%)
  between operations  14.9 us (3%)
    pallas_call x47, Pallas kernels, run(): pl.pallas_call(kernel, grid=grid, in_specs=in_specs, out_specs=out_specs,...  278 us
    ppermute x61, waiting for transfers between devices, swap(): lax.ppermute(value, axis, [(place, place ^ distance) for place in range(c...  85.7 us
    ppermute x61, starting transfers between devices, swap(): lax.ppermute(value, axis, [(place, place ^ distance) for place in range(c...  55.3 us
    all_gather x1, waiting for transfers between devices, whole_page_body(): lax.all_gather(jnp.concatenate([own_small, other_small, shared_small]), (...  35.7 us
    pallas_call x4, Pallas kernels, heads_forward(): pl.pallas_call(heads_kernel, grid=(pages,), in_specs=[scalar_spec()] + qk...  32.8 us
    unnamed x118, local copies, waits for them, and re-layouts  15.2 us
  transfers between devices with their start and end apart: 62, of which 21 were waited for; matrix products, arithmetic and copies ran while one was open for 3% of the time, Pallas kernels for 47%

profile of v2, /device:TPU:0, one launch (start us, length us, event | category | flops | bytes accessed | tf_op | source)
XLA Modules:
  0.0 539.8 jit_solution(758224607928638375)
XLA Ops:
  7.8 2.7 take_blocks.2
  10.5 2.9 collective-permute-start
  13.5 3.0 take_blocks.3
  19.8 8.2 %heads.4 = (bf16[832,1536]{1,0:T(8,128)(2,1)}, bf16[832,512]{1,0:T(8,128)(2,1)}, f32[2,2,4,416]{3,2,1,0:T(4,128)}) custom-call(s32[1]{0:T(128)} %constant.8.clone.1.order_ref, bf16[1,3,1024,512]{3,2,1,0:T(8,128)(2,1)} %refs_6_.3, bf16[1,3,1024,512]{3,2,1,0:T(8,128)(2,1)} %refs_6_.3, bf16[1,3,1024,512]{3,2,1,0:T(8,128)(2,1)} %refs_6_.3, ...), custom_call_target="tpu_custom_call" | custom-call | flops 263999995904 | bytes 1 | tf_op jit(solution)/shard_map/heads/pallas_call | solution.py:436
  31.2 8.2 %heads.5 = (bf16[832,1536]{1,0:T(8,128)(2,1)}, bf16[832,512]{1,0:T(8,128)(2,1)}, f32[2,2,4,416]{3,2,1,0:T(4,128)}) custom-call(s32[1]{0:T(128)} %constant.8.clone.1.order_ref, bf16[1,3,1024,512]{3,2,1,0:T(8,128)(2,1)} %refs_6_.3, bf16[1,3,1024,512]{3,2,1,0:T(8,128)(2,1)} %refs_6_.3, ...), custom_call_target="tpu_custom_call", output_to_operand_aliasing={{0}: (7, {}), {1}: (8, {}), {2}: (9, {})} | custom-call | flops 263999995904 | bytes 1 | tf_op jit(solution)/shard_map/heads/pallas_call | solution.py:436
  42.1 6.9 %collective-permute-done.6.piece_ref = bf16[1,128,2048]{2,1,0:T(8,128)(2,1)} collective-permute-done((bf16[1,128,2048]{2,1,0:T(8,128)(2,1)}, bf16[1,128,2048]{2,1,0:T(8,128)(2,1)}, u32[]{:S(2)}, u32[]{:S(2)}) %collective-permute-start.6) | collective-permute-done | bytes 524320 | tf_op jit(solution)/shard_map/ppermute | solution.py:860
  52.7 8.2 %heads.6 = (bf16[832,1536]{1,0:T(8,128)(2,1)}, bf16[832,512]{1,0:T(8,128)(2,1)}, f32[2,2,4,416]{3,2,1,0:T(4,128)}) custom-call(s32[1]{0:T(128)} %bitcast.order_ref, bf16[1,3,256,256]{3,2,1,0:T(8,128)(2,1)} %collective-permute-done.w0_ref.refs_14_, bf16[1,3,256,256]{3,2,1,0:T(8,128)(2,1)} %collective-permute-done.3.w1_ref.refs_15_, ...), custom_call_target="tpu_custom_call" | custom-call | flops 263999995904 | bytes 1 | tf_op jit(solution)/shard_map/heads/pallas_call | solution.py:436
  69.3 8.2 %heads.7 = (bf16[832,1536]{1,0:T(8,128)(2,1)}, bf16[832,512]{1,0:T(8,128)(2,1)}, f32[2,2,4,416]{3,2,1,0:T(4,128)}) custom-call(s32[1]{0:T(128)} %bitcast.order_ref, bf16[1,3,256,256]{3,2,1,0:T(8,128)(2,1)} %collective-permute-done.1.w0_ref.refs_14_, ...), custom_call_target="tpu_custom_call", output_to_operand_aliasing={{0}: (7, {}), {1}: (8, {}), {2}: (9, {})} | custom-call | flops 263999995904 | bytes 1 | tf_op jit(solution)/shard_map/heads/pallas_call | solution.py:436
  82.7 7.8 %project.1 = (f32[832,1024]{1,0:T(8,128)}, f32[832,1024]{1,0:T(8,128)}, bf16[832,1024]{1,0:T(8,128)(2,1)}) custom-call(s32[1]{0:T(128)} %bitcast.order_ref, bf16[832,512]{1,0:T(8,128)(2,1)} %get-tuple-element.181.a_ref.refs_2_, bf16[832,512]{1,0:T(8,128)(2,1)} %get-tuple-element.199.b_ref.refs_13_, bf16[1,512,1024]{2,1,0:T(8,128)(2,1)} %refs_10_.3, ...), custom_call_target="tpu_custom_call" | custom-call | flops 230999998464 | bytes 1 | tf_op jit(solution)/shard_map/project/pallas_call | solution.py:351
  98.3 3.0 join_depth.2.up_a.refs_8_
  101.3 20.3 %units.2 = (bf16[832,2048]{1,0:T(8,128)(2,1)}, bf16[832,2048]{1,0:T(8,128)(2,1)}, f32[832,1024]{1,0:T(8,128)}) custom-call(s32[1]{0:T(128)} %constant.8.clone.1.order_ref, bf16[832,1024]{1,0:T(8,128)(2,1)} %get-tuple-element.212.h_ref, bf16[1,1024,2048]{2,1,0:T(8,128)(2,1)} %refs_3_.5, bf16[1,1024,2048]{2,1,0:T(8,128)(2,1)} %refs_3_.5, f32[1,2048]{1,0:T(1,128)} %b_ref.1, ...), custom_call_target="tpu_custom_call" | custom-call | flops 660000014336 | bytes 1 | tf_op jit(solution)/shard_map/units/pallas_call | solution.py:351
  121.6 3.2 join_depth.3.down_a.refs_10_
  126.0 3.4 collective-permute-done.24.down_b.refs_11_
  130.6 20.3 %units.3 = (bf16[832,2048]{1,0:T(8,128)(2,1)}, bf16[832,2048]{1,0:T(8,128)(2,1)}, f32[832,1024]{1,0:T(8,128)}) custom-call(s32[1]{0:T(128)} %bitcast.3.order_ref.core_ref, bf16[832,1024]{1,0:T(8,128)(2,1)} %get-tuple-element.212.h_ref, bf16[1,512,2048]{2,1,0:T(8,128)(2,1)} %join_depth.2.up_a.refs_8_, ...), custom_call_target="tpu_custom_call" | custom-call | flops 660000014336 | bytes 1 | tf_op jit(solution)/shard_map/units/pallas_call | solution.py:351
  151.0 8.7 %turn.1 = (f32[832,1024]{1,0:T(8,128)}, f32[832,1024]{1,0:T(8,128)}, bf16[832,1024]{1,0:T(8,128)(2,1)}, f32[1,1024]{1,0:T(1,128)}, f32[1,1024]{1,0:T(1,128)}, /*index=5*/f32[1,1024]{1,0:T(1,128)}) custom-call(f32[832,1024]{1,0:T(8,128)} %get-tuple-element.210.a_ref, f32[832,1024]{1,0:T(8,128)} %get-tuple-element.214.b_ref, ...), custom_call_target="tpu_custom_call" | custom-call | flops 297000009728 | bytes 1 | tf_op jit(solution)/shard_map/turn/pallas_call | solution.py:351
  159.6 24.7 %units_back.2 = (bf16[8,512,512]{2,1,0:T(8,128)(2,1)}, bf16[8,512,512]{2,1,0:T(8,128)(2,1)}, f32[832,1024]{1,0:T(8,128)}, f32[4,1,512]{2,1,0:T(1,128)}) custom-call(s32[1]{0:T(128)} %bitcast.3.order_ref.core_ref, s32[1]{0:T(128)} %bitcast.3.order_ref.core_ref, bf16[832,1024]{1,0:T(8,128)(2,1)} %get-tuple-element.224.g_ref, ...), custom_call_target="tpu_custom_call" | custom-call | flops 726000009216 | bytes 1 | tf_op jit(solution)/shard_map/units_back/pallas_call | solution.py:351
  184.8 23.9 %units_back.3 = (bf16[8,512,512]{2,1,0:T(8,128)(2,1)}, bf16[8,512,512]{2,1,0:T(8,128)(2,1)}, f32[832,1024]{1,0:T(8,128)}, f32[4,1,512]{2,1,0:T(1,128)}) custom-call(s32[1]{0:T(128)} %bitcast.3.order_ref.core_ref, s32[1]{0:T(128)} %bitcast.3.order_ref.core_ref, bf16[832,1024]{1,0:T(8,128)(2,1)} %get-tuple-element.224.g_ref, ...), custom_call_target="tpu_custom_call" | custom-call | flops 726000009216 | bytes 1 | tf_op jit(solution)/shard_map/units_back/pallas_call | solution.py:351
  210.8 4.1 combine.20
  216.4 8.6 %first_back.1 = (f32[832,1024]{1,0:T(8,128)}, bf16[832,1024]{1,0:T(8,128)(2,1)}, f32[1,1024]{1,0:T(1,128)}, f32[1,1024]{1,0:T(1,128)}, f32[1,1024]{1,0:T(1,128)}) custom-call(f32[832,1024]{1,0:T(8,128)} %get-tuple-element.223.refs_0_, f32[832,1024]{1,0:T(8,128)} %get-tuple-element.225.refs_1_, f32[832,1024]{1,0:T(8,128)} %get-tuple-element.230.refs_2_, ...), custom_call_target="tpu_custom_call" | custom-call | flops 330000007168 | bytes 1 | tf_op jit(solution)/shard_map/first_back/pallas_call | solution.py:351
  225.0 6.4 %combine.21 = (bf16[8,256,512]{2,1,0:T(8,128)(2,1)}, bf16[4,256,512]{2,1,0:T(8,128)(2,1)}, bf16[4,256,512]{2,1,0:T(8,128)(2,1)}) custom-call(s32[4]{0:T(128)} %pad_add_fusion.word_ref, bf16[8,512,512]{2,1,0:T(8,128)(2,1)} %get-tuple-element.234.refs_0_.refs_2_, bf16[8,512,512]{2,1,0:T(8,128)(2,1)} %collective-permute-done.26.refs_1_.refs_3_, ...), custom_call_target="tpu_custom_call" | custom-call | flops 65999998976 | bytes 1 | tf_op jit(solution)/shard_map/combine/pallas_call | solution.py:351
  232.6 27.5 %heads_back.2 = (bf16[8,512,256]{2,1,0:T(8,128)(2,1)}, bf16[8,512,256]{2,1,0:T(8,128)(2,1)}, f32[832,1024]{1,0:T(8,128)}, f32[2,1,768]{2,1,0:T(1,128)}) custom-call(s32[1]{0:T(128)} %bitcast.3.order_ref.core_ref, s32[1]{0:T(128)} %bitcast.order_ref, bf16[832,1024]{1,0:T(8,128)(2,1)} %x_ref.8, bf16[832,1024]{1,0:T(8,128)(2,1)} %get-tuple-element.244.g_ref, ...), custom_call_target="tpu_custom_call" | custom-call | flops 857999998976 | bytes 1 | tf_op jit(solution)/shard_map/heads_back/pallas_call | solution.py:351
  262.9 28.0 %heads_back.3 = (bf16[8,512,256]{2,1,0:T(8,128)(2,1)}, bf16[8,512,256]{2,1,0:T(8,128)(2,1)}, f32[832,1024]{1,0:T(8,128)}, f32[2,1,768]{2,1,0:T(1,128)}) custom-call(s32[1]{0:T(128)} %bitcast.3.order_ref.core_ref, s32[1]{0:T(128)} %bitcast.order_ref, bf16[832,1024]{1,0:T(8,128)(2,1)} %x_ref.8, bf16[832,1024]{1,0:T(8,128)(2,1)} %get-tuple-element.244.g_ref, ...), custom_call_target="tpu_custom_call" | custom-call | flops 857999998976 | bytes 1 | tf_op jit(solution)/shard_map/heads_back/pallas_call | solution.py:351
  293.1 4.9 combine.22
  298.9 3.8 combine.23
  304.0 3.9 combine.24
  309.1 4.0 combine.25
  314.5 35.7 %all-gather.3.cloned.1.call-done = f32[393216]{0:T(1024)} async-done(((f32[12288]{0:T(1024)}), f32[393216]{0:T(1024)}) %all-gather.3.cloned.1.call-update) | async-done | bytes 1572880 | tf_op jit(solution)/shard_map/all_gather | solution.py:1487
  353.7 2.7 combine.26
  356.9 2.7 combine.27
  361.1 10.2 %collective-permute-done.33.refs_1_ = bf16[4,128,512]{2,1,0:T(8,128)(2,1)S(1)} collective-permute-done((bf16[4,128,512]{2,1,0:T(8,128)(2,1)}, bf16[4,128,512]{2,1,0:T(8,128)(2,1)S(1)}, u32[]{:S(2)}, u32[]{:S(2)}) %collective-permute-start.33) | collective-permute-done | bytes 524320 | tf_op jit(solution)/shard_map/ppermute | solution.py:860
  375.0 2.6 combine.29
  377.6 9.9 %collective-permute-done.35.refs_1_ = bf16[4,128,512]{2,1,0:T(8,128)(2,1)S(1)} collective-permute-done((bf16[4,128,512]{2,1,0:T(8,128)(2,1)}, bf16[4,128,512]{2,1,0:T(8,128)(2,1)S(1)}, u32[]{:S(2)}, u32[]{:S(2)}) %collective-permute-start.35) | collective-permute-done | bytes 524320 | tf_op jit(solution)/shard_map/ppermute | solution.py:860
  394.5 2.9 collective-permute-start.40
  397.3 2.6 combine.32
  400.5 4.8 collective-permute-done.38.refs_1_
  412.9 3.3 collective-permute-done.40.refs_1_
  422.2 2.4 collective-permute-done.42.refs_1_
  430.8 9.9 %collective-permute-done.44.refs_1_ = bf16[4,128,512]{2,1,0:T(8,128)(2,1)} collective-permute-done((bf16[4,128,512]{2,1,0:T(8,128)(2,1)}, bf16[4,128,512]{2,1,0:T(8,128)(2,1)}, u32[]{:S(2)}, u32[]{:S(2)}) %collective-permute-start.44) | collective-permute-done | bytes 524320 | tf_op jit(solution)/shard_map/ppermute | solution.py:860
  449.9 2.8 collective-permute-start.50
  452.7 6.8 %collective-permute-done.47.refs_1_ = bf16[4,128,512]{2,1,0:T(8,128)(2,1)} collective-permute-done((bf16[4,128,512]{2,1,0:T(8,128)(2,1)}, bf16[4,128,512]{2,1,0:T(8,128)(2,1)}, u32[]{:S(2)}, u32[]{:S(2)}) %collective-permute-start.47) | collective-permute-done | bytes 524320 | tf_op jit(solution)/shard_map/ppermute | solution.py:860
  465.4 3.9 collective-permute-done.49.refs_1_
  469.3 3.0 join_rows.16.refs_0_
  478.4 4.9 collective-permute-done.53.refs_1_
  486.0 4.8 collective-permute-done.54.refs_1_
  490.7 3.1 join_rows.20.refs_2_
  499.8 9.8 %finish.2 = (f32[2048,1024]{1,0:T(8,128)}, f32[1024,2048]{1,0:T(8,128)}) custom-call(s32[1]{0:T(128)} %bitcast.3.order_ref.core_ref, bf16[4,512,512]{2,1,0:T(8,128)(2,1)} %join_rows.16.refs_0_, bf16[4,512,512]{2,1,0:T(8,128)(2,1)} %copy-done.32, bf16[4,512,512]{2,1,0:T(8,128)(2,1)} %join_rows.20.refs_2_, bf16[4,512,512]{2,1,0:T(8,128)(2,1)} %copy-done.35), custom_call_target="tpu_custom_call" | custom-call | flops 198000001024 | bytes 1 | tf_op jit(solution)/shard_map/finish/pallas_call | solution.py:351
  511.9 7.8 %collective-permute-done.58.refs_1_ = bf16[4,256,256]{2,1,0:T(8,128)(2,1)} collective-permute-done((bf16[4,256,256]{2,1,0:T(8,128)(2,1)}, bf16[4,256,256]{2,1,0:T(8,128)(2,1)}, u32[]{:S(2)}, u32[]{:S(2)}) %collective-permute-start.58) | collective-permute-done | bytes 524320 | tf_op jit(solution)/shard_map/ppermute | solution.py:860
  527.0 5.8 %finish.3 = (f32[3,1024,512]{2,1,0:T(8,128)}, f32[512,1024]{1,0:T(8,128)}) custom-call(s32[1]{0:T(128)} %bitcast.3.order_ref.core_ref, bf16[4,512,256]{2,1,0:T(8,128)(2,1)} %join_rows.22.refs_0_, bf16[4,512,256]{2,1,0:T(8,128)(2,1)} %copy-done.37, bf16[4,512,256]{2,1,0:T(8,128)(2,1)} %join_rows.23.refs_2_, bf16[4,512,256]{2,1,0:T(8,128)(2,1)} %copy-done.38), custom_call_target="tpu_custom_call" | custom-call | flops 198000001024 | bytes 1 | tf_op jit(solution)/shard_map/finish/pallas_call | solution.py:351
  (280 shorter events, 127.8 us)
Async XLA Ops:
  7.2 343.0 %all-gather.3.cloned.1.call-start = ((), (), s32[]{:S(2)}) async-start(), calls=%async_computation | async-start | bytes 1622016 | tf_op jit(solution)/shard_map/all_gather | solution.py:1487
  10.5 18.7 %collective-permute-start = (bf16[1,3,256,256]{3,2,1,0:T(8,128)(2,1)}, bf16[1,3,256,256]{3,2,1,0:T(8,128)(2,1)}, u32[]{:S(2)}, u32[]{:S(2)}) collective-permute-start(bf16[1,3,256,256]{3,2,1,0:T(8,128)(2,1)} %get-tuple-element.172), channel_id=1, source_target_pairs={{0,1},{1,0},{2,3},{3,2},{4,5},{5,4},{6,7},{7,6},{8,9},{9,8},{10,11... | collective-permute-start | bytes 1179656 | tf_op jit(solution)/shard_map/ppermute | solution.py:860
  13.5 26.0 %collective-permute-start.1 = (bf16[1,3,256,256]{3,2,1,0:T(8,128)(2,1)}, bf16[1,3,256,256]{3,2,1,0:T(8,128)(2,1)}, u32[]{:S(2)}, u32[]{:S(2)}) collective-permute-start(bf16[1,3,256,256]{3,2,1,0:T(8,128)(2,1)} %get-tuple-element.182), channel_id=1, source_target_pairs={{0,1},{1,0},{2,3},{3,2},{4,5},{5,4},{6,7},{7,6},{8,9},{9,8},{10,11... | collective-permute-start | bytes 1179656 | tf_op jit(solution)/shard_map/ppermute | solution.py:860
  16.5 25.1 %collective-permute-start.7 = (bf16[1,512,256]{2,1,0:T(8,128)(2,1)}, bf16[1,512,256]{2,1,0:T(8,128)(2,1)}, u32[]{:S(2)}, u32[]{:S(2)}) collective-permute-start(bf16[1,512,256]{2,1,0:T(8,128)(2,1)} %get-tuple-element.174), channel_id=1, source_target_pairs={{0,1},{1,0},{2,3},{3,2},{4,5},{5,4},{6,7},{7,6},{8,9},{9,8},{10,11... | collective-permute-start | bytes 786440 | tf_op jit(solution)/shard_map/ppermute | solution.py:860
  18.5 30.5 %collective-permute-start.6 = (bf16[1,128,2048]{2,1,0:T(8,128)(2,1)}, bf16[1,128,2048]{2,1,0:T(8,128)(2,1)}, u32[]{:S(2)}, u32[]{:S(2)}) collective-permute-start(bf16[1,128,2048]{2,1,0:T(8,128)(2,1)} %get-tuple-element.185), channel_id=1, source_target_pairs={{0,1},{1,0},{2,3},{3,2},{4,5},{5,4},{6,7},{7,6},{8,9},{9,8},{10,11... | collective-permute-start | bytes 1572872 | tf_op jit(solution)/shard_map/ppermute | solution.py:860
  31.2 20.5 %collective-permute-start.4 = (bf16[1,3,256,256]{3,2,1,0:T(8,128)(2,1)}, bf16[1,3,256,256]{3,2,1,0:T(8,128)(2,1)}, u32[]{:S(2)}, u32[]{:S(2)}) collective-permute-start(bf16[1,3,256,256]{3,2,1,0:T(8,128)(2,1)} %collective-permute-done.w0_ref.refs_14_), channel_id=1, source_target_pairs={{0,2},{2,0},{4,6},{6,4},{8,10},{10,8},{12,14},{14,12},{16,18},{18,... | collective-permute-start | bytes 1179656 | tf_op jit(solution)/shard_map/ppermute | solution.py:860
  41.6 24.3 %collective-permute-start.11 = (bf16[1,2048,128]{2,1,0:T(8,128)(2,1)}, bf16[1,2048,128]{2,1,0:T(8,128)(2,1)}, u32[]{:S(2)}, u32[]{:S(2)}) collective-permute-start(bf16[1,2048,128]{2,1,0:T(8,128)(2,1)} %get-tuple-element.192), channel_id=1, source_target_pairs={{0,1},{1,0},{2,3},{3,2},{4,5},{5,4},{6,7},{7,6},{8,9},{9,8},{10,11... | collective-permute-start | bytes 1572872 | tf_op jit(solution)/shard_map/ppermute | solution.py:860
  51.1 16.2 %collective-permute-start.9 = (bf16[1,3,256,256]{3,2,1,0:T(8,128)(2,1)}, bf16[1,3,256,256]{3,2,1,0:T(8,128)(2,1)}, u32[]{:S(2)}, u32[]{:S(2)}) collective-permute-start(bf16[1,3,256,256]{3,2,1,0:T(8,128)(2,1)} %collective-permute-done.1.w0_ref.refs_14_), channel_id=1, source_target_pairs={{0,2},{2,0},{4,6},{6,4},{8,10},{10,8},{12,14},{14,12},{16,18},{18,... | collective-permute-start | bytes 1179656 | tf_op jit(solution)/shard_map/ppermute | solution.py:860
  62.1 15.4 %collective-permute-start.15 = (bf16[1,128,2048]{2,1,0:T(8,128)(2,1)}, bf16[1,128,2048]{2,1,0:T(8,128)(2,1)}, u32[]{:S(2)}, u32[]{:S(2)}) collective-permute-start(bf16[1,128,2048]{2,1,0:T(8,128)(2,1)} %collective-permute-done.6.piece_ref), channel_id=1, source_target_pairs={{0,4},{2,6},{4,0},{6,2},{8,12},{10,14},{12,8},{14,10},{16,20},{18,... | collective-permute-start | bytes 1572872 | tf_op jit(solution)/shard_map/ppermute | solution.py:860
  64.4 14.4 %collective-permute-start.16 = (bf16[1,128,2048]{2,1,0:T(8,128)(2,1)}, bf16[1,128,2048]{2,1,0:T(8,128)(2,1)}, u32[]{:S(2)}, u32[]{:S(2)}) collective-permute-start(bf16[1,128,2048]{2,1,0:T(8,128)(2,1)} %collective-permute-done.6.piece_ref), channel_id=1, source_target_pairs={{0,8},{2,10},{4,12},{6,14},{8,0},{10,2},{12,4},{14,6},{16,24},{18,... | collective-permute-start | bytes 1572872 | tf_op jit(solution)/shard_map/ppermute | solution.py:860
  65.9 15.7 %collective-permute-start.13 = (bf16[1,512,256]{2,1,0:T(8,128)(2,1)}, bf16[1,512,256]{2,1,0:T(8,128)(2,1)}, u32[]{:S(2)}, u32[]{:S(2)}) collective-permute-start(bf16[1,512,256]{2,1,0:T(8,128)(2,1)} %collective-permute-done.7.w0.refs_18_), channel_id=1, source_target_pairs={{0,2},{2,0},{4,6},{6,4},{8,10},{10,8},{12,14},{14,12},{16,18},{18,... | collective-permute-start | bytes 786440 | tf_op jit(solution)/shard_map/ppermute | solution.py:860
  67.3 15.5 %collective-permute-start.14 = (bf16[1,512,256]{2,1,0:T(8,128)(2,1)}, bf16[1,512,256]{2,1,0:T(8,128)(2,1)}, u32[]{:S(2)}, u32[]{:S(2)}) collective-permute-start(bf16[1,512,256]{2,1,0:T(8,128)(2,1)} %collective-permute-done.12.w1.refs_19_), channel_id=1, source_target_pairs={{0,2},{2,0},{4,6},{6,4},{8,10},{10,8},{12,14},{14,12},{16,18},{18,... | collective-permute-start | bytes 786440 | tf_op jit(solution)/shard_map/ppermute | solution.py:860
  67.8 22.8 %collective-permute-start.17 = (bf16[1,2048,128]{2,1,0:T(8,128)(2,1)}, bf16[1,2048,128]{2,1,0:T(8,128)(2,1)}, u32[]{:S(2)}, u32[]{:S(2)}) collective-permute-start(bf16[1,2048,128]{2,1,0:T(8,128)(2,1)} %collective-permute-done.11.piece_ref), channel_id=1, source_target_pairs={{0,4},{2,6},{4,0},{6,2},{8,12},{10,14},{12,8},{14,10},{16,20},{18,... | collective-permute-start | bytes 1572872 | tf_op jit(solution)/shard_map/ppermute | solution.py:860
  77.5 15.2 %collective-permute-start.18 = (bf16[1,2048,128]{2,1,0:T(8,128)(2,1)}, bf16[1,2048,128]{2,1,0:T(8,128)(2,1)}, u32[]{:S(2)}, u32[]{:S(2)}) collective-permute-start(bf16[1,2048,128]{2,1,0:T(8,128)(2,1)} %collective-permute-done.11.piece_ref), channel_id=1, source_target_pairs={{0,8},{2,10},{4,12},{6,14},{8,0},{10,2},{12,4},{14,6},{16,24},{18,... | collective-permute-start | bytes 1572872 | tf_op jit(solution)/shard_map/ppermute | solution.py:860
  80.8 17.5 %collective-permute-start.19 = (bf16[1,128,1024]{2,1,0:T(8,128)(2,1)}, bf16[1,128,1024]{2,1,0:T(8,128)(2,1)}, u32[]{:S(2)}, u32[]{:S(2)}) collective-permute-start(bf16[1,128,1024]{2,1,0:T(8,128)(2,1)} %get-tuple-element.201), channel_id=1, source_target_pairs={{0,8},{2,10},{4,12},{6,14},{8,0},{10,2},{12,4},{14,6},{16,24},{18,... | collective-permute-start | bytes 786440 | tf_op jit(solution)/shard_map/ppermute | solution.py:860
  81.6 16.6 %collective-permute-start.20 = (bf16[1,128,1024]{2,1,0:T(8,128)(2,1)}, bf16[1,128,1024]{2,1,0:T(8,128)(2,1)}, u32[]{:S(2)}, u32[]{:S(2)}) collective-permute-start(bf16[1,128,1024]{2,1,0:T(8,128)(2,1)} %get-tuple-element.202), channel_id=1, source_target_pairs={{0,4},{2,6},{4,0},{6,2},{8,12},{10,14},{12,8},{14,10},{16,20},{18,... | collective-permute-start | bytes 786440 | tf_op jit(solution)/shard_map/ppermute | solution.py:860
  94.7 26.9 %collective-permute-start.21 = (bf16[1,1024,128]{2,1,0:T(8,128)(2,1)}, bf16[1,1024,128]{2,1,0:T(8,128)(2,1)}, u32[]{:S(2)}, u32[]{:S(2)}) collective-permute-start(bf16[1,1024,128]{2,1,0:T(8,128)(2,1)} %get-tuple-element.206), channel_id=1, source_target_pairs={{0,8},{2,10},{4,12},{6,14},{8,0},{10,2},{12,4},{14,6},{16,24},{18,... | collective-permute-start | bytes 786440 | tf_op jit(solution)/shard_map/ppermute | solution.py:860
  95.9 25.7 %collective-permute-start.22 = (bf16[1,1024,128]{2,1,0:T(8,128)(2,1)}, bf16[1,1024,128]{2,1,0:T(8,128)(2,1)}, u32[]{:S(2)}, u32[]{:S(2)}) collective-permute-start(bf16[1,1024,128]{2,1,0:T(8,128)(2,1)} %get-tuple-element.207), channel_id=1, source_target_pairs={{0,4},{2,6},{4,0},{6,2},{8,12},{10,14},{12,8},{14,10},{16,20},{18,... | collective-permute-start | bytes 786440 | tf_op jit(solution)/shard_map/ppermute | solution.py:860
  101.2 24.7 %collective-permute-start.23 = (bf16[1,512,2048]{2,1,0:T(8,128)(2,1)}, bf16[1,512,2048]{2,1,0:T(8,128)(2,1)}, u32[]{:S(2)}, u32[]{:S(2)}) collective-permute-start(bf16[1,512,2048]{2,1,0:T(8,128)(2,1)} %join_depth.2.up_a.refs_8_), channel_id=1, source_target_pairs={{0,2},{2,0},{4,6},{6,4},{8,10},{10,8},{12,14},{14,12},{16,18},{18,... | collective-permute-start | bytes 6291464 | tf_op jit(solution)/shard_map/ppermute | solution.py:860
  184.4 26.5 %collective-permute-start.25 = (bf16[8,512,512]{2,1,0:T(8,128)(2,1)}, bf16[8,512,512]{2,1,0:T(8,128)(2,1)}, u32[]{:S(2)}, u32[]{:S(2)}) collective-permute-start(bf16[8,512,512]{2,1,0:T(8,128)(2,1)} %get-tuple-element.229), channel_id=1, source_target_pairs={{0,2},{2,0},{4,6},{6,4},{8,10},{10,8},{12,14},{14,12},{16,18},{18,... | collective-permute-start | bytes 12582920 | tf_op jit(solution)/shard_map/ppermute | solution.py:860
  208.7 16.3 %collective-permute-start.26 = (bf16[8,512,512]{2,1,0:T(8,128)(2,1)}, bf16[8,512,512]{2,1,0:T(8,128)(2,1)}, u32[]{:S(2)}, u32[]{:S(2)}) collective-permute-start(bf16[8,512,512]{2,1,0:T(8,128)(2,1)} %get-tuple-element.235), channel_id=1, source_target_pairs={{0,2},{2,0},{4,6},{6,4},{8,10},{10,8},{12,14},{14,12},{16,18},{18,... | collective-permute-start | bytes 12582920 | tf_op jit(solution)/shard_map/ppermute | solution.py:860
  214.9 78.2 %collective-permute-start.27 = (bf16[4,512,512]{2,1,0:T(8,128)(2,1)}, bf16[4,512,512]{2,1,0:T(8,128)(2,1)}, u32[]{:S(2)}, u32[]{:S(2)}) collective-permute-start(bf16[4,512,512]{2,1,0:T(8,128)(2,1)} %combine.20), channel_id=1, source_target_pairs={{0,1},{1,0},{2,3},{3,2},{4,5},{5,4},{6,7},{7,6},{8,9},{9,8},{10,11... | collective-permute-start | bytes 6291464 | tf_op jit(solution)/shard_map/ppermute | solution.py:860
  231.4 67.5 %collective-permute-start.28 = (bf16[8,256,512]{2,1,0:T(8,128)(2,1)}, bf16[8,256,512]{2,1,0:T(8,128)(2,1)}, u32[]{:S(2)}, u32[]{:S(2)}) collective-permute-start(bf16[8,256,512]{2,1,0:T(8,128)(2,1)} %get-tuple-element.236), channel_id=1, source_target_pairs={{0,4},{2,6},{4,0},{6,2},{8,12},{10,14},{12,8},{14,10},{16,20},{18,... | collective-permute-start | bytes 6291464 | tf_op jit(solution)/shard_map/ppermute | solution.py:860
  292.6 16.5 %collective-permute-start.30 = (bf16[8,512,256]{2,1,0:T(8,128)(2,1)}, bf16[8,512,256]{2,1,0:T(8,128)(2,1)}, u32[]{:S(2)}, u32[]{:S(2)}) collective-permute-start(bf16[8,512,256]{2,1,0:T(8,128)(2,1)} %get-tuple-element.260), channel_id=1, source_target_pairs={{0,2},{2,0},{4,6},{6,4},{8,10},{10,8},{12,14},{14,12},{16,18},{18,... | collective-permute-start | bytes 6291464 | tf_op jit(solution)/shard_map/ppermute | solution.py:860
  298.1 55.6 %collective-permute-start.31 = (bf16[4,256,512]{2,1,0:T(8,128)(2,1)}, bf16[4,256,512]{2,1,0:T(8,128)(2,1)}, u32[]{:S(2)}, u32[]{:S(2)}) collective-permute-start(bf16[4,256,512]{2,1,0:T(8,128)(2,1)} %get-tuple-element.249), channel_id=1, source_target_pairs={{0,4},{2,6},{4,0},{6,2},{8,12},{10,14},{12,8},{14,10},{16,20},{18,... | collective-permute-start | bytes 3145736 | tf_op jit(solution)/shard_map/ppermute | solution.py:860
  307.9 67.1 %collective-permute-start.34 = (bf16[8,256,256]{2,1,0:T(8,128)(2,1)}, bf16[8,256,256]{2,1,0:T(8,128)(2,1)}, u32[]{:S(2)}, u32[]{:S(2)}) collective-permute-start(bf16[8,256,256]{2,1,0:T(8,128)(2,1)} %get-tuple-element.258), channel_id=1, source_target_pairs={{0,4},{2,6},{4,0},{6,2},{8,12},{10,14},{12,8},{14,10},{16,20},{18,... | collective-permute-start | bytes 3145736 | tf_op jit(solution)/shard_map/ppermute | solution.py:860
  313.1 84.2 %collective-permute-start.37 = (bf16[8,256,256]{2,1,0:T(8,128)(2,1)}, bf16[8,256,256]{2,1,0:T(8,128)(2,1)}, u32[]{:S(2)}, u32[]{:S(2)}) collective-permute-start(bf16[8,256,256]{2,1,0:T(8,128)(2,1)} %get-tuple-element.261), channel_id=1, source_target_pairs={{0,4},{2,6},{4,0},{6,2},{8,12},{10,14},{12,8},{14,10},{16,20},{18,... | collective-permute-start | bytes 3145736 | tf_op jit(solution)/shard_map/ppermute | solution.py:860
  314.0 42.9 %collective-permute-start.32 = (bf16[4,256,512]{2,1,0:T(8,128)(2,1)S(1)}, bf16[4,256,512]{2,1,0:T(8,128)(2,1)}, u32[]{:S(2)}, u32[]{:S(2)}) collective-permute-start(bf16[4,256,512]{2,1,0:T(8,128)(2,1)S(1)} %copy-done.36), channel_id=1, source_target_pairs={{0,1},{1,0},{2,3},{3,2},{4,5},{5,4},{6,7},{7,6},{8,9},{9,8},{10,11... | collective-permute-start | bytes 3145736 | tf_op jit(solution)/shard_map/ppermute | solution.py:860
  356.4 15.0 %collective-permute-start.33 = (bf16[4,128,512]{2,1,0:T(8,128)(2,1)}, bf16[4,128,512]{2,1,0:T(8,128)(2,1)S(1)}, u32[]{:S(2)}, u32[]{:S(2)}) collective-permute-start(bf16[4,128,512]{2,1,0:T(8,128)(2,1)} %get-tuple-element.264), channel_id=1, source_target_pairs={{0,8},{2,10},{4,12},{6,14},{8,0},{10,2},{12,4},{14,6},{16,24},{18,... | collective-permute-start | bytes 1572872 | tf_op jit(solution)/shard_map/ppermute | solution.py:860
  359.6 27.9 %collective-permute-start.35 = (bf16[4,128,512]{2,1,0:T(8,128)(2,1)}, bf16[4,128,512]{2,1,0:T(8,128)(2,1)S(1)}, u32[]{:S(2)}, u32[]{:S(2)}) collective-permute-start(bf16[4,128,512]{2,1,0:T(8,128)(2,1)} %get-tuple-element.267), channel_id=1, source_target_pairs={{0,8},{2,10},{4,12},{6,14},{8,0},{10,2},{12,4},{14,6},{16,24},{18,... | collective-permute-start | bytes 1572872 | tf_op jit(solution)/shard_map/ppermute | solution.py:860
  374.2 17.7 %collective-permute-start.36 = (bf16[4,64,512]{2,1,0:T(8,128)(2,1)}, bf16[4,64,512]{2,1,0:T(8,128)(2,1)S(1)}, u32[]{:S(2)}, u32[]{:S(2)}) collective-permute-start(bf16[4,64,512]{2,1,0:T(8,128)(2,1)} %get-tuple-element.269), channel_id=1, source_target_pairs={{0,16},{2,18},{4,20},{6,22},{8,24},{10,26},{12,28},{14,30},{16,0},... | collective-permute-start | bytes 786440 | tf_op jit(solution)/shard_map/ppermute | solution.py:860
  390.4 20.1 %collective-permute-start.39 = (bf16[4,64,512]{2,1,0:T(8,128)(2,1)}, bf16[4,64,512]{2,1,0:T(8,128)(2,1)}, u32[]{:S(2)}, u32[]{:S(2)}) collective-permute-start(bf16[4,64,512]{2,1,0:T(8,128)(2,1)} %get-tuple-element.277), channel_id=1, source_target_pairs={{0,16},{2,18},{4,20},{6,22},{8,24},{10,26},{12,28},{14,30},{16,0},... | collective-permute-start | bytes 786440 | tf_op jit(solution)/shard_map/ppermute | solution.py:860
  390.4 14.9 %collective-permute-start.38 = (bf16[4,256,256]{2,1,0:T(8,128)(2,1)S(1)}, bf16[4,256,256]{2,1,0:T(8,128)(2,1)S(1)}, u32[]{:S(2)}, u32[]{:S(2)}) collective-permute-start(bf16[4,256,256]{2,1,0:T(8,128)(2,1)S(1)} %copy-done.39), channel_id=1, source_target_pairs={{0,1},{1,0},{2,3},{3,2},{4,5},{5,4},{6,7},{7,6},{8,9},{9,8},{10,11... | collective-permute-start | bytes 1572872 | tf_op jit(solution)/shard_map/ppermute | solution.py:860
  394.5 21.7 %collective-permute-start.40 = (bf16[4,64,512]{2,1,0:T(8,128)(2,1)}, bf16[4,64,512]{2,1,0:T(8,128)(2,1)}, u32[]{:S(2)}, u32[]{:S(2)}) collective-permute-start(bf16[4,64,512]{2,1,0:T(8,128)(2,1)} %combine.31.refs_0_), channel_id=1, source_target_pairs={{0,16},{2,18},{4,20},{6,22},{8,24},{10,26},{12,28},{14,30},{16,0},... | collective-permute-start | bytes 786440 | tf_op jit(solution)/shard_map/ppermute | solution.py:860
  399.9 18.2 %collective-permute-start.41 = (bf16[4,256,256]{2,1,0:T(8,128)(2,1)}, bf16[4,256,256]{2,1,0:T(8,128)(2,1)}, u32[]{:S(2)}, u32[]{:S(2)}) collective-permute-start(bf16[4,256,256]{2,1,0:T(8,128)(2,1)} %get-tuple-element.290), channel_id=1, source_target_pairs={{0,1},{1,0},{2,3},{3,2},{4,5},{5,4},{6,7},{7,6},{8,9},{9,8},{10,11... | collective-permute-start | bytes 1572872 | tf_op jit(solution)/shard_map/ppermute | solution.py:860
  408.2 16.3 %collective-permute-start.42 = (bf16[4,128,256]{2,1,0:T(8,128)(2,1)}, bf16[4,128,256]{2,1,0:T(8,128)(2,1)}, u32[]{:S(2)}, u32[]{:S(2)}) collective-permute-start(bf16[4,128,256]{2,1,0:T(8,128)(2,1)} %get-tuple-element.286), channel_id=1, source_target_pairs={{0,8},{2,10},{4,12},{6,14},{8,0},{10,2},{12,4},{14,6},{16,24},{18,... | collective-permute-start | bytes 786440 | tf_op jit(solution)/shard_map/ppermute | solution.py:860
  412.4 14.3 %collective-permute-start.43 = (bf16[4,64,512]{2,1,0:T(8,128)(2,1)}, bf16[4,64,512]{2,1,0:T(8,128)(2,1)}, u32[]{:S(2)}, u32[]{:S(2)}) collective-permute-start(bf16[4,64,512]{2,1,0:T(8,128)(2,1)} %combine.34.refs_0_), channel_id=1, source_target_pairs={{0,16},{2,18},{4,20},{6,22},{8,24},{10,26},{12,28},{14,30},{16,0},... | collective-permute-start | bytes 786440 | tf_op jit(solution)/shard_map/ppermute | solution.py:860
  418.1 22.6 %collective-permute-start.44 = (bf16[4,128,512]{2,1,0:T(8,128)(2,1)}, bf16[4,128,512]{2,1,0:T(8,128)(2,1)}, u32[]{:S(2)}, u32[]{:S(2)}) collective-permute-start(bf16[4,128,512]{2,1,0:T(8,128)(2,1)} %join_rows.12.refs_0_), channel_id=1, source_target_pairs={{0,8},{2,10},{4,12},{6,14},{8,0},{10,2},{12,4},{14,6},{16,24},{18,... | collective-permute-start | bytes 1572872 | tf_op jit(solution)/shard_map/ppermute | solution.py:860
  420.2 26.1 %collective-permute-start.45 = (bf16[4,128,256]{2,1,0:T(8,128)(2,1)}, bf16[4,128,256]{2,1,0:T(8,128)(2,1)}, u32[]{:S(2)}, u32[]{:S(2)}) collective-permute-start(bf16[4,128,256]{2,1,0:T(8,128)(2,1)} %get-tuple-element.291), channel_id=1, source_target_pairs={{0,8},{2,10},{4,12},{6,14},{8,0},{10,2},{12,4},{14,6},{16,24},{18,... | collective-permute-start | bytes 786440 | tf_op jit(solution)/shard_map/ppermute | solution.py:860
  426.4 21.8 %collective-permute-start.46 = (bf16[4,64,256]{2,1,0:T(8,128)(2,1)}, bf16[4,64,256]{2,1,0:T(8,128)(2,1)}, u32[]{:S(2)}, u32[]{:S(2)}) collective-permute-start(bf16[4,64,256]{2,1,0:T(8,128)(2,1)} %get-tuple-element.295), channel_id=1, source_target_pairs={{0,16},{2,18},{4,20},{6,22},{8,24},{10,26},{12,28},{14,30},{16,0},... | collective-permute-start | bytes 393224 | tf_op jit(solution)/shard_map/ppermute | solution.py:860
  428.6 30.9 %collective-permute-start.47 = (bf16[4,128,512]{2,1,0:T(8,128)(2,1)}, bf16[4,128,512]{2,1,0:T(8,128)(2,1)}, u32[]{:S(2)}, u32[]{:S(2)}) collective-permute-start(bf16[4,128,512]{2,1,0:T(8,128)(2,1)} %join_rows.13.refs_0_), channel_id=1, source_target_pairs={{0,8},{2,10},{4,12},{6,14},{8,0},{10,2},{12,4},{14,6},{16,24},{18,... | collective-permute-start | bytes 1572872 | tf_op jit(solution)/shard_map/ppermute | solution.py:860
  442.9 26.4 %collective-permute-start.49 = (bf16[4,256,512]{2,1,0:T(8,128)(2,1)}, bf16[4,256,512]{2,1,0:T(8,128)(2,1)}, u32[]{:S(2)}, u32[]{:S(2)}) collective-permute-start(bf16[4,256,512]{2,1,0:T(8,128)(2,1)} %join_rows.14.refs_0_), channel_id=1, source_target_pairs={{0,4},{2,6},{4,0},{6,2},{8,12},{10,14},{12,8},{14,10},{16,20},{18,... | collective-permute-start | bytes 3145736 | tf_op jit(solution)/shard_map/ppermute | solution.py:860
  448.1 13.7 %collective-permute-start.48 = (bf16[4,64,256]{2,1,0:T(8,128)(2,1)}, bf16[4,64,256]{2,1,0:T(8,128)(2,1)S(1)}, u32[]{:S(2)}, u32[]{:S(2)}) collective-permute-start(bf16[4,64,256]{2,1,0:T(8,128)(2,1)} %get-tuple-element.299), channel_id=1, source_target_pairs={{0,16},{2,18},{4,20},{6,22},{8,24},{10,26},{12,28},{14,30},{16,0},... | collective-permute-start | bytes 393224 | tf_op jit(solution)/shard_map/ppermute | solution.py:860
  449.9 22.5 %collective-permute-start.50 = (bf16[4,64,256]{2,1,0:T(8,128)(2,1)}, bf16[4,64,256]{2,1,0:T(8,128)(2,1)}, u32[]{:S(2)}, u32[]{:S(2)}) collective-permute-start(bf16[4,64,256]{2,1,0:T(8,128)(2,1)} %combine.38.refs_0_), channel_id=1, source_target_pairs={{0,16},{2,18},{4,20},{6,22},{8,24},{10,26},{12,28},{14,30},{16,0},... | collective-permute-start | bytes 393224 | tf_op jit(solution)/shard_map/ppermute | solution.py:860
  464.2 26.5 %collective-permute-start.54 = (bf16[4,256,512]{2,1,0:T(8,128)(2,1)}, bf16[4,256,512]{2,1,0:T(8,128)(2,1)}, u32[]{:S(2)}, u32[]{:S(2)}) collective-permute-start(bf16[4,256,512]{2,1,0:T(8,128)(2,1)} %join_rows.15.refs_0_), channel_id=1, source_target_pairs={{0,4},{2,6},{4,0},{6,2},{8,12},{10,14},{12,8},{14,10},{16,20},{18,... | collective-permute-start | bytes 3145736 | tf_op jit(solution)/shard_map/ppermute | solution.py:860
  476.4 18.6 %collective-permute-start.56 = (bf16[4,128,256]{2,1,0:T(8,128)(2,1)}, bf16[4,128,256]{2,1,0:T(8,128)(2,1)S(1)}, u32[]{:S(2)}, u32[]{:S(2)}) collective-permute-start(bf16[4,128,256]{2,1,0:T(8,128)(2,1)} %join_rows.18.refs_0_), channel_id=1, source_target_pairs={{0,8},{2,10},{4,12},{6,14},{8,0},{10,2},{12,4},{14,6},{16,24},{18,... | collective-permute-start | bytes 786440 | tf_op jit(solution)/shard_map/ppermute | solution.py:860
  493.8 15.8 %collective-permute-start.57 = (bf16[4,256,256]{2,1,0:T(8,128)(2,1)}, bf16[4,256,256]{2,1,0:T(8,128)(2,1)}, u32[]{:S(2)}, u32[]{:S(2)}) collective-permute-start(bf16[4,256,256]{2,1,0:T(8,128)(2,1)} %join_rows.19.refs_0_), channel_id=1, source_target_pairs={{0,4},{2,6},{4,0},{6,2},{8,12},{10,14},{12,8},{14,10},{16,20},{18,... | collective-permute-start | bytes 1572872 | tf_op jit(solution)/shard_map/ppermute | solution.py:860
  497.6 22.1 %collective-permute-start.58 = (bf16[4,256,256]{2,1,0:T(8,128)(2,1)}, bf16[4,256,256]{2,1,0:T(8,128)(2,1)}, u32[]{:S(2)}, u32[]{:S(2)}) collective-permute-start(bf16[4,256,256]{2,1,0:T(8,128)(2,1)} %join_rows.21.refs_0_), channel_id=1, source_target_pairs={{0,4},{2,6},{4,0},{6,2},{8,12},{10,14},{12,8},{14,10},{16,20},{18,... | collective-permute-start | bytes 1572872 | tf_op jit(solution)/shard_map/ppermute | solution.py:860
  (64 other events, 746.5 us)
Sparse Core Ops, SparseCore 0:
  292.7 57.4 all-gather.2

commit v3 on v2

--- a/solution.py
+++ b/solution.py
@@ -272,17 +272,6 @@
     )
 
 
-RATE = 0.42
-POLY = (
-    0.23672758308126046,
-    0.24094666497815675,
-    0.18682847081810067,
-    0.2932523313321973,
-    -0.17452300094788806,
-    0.4864472432641871,
-    -0.34587320596419,
-    0.0761939461469462,
-)
 LARGE = 58 * 2**20
 SPEED = 30 * 1.1e9
 HEAVY = 1
@@ -291,14 +280,8 @@
 
 
 def gelu_pair(u):
-    t = 1.0 / (1.0 + (RATE * 0.5**0.5) * jnp.abs(u))
-    total = 0.5 * POLY[-1] * t + 0.5 * POLY[-2]
-    for factor in POLY[-3::-1]:
-        total = total * t + 0.5 * factor
-    bell = jnp.exp(u * u * -0.5)
-    tail = total * t * bell
-    below = jnp.where(u >= 0, 1.0 - tail, tail)
-    return u * below, below + u * bell * 0.3989422804014327
+    below = 0.5 * lax.erf(u * 0.5**0.5) + 0.5
+    return u * below, below + u * jnp.exp(u * u * -0.5) * 0.3989422804014327
 
 
 def matmul(left, right, left_dim=1, right_dim=0):
@@ -327,7 +310,7 @@
 TIMES = {
     "heads": 8,
     "heads_back": 26,
-    "units": 20,
+    "units": 14,
     "units_back": 22,
     "project": 7,
     "turn": 9,
@@ -604,7 +587,7 @@
     )
 
 
-ROW_STEPS = 4
+ROW_STEPS = 1
 
 
 def pair_specs(pair, shape, axis, first=0):
@@ -1213,8 +1196,8 @@
     )
 
 
-MLP_ORDERS = (("x", 2, 4, 8), (2, "x", 4, 8))
-HEAD_ORDERS = ((2, "x", 4, 8), (2, "x", 4, 8))
+MLP_ORDERS = ((4, 8, 2, "x"), ("x", 2, 4, 8))
+HEAD_ORDERS = ((4, "x", 2, 8), (4, 2, "x", 8))
 FORWARD = (
     ("own", 0),
     "a",
@@ -1239,43 +1222,44 @@
     ("ub", 0),
     ("ub", 1),
     ("m", 0),
+    ("m", 1),
     ("fb",),
+    ("hb", 0),
+    ("m", 0),
+    ("h", 0),
     ("m", 1),
-    ("hb", 0),
     ("hb", 1),
-    ("m", 0),
     ("m", 1),
     ("h", 0),
+    ("m", 0),
     ("h", 1),
-    ("m", 0),
     ("m", 1),
+    ("h", 0),
     ("m", 0),
     ("h", 0),
     ("m", 1),
     ("m", 0),
     ("h", 1),
     ("h", 0),
+    ("m", 0),
     ("m", 1),
-    ("m", 0),
-    ("h", 1),
     ("h", 0),
-    ("m", 1),
-    ("m", 0),
     ("h", 1),
     ("h", 0),
     ("m", 1),
     ("h", 1),
     ("m", 0),
     ("h", 0),
+    ("small",),
     ("h", 1),
-    ("m", 0),
     ("h", 0),
     ("m", 1),
     ("h", 1),
+    ("m", 0),
     ("m", 1),
-    ("h", 0),
     ("h", 1),
-    ("h", 0),
+    ("m", 0),
+    ("h", 1),
     ("h", 1),
 )
 
@@ -1431,6 +1415,38 @@
         state["grad_x"] = grad_x
         clock.tick(grad_x)
 
+    def gather_small():
+        def small_of(side):
+            sums = [head_sums[part][side, 0] for part in range(parts)]
+            entries = [entry[:GROUP] for entry in sums] + [entry[2 * GROUP :] for entry in sums]
+            for part in range(2):
+                steps = up_sums[part].shape[0] // 2
+                entries.append(up_sums[part][side * steps : (side + 1) * steps].reshape(-1))
+            return jnp.concatenate(entries)
+
+        gain_one, shift_one, out_sum = state["first"][2:]
+        sums = (out_sum, gain_one, gain_two, shift_one, shift_two, down_sum)
+        split = [small_of(0), small_of(1)]
+        every = lax.all_gather(
+            jnp.concatenate(split + [entry[0] for entry in sums]), ("dp", "mp"), axis=0
+        )
+        state["every"], state["split"] = every, split[0].shape[0]
+
+    def add_small():
+        every = clock.hold(state["every"]).reshape(lax.axis_size("dp"), 2, -1)
+        split_width = state["split"]
+        same = jnp.sum(every, axis=0)
+        straight = same[0, :split_width] + same[1, split_width : 2 * split_width]
+        turned = same[1, :split_width] + same[0, split_width : 2 * split_width]
+        split_sum = jnp.where(lax.axis_index("mp") == 0, straight, turned)
+        shared = (same[0] + same[1])[2 * split_width :].reshape(6, -1)
+        clock.tick(split_sum, shared)
+        state["small"] = (
+            split_sum[: 2 * width].reshape(1, 2, width),
+            split_sum[2 * width :].reshape(1, -1),
+            shared,
+        )
+
     pieces = {}
     outcome = {}
 
@@ -1459,6 +1475,10 @@
             run_first_back()
         elif name == "hb":
             run_heads_back(*rest)
+            if rest[0] == parts - 1:
+                gather_small()
+        elif name == "small":
+            add_small()
         else:
             run_piece(*action)
     for kind in "mh":
@@ -1467,36 +1487,10 @@
                 if not pieces[kind, number].complete:
                     run_piece(kind, number)
     grad_x = state["grad_x"]
-    gain_one, shift_one, out_sum = state["first"][2:]
     grad_down, grad_up = outcome["m"]
     grad_qkv, grad_out_w = outcome["h"]
 
-    def small_of(side):
-        sums = [head_sums[part][side, 0] for part in range(parts)]
-        entries = [entry[:GROUP] for entry in sums] + [entry[2 * GROUP :] for entry in sums]
-        for part in range(2):
-            steps = up_sums[part].shape[0] // 2
-            entries.append(up_sums[part][side * steps : (side + 1) * steps].reshape(-1))
-        return jnp.concatenate(entries)
-
-    shared_small = jnp.concatenate(
-        [entry[0] for entry in (out_sum, gain_one, gain_two, shift_one, shift_two, down_sum)]
-    )
-    own_small, other_small = small_of(0), small_of(1)
-    split_width = own_small.shape[0]
-    every = lax.all_gather(
-        jnp.concatenate([own_small, other_small, shared_small]), ("dp", "mp"), axis=0
-    ).reshape(lax.axis_size("dp"), 2, -1)
-    same = jnp.sum(every, axis=0)
-    column = lax.axis_index("mp")
-    straight = same[0, :split_width] + same[1, split_width : 2 * split_width]
-    turned = same[1, :split_width] + same[0, split_width : 2 * split_width]
-    split_sum = jnp.where(column == 0, straight, turned)
-    grad_qv_bias = split_sum[: 2 * width].reshape(1, 2, width)
-    grad_up_bias = split_sum[2 * width :].reshape(1, -1)
-    small = same[0] + same[1]
-    split_width = 2 * split_width
-    shared = small[split_width:].reshape(6, -1)
+    grad_qv_bias, grad_up_bias, shared = state["small"]
     return (
         layer_out,
         grad_x,

time: 550 us -> 504 us (0.916)
  waiting for transfers between devices: 121 us -> 72.7 us
  Pallas kernels: 317 us -> 304 us
  starting transfers between devices: 55.4 us -> 67.1 us
    all_gather x1, waiting for transfers between devices: 35.7 us -> 7.63 us  [gather_small(): lax.all_gather(jnp.concatenate(split + [entry[0] for entry in sums]), ('d...]
    ppermute x61, waiting for transfers between devices: 85.7 us -> 65.1 us  [swap(): lax.ppermute(value, axis, [(place, place ^ distance) for place in range(c...]
    pallas_call x47, Pallas kernels: 278 us -> 266 us  [run(): pl.pallas_call(kernel, grid=grid, in_specs=in_specs, out_specs=out_specs,...]
    ppermute x61, starting transfers between devices: 55.3 us -> 67.1 us  [swap(): lax.ppermute(value, axis, [(place, place ^ distance) for place in range(c...]
    unnamed x118 -> x122, local copies, waits for them, and re-layouts: 15.2 us -> 17.4 us
  transfers between devices with their start and end apart: 62 -> 62, of which waited for: 21 -> 21; matrix products, arithmetic and copies ran while one was open for 3% -> 4% of each run, Pallas kernels for 47% -> 49%
where the time goes in v3:
time: 504 us; the launch traced here: 494 us
  Pallas kernels  304 us (60%)
  waiting for transfers between devices  72.7 us (14%)
  starting transfers between devices  67.1 us (13%)
  local copies, waits for them, and re-layouts  32.2 us (6%)
  between operations  15.1 us (3%)
    pallas_call x47, Pallas kernels, run(): pl.pallas_call(kernel, grid=grid, in_specs=in_specs, out_specs=out_specs,...  266 us
    ppermute x61, starting transfers between devices, swap(): lax.ppermute(value, axis, [(place, place ^ distance) for place in range(c...  67.1 us
    ppermute x61, waiting for transfers between devices, swap(): lax.ppermute(value, axis, [(place, place ^ distance) for place in range(c...  65.1 us
    pallas_call x4, Pallas kernels, heads_forward(): pl.pallas_call(heads_kernel, grid=(pages,), in_specs=[scalar_spec()] + qk...  32.9 us
    unnamed x122, local copies, waits for them, and re-layouts  17.4 us
  transfers between devices with their start and end apart: 62, of which 21 were waited for; matrix products, arithmetic and copies ran while one was open for 4% of the time, Pallas kernels for 49%

profile of v3, /device:TPU:0, one launch (start us, length us, event | category | flops | bytes accessed | tf_op | source)
XLA Modules:
  0.0 494.0 jit_solution(10197212138750820438)
XLA Ops:
  7.9 2.7 take_blocks.2
  10.6 2.9 collective-permute-start
  13.6 3.0 take_blocks.3
  19.8 8.2 %heads.4 = (bf16[832,1536]{1,0:T(8,128)(2,1)}, bf16[832,512]{1,0:T(8,128)(2,1)}, f32[2,2,4,416]{3,2,1,0:T(4,128)}) custom-call(s32[1]{0:T(128)} %constant.8.clone.1.order_ref, bf16[1,3,1024,512]{3,2,1,0:T(8,128)(2,1)} %refs_6_.3, bf16[1,3,1024,512]{3,2,1,0:T(8,128)(2,1)} %refs_6_.3, bf16[1,3,1024,512]{3,2,1,0:T(8,128)(2,1)} %refs_6_.3, ...), custom_call_target="tpu_custom_call" | custom-call | flops 263999995904 | bytes 1 | tf_op jit(solution)/shard_map/heads/pallas_call | solution.py:419
  31.3 8.3 %heads.5 = (bf16[832,1536]{1,0:T(8,128)(2,1)}, bf16[832,512]{1,0:T(8,128)(2,1)}, f32[2,2,4,416]{3,2,1,0:T(4,128)}) custom-call(s32[1]{0:T(128)} %constant.8.clone.1.order_ref, bf16[1,3,1024,512]{3,2,1,0:T(8,128)(2,1)} %refs_6_.3, bf16[1,3,1024,512]{3,2,1,0:T(8,128)(2,1)} %refs_6_.3, ...), custom_call_target="tpu_custom_call", output_to_operand_aliasing={{0}: (7, {}), {1}: (8, {}), {2}: (9, {})} | custom-call | flops 263999995904 | bytes 1 | tf_op jit(solution)/shard_map/heads/pallas_call | solution.py:419
  42.2 6.8 %collective-permute-done.6.piece_ref = bf16[1,128,2048]{2,1,0:T(8,128)(2,1)} collective-permute-done((bf16[1,128,2048]{2,1,0:T(8,128)(2,1)}, bf16[1,128,2048]{2,1,0:T(8,128)(2,1)}, u32[]{:S(2)}, u32[]{:S(2)}) %collective-permute-start.6) | collective-permute-done | bytes 524320 | tf_op jit(solution)/shard_map/ppermute | solution.py:843
  52.7 8.2 %heads.6 = (bf16[832,1536]{1,0:T(8,128)(2,1)}, bf16[832,512]{1,0:T(8,128)(2,1)}, f32[2,2,4,416]{3,2,1,0:T(4,128)}) custom-call(s32[1]{0:T(128)} %bitcast.order_ref, bf16[1,3,256,256]{3,2,1,0:T(8,128)(2,1)} %collective-permute-done.w0_ref.refs_14_, bf16[1,3,256,256]{3,2,1,0:T(8,128)(2,1)} %collective-permute-done.3.w1_ref.refs_15_, ...), custom_call_target="tpu_custom_call" | custom-call | flops 263999995904 | bytes 1 | tf_op jit(solution)/shard_map/heads/pallas_call | solution.py:419
  69.4 8.2 %heads.7 = (bf16[832,1536]{1,0:T(8,128)(2,1)}, bf16[832,512]{1,0:T(8,128)(2,1)}, f32[2,2,4,416]{3,2,1,0:T(4,128)}) custom-call(s32[1]{0:T(128)} %bitcast.order_ref, bf16[1,3,256,256]{3,2,1,0:T(8,128)(2,1)} %collective-permute-done.1.w0_ref.refs_14_, ...), custom_call_target="tpu_custom_call", output_to_operand_aliasing={{0}: (7, {}), {1}: (8, {}), {2}: (9, {})} | custom-call | flops 263999995904 | bytes 1 | tf_op jit(solution)/shard_map/heads/pallas_call | solution.py:419
  82.8 7.6 %project.1 = (f32[832,1024]{1,0:T(8,128)}, f32[832,1024]{1,0:T(8,128)}, bf16[832,1024]{1,0:T(8,128)(2,1)}) custom-call(s32[1]{0:T(128)} %bitcast.order_ref, bf16[832,512]{1,0:T(8,128)(2,1)} %get-tuple-element.184.a_ref.refs_2_, bf16[832,512]{1,0:T(8,128)(2,1)} %get-tuple-element.202.b_ref.refs_13_, bf16[1,512,1024]{2,1,0:T(8,128)(2,1)} %refs_10_.3, ...), custom_call_target="tpu_custom_call" | custom-call | flops 230999998464 | bytes 1 | tf_op jit(solution)/shard_map/project/pallas_call | solution.py:334
  98.4 3.0 join_depth.2.up_a.refs_8_
  101.3 14.1 %units.2 = (bf16[832,2048]{1,0:T(8,128)(2,1)}, bf16[832,2048]{1,0:T(8,128)(2,1)}, f32[832,1024]{1,0:T(8,128)}) custom-call(s32[1]{0:T(128)} %constant.8.clone.1.order_ref, bf16[832,1024]{1,0:T(8,128)(2,1)} %get-tuple-element.215.h_ref, bf16[1,1024,2048]{2,1,0:T(8,128)(2,1)} %refs_3_.5, bf16[1,1024,2048]{2,1,0:T(8,128)(2,1)} %refs_3_.5, f32[1,2048]{1,0:T(1,128)} %b_ref.1, ...), custom_call_target="tpu_custom_call" | custom-call | flops 461999996928 | bytes 1 | tf_op jit(solution)/shard_map/units/pallas_call | solution.py:334
  115.5 3.2 join_depth.3.down_a.refs_10_
  119.9 3.4 collective-permute-done.24.down_b.refs_11_
  124.5 14.1 %units.3 = (bf16[832,2048]{1,0:T(8,128)(2,1)}, bf16[832,2048]{1,0:T(8,128)(2,1)}, f32[832,1024]{1,0:T(8,128)}) custom-call(s32[1]{0:T(128)} %bitcast.3.order_ref.core_ref, bf16[832,1024]{1,0:T(8,128)(2,1)} %get-tuple-element.215.h_ref, bf16[1,512,2048]{2,1,0:T(8,128)(2,1)} %join_depth.2.up_a.refs_8_, ...), custom_call_target="tpu_custom_call" | custom-call | flops 461999996928 | bytes 1 | tf_op jit(solution)/shard_map/units/pallas_call | solution.py:334
  138.7 8.6 %turn.1 = (f32[832,1024]{1,0:T(8,128)}, f32[832,1024]{1,0:T(8,128)}, bf16[832,1024]{1,0:T(8,128)(2,1)}, f32[1,1024]{1,0:T(1,128)}, f32[1,1024]{1,0:T(1,128)}, /*index=5*/f32[1,1024]{1,0:T(1,128)}) custom-call(f32[832,1024]{1,0:T(8,128)} %get-tuple-element.213.a_ref, f32[832,1024]{1,0:T(8,128)} %get-tuple-element.217.b_ref, ...), custom_call_target="tpu_custom_call" | custom-call | flops 297000009728 | bytes 1 | tf_op jit(solution)/shard_map/turn/pallas_call | solution.py:334
  147.3 24.4 %units_back.2 = (bf16[8,512,512]{2,1,0:T(8,128)(2,1)}, bf16[8,512,512]{2,1,0:T(8,128)(2,1)}, f32[832,1024]{1,0:T(8,128)}, f32[4,1,512]{2,1,0:T(1,128)}) custom-call(s32[1]{0:T(128)} %bitcast.3.order_ref.core_ref, s32[1]{0:T(128)} %bitcast.3.order_ref.core_ref, bf16[832,1024]{1,0:T(8,128)(2,1)} %get-tuple-element.227.g_ref, ...), custom_call_target="tpu_custom_call" | custom-call | flops 726000009216 | bytes 1 | tf_op jit(solution)/shard_map/units_back/pallas_call | solution.py:334
  172.3 24.0 %units_back.3 = (bf16[8,512,512]{2,1,0:T(8,128)(2,1)}, bf16[8,512,512]{2,1,0:T(8,128)(2,1)}, f32[832,1024]{1,0:T(8,128)}, f32[4,1,512]{2,1,0:T(1,128)}) custom-call(s32[1]{0:T(128)} %bitcast.3.order_ref.core_ref, s32[1]{0:T(128)} %bitcast.3.order_ref.core_ref, bf16[832,1024]{1,0:T(8,128)(2,1)} %get-tuple-element.227.g_ref, ...), custom_call_target="tpu_custom_call" | custom-call | flops 726000009216 | bytes 1 | tf_op jit(solution)/shard_map/units_back/pallas_call | solution.py:334
  198.4 6.4 %combine.20 = (bf16[8,256,512]{2,1,0:T(8,128)(2,1)}, bf16[4,256,512]{2,1,0:T(8,128)(2,1)}, bf16[4,256,512]{2,1,0:T(8,128)(2,1)}) custom-call(s32[4]{0:T(128)} %pad_add_fusion.word_ref, bf16[8,512,512]{2,1,0:T(8,128)(2,1)} %get-tuple-element.232.refs_0_.refs_2_, bf16[8,512,512]{2,1,0:T(8,128)(2,1)} %collective-permute-done.25.refs_1_.refs_3_, ...), custom_call_target="tpu_custom_call" | custom-call | flops 65999998976 | bytes 1 | tf_op jit(solution)/shard_map/combine/pallas_call | solution.py:334
  208.1 4.1 combine.21
  213.7 8.6 %first_back.1 = (f32[832,1024]{1,0:T(8,128)}, bf16[832,1024]{1,0:T(8,128)(2,1)}, f32[1,1024]{1,0:T(1,128)}, f32[1,1024]{1,0:T(1,128)}, f32[1,1024]{1,0:T(1,128)}) custom-call(f32[832,1024]{1,0:T(8,128)} %get-tuple-element.226.refs_0_, f32[832,1024]{1,0:T(8,128)} %get-tuple-element.228.refs_1_, f32[832,1024]{1,0:T(8,128)} %get-tuple-element.237.refs_2_, ...), custom_call_target="tpu_custom_call" | custom-call | flops 330000007168 | bytes 1 | tf_op jit(solution)/shard_map/first_back/pallas_call | solution.py:334
  222.4 27.6 %heads_back.2 = (bf16[8,512,256]{2,1,0:T(8,128)(2,1)}, bf16[8,512,256]{2,1,0:T(8,128)(2,1)}, f32[832,1024]{1,0:T(8,128)}, f32[2,1,768]{2,1,0:T(1,128)}) custom-call(s32[1]{0:T(128)} %bitcast.3.order_ref.core_ref, s32[1]{0:T(128)} %bitcast.order_ref, bf16[832,1024]{1,0:T(8,128)(2,1)} %x_ref.8, bf16[832,1024]{1,0:T(8,128)(2,1)} %get-tuple-element.257.g_ref, ...), custom_call_target="tpu_custom_call" | custom-call | flops 857999998976 | bytes 1 | tf_op jit(solution)/shard_map/heads_back/pallas_call | solution.py:334
  253.1 3.9 combine.22
  258.3 3.9 combine.23
  262.2 4.9 combine.24
  269.9 2.6 collective-permute-start.32
  272.6 27.8 %heads_back.3 = (bf16[8,512,256]{2,1,0:T(8,128)(2,1)}, bf16[8,512,256]{2,1,0:T(8,128)(2,1)}, f32[832,1024]{1,0:T(8,128)}, f32[2,1,768]{2,1,0:T(1,128)}) custom-call(s32[1]{0:T(128)} %bitcast.3.order_ref.core_ref, s32[1]{0:T(128)} %bitcast.order_ref, bf16[832,1024]{1,0:T(8,128)(2,1)} %x_ref.8, bf16[832,1024]{1,0:T(8,128)(2,1)} %get-tuple-element.257.g_ref, ...), custom_call_target="tpu_custom_call" | custom-call | flops 857999998976 | bytes 1 | tf_op jit(solution)/shard_map/heads_back/pallas_call | solution.py:334
  302.2 2.8 combine.25
  305.4 12.2 %collective-permute-done.31.refs_1_.refs_3_ = bf16[8,256,256]{2,1,0:T(8,128)(2,1)} collective-permute-done((bf16[8,256,256]{2,1,0:T(8,128)(2,1)}, bf16[8,256,256]{2,1,0:T(8,128)(2,1)}, u32[]{:S(2)}, u32[]{:S(2)}) %collective-permute-start.31) | collective-permute-done | bytes 1048608 | tf_op jit(solution)/shard_map/ppermute | solution.py:843
  317.6 2.6 combine.26
  320.2 2.7 combine.27
  325.6 4.0 combine.28
  343.7 2.6 collective-permute-done.37.refs_1_
  350.6 2.9 collective-permute-start.43
  357.7 7.6 %all-gather.3.cloned.1.call-done = f32[393216]{0:T(1024)} async-done(((f32[12288]{0:T(1024)}), f32[393216]{0:T(1024)}) %all-gather.3.cloned.1.call-update) | async-done | bytes 1572880 | tf_op jit(solution)/shard_map/all_gather | solution.py:1430
  365.3 2.6 reshape.99
  367.9 9.0 %collective-permute-done.40.refs_1_.refs_3_ = bf16[8,256,256]{2,1,0:T(8,128)(2,1)} collective-permute-done((bf16[8,256,256]{2,1,0:T(8,128)(2,1)}, bf16[8,256,256]{2,1,0:T(8,128)(2,1)}, u32[]{:S(2)}, u32[]{:S(2)}) %collective-permute-start.40) | collective-permute-done | bytes 1048608 | tf_op jit(solution)/shard_map/ppermute | solution.py:843
  376.9 2.7 combine.35
  393.1 2.5 collective-permute-done.45.refs_1_.refs_3_
  403.9 7.6 %collective-permute-done.47.refs_1_ = bf16[4,128,512]{2,1,0:T(8,128)(2,1)} collective-permute-done((bf16[4,128,512]{2,1,0:T(8,128)(2,1)}, bf16[4,128,512]{2,1,0:T(8,128)(2,1)}, u32[]{:S(2)}, u32[]{:S(2)}) %collective-permute-start.47) | collective-permute-done | bytes 524320 | tf_op jit(solution)/shard_map/ppermute | solution.py:843
  421.5 2.6 collective-permute-start.56
  427.2 3.3 collective-permute-start.54
  435.8 2.4 collective-permute-done.53.refs_1_
  438.2 3.0 join_rows.19.refs_2_
  441.2 6.4 %collective-permute-done.54.refs_1_ = bf16[4,64,256]{2,1,0:T(8,128)(2,1)S(1)} collective-permute-done((bf16[4,64,256]{2,1,0:T(8,128)(2,1)}, bf16[4,64,256]{2,1,0:T(8,128)(2,1)S(1)}, u32[]{:S(2)}, u32[]{:S(2)}) %collective-permute-start.54) | collective-permute-done | bytes 131104 | tf_op jit(solution)/shard_map/ppermute | solution.py:843
  451.8 3.0 join_rows.21.refs_0_
  459.2 4.2 collective-permute-start.59
  464.8 9.8 %finish.2 = (f32[2048,1024]{1,0:T(8,128)}, f32[1024,2048]{1,0:T(8,128)}) custom-call(s32[1]{0:T(128)} %bitcast.3.order_ref.core_ref, bf16[4,512,512]{2,1,0:T(8,128)(2,1)} %join_rows.21.refs_0_, bf16[4,512,512]{2,1,0:T(8,128)(2,1)} %copy-done.36, bf16[4,512,512]{2,1,0:T(8,128)(2,1)} %join_rows.19.refs_2_, bf16[4,512,512]{2,1,0:T(8,128)(2,1)} %copy-done.34), custom_call_target="tpu_custom_call" | custom-call | flops 198000001024 | bytes 1 | tf_op jit(solution)/shard_map/finish/pallas_call | solution.py:334
  481.0 5.8 %finish.3 = (f32[3,1024,512]{2,1,0:T(8,128)}, f32[512,1024]{1,0:T(8,128)}) custom-call(s32[1]{0:T(128)} %bitcast.3.order_ref.core_ref, bf16[4,512,256]{2,1,0:T(8,128)(2,1)} %join_rows.18.refs_0_, bf16[4,512,256]{2,1,0:T(8,128)(2,1)} %collective-permute-done.52.refs_1_, bf16[4,512,256]{2,1,0:T(8,128)(2,1)} %join_rows.23.refs_2_, bf16[4,512,256]{2,1,0:T(8,128)(2,1)} %copy-done.37), custom_call_target="tpu_custom_call" | custom-call | flops 198000001024 | bytes 1 | tf_op jit(solution)/shard_map/finish/pallas_call | solution.py:334
  (285 shorter events, 135.7 us)
Async XLA Ops:
  7.2 358.1 %all-gather.3.cloned.1.call-start = ((), (), s32[]{:S(2)}) async-start(), calls=%async_computation | async-start | bytes 1622016 | tf_op jit(solution)/shard_map/all_gather | solution.py:1430
  10.6 18.7 %collective-permute-start = (bf16[1,3,256,256]{3,2,1,0:T(8,128)(2,1)}, bf16[1,3,256,256]{3,2,1,0:T(8,128)(2,1)}, u32[]{:S(2)}, u32[]{:S(2)}) collective-permute-start(bf16[1,3,256,256]{3,2,1,0:T(8,128)(2,1)} %get-tuple-element.175), channel_id=1, source_target_pairs={{0,1},{1,0},{2,3},{3,2},{4,5},{5,4},{6,7},{7,6},{8,9},{9,8},{10,11... | collective-permute-start | bytes 1179656 | tf_op jit(solution)/shard_map/ppermute | solution.py:843
  13.5 26.0 %collective-permute-start.1 = (bf16[1,3,256,256]{3,2,1,0:T(8,128)(2,1)}, bf16[1,3,256,256]{3,2,1,0:T(8,128)(2,1)}, u32[]{:S(2)}, u32[]{:S(2)}) collective-permute-start(bf16[1,3,256,256]{3,2,1,0:T(8,128)(2,1)} %get-tuple-element.185), channel_id=1, source_target_pairs={{0,1},{1,0},{2,3},{3,2},{4,5},{5,4},{6,7},{7,6},{8,9},{9,8},{10,11... | collective-permute-start | bytes 1179656 | tf_op jit(solution)/shard_map/ppermute | solution.py:843
  16.6 25.1 %collective-permute-start.7 = (bf16[1,512,256]{2,1,0:T(8,128)(2,1)}, bf16[1,512,256]{2,1,0:T(8,128)(2,1)}, u32[]{:S(2)}, u32[]{:S(2)}) collective-permute-start(bf16[1,512,256]{2,1,0:T(8,128)(2,1)} %get-tuple-element.177), channel_id=1, source_target_pairs={{0,1},{1,0},{2,3},{3,2},{4,5},{5,4},{6,7},{7,6},{8,9},{9,8},{10,11... | collective-permute-start | bytes 786440 | tf_op jit(solution)/shard_map/ppermute | solution.py:843
  18.6 30.5 %collective-permute-start.6 = (bf16[1,128,2048]{2,1,0:T(8,128)(2,1)}, bf16[1,128,2048]{2,1,0:T(8,128)(2,1)}, u32[]{:S(2)}, u32[]{:S(2)}) collective-permute-start(bf16[1,128,2048]{2,1,0:T(8,128)(2,1)} %get-tuple-element.188), channel_id=1, source_target_pairs={{0,1},{1,0},{2,3},{3,2},{4,5},{5,4},{6,7},{7,6},{8,9},{9,8},{10,11... | collective-permute-start | bytes 1572872 | tf_op jit(solution)/shard_map/ppermute | solution.py:843
  31.3 20.5 %collective-permute-start.4 = (bf16[1,3,256,256]{3,2,1,0:T(8,128)(2,1)}, bf16[1,3,256,256]{3,2,1,0:T(8,128)(2,1)}, u32[]{:S(2)}, u32[]{:S(2)}) collective-permute-start(bf16[1,3,256,256]{3,2,1,0:T(8,128)(2,1)} %collective-permute-done.w0_ref.refs_14_), channel_id=1, source_target_pairs={{0,2},{2,0},{4,6},{6,4},{8,10},{10,8},{12,14},{14,12},{16,18},{18,... | collective-permute-start | bytes 1179656 | tf_op jit(solution)/shard_map/ppermute | solution.py:843
  39.6 12.4 %collective-permute-start.5 = (bf16[1,3,256,256]{3,2,1,0:T(8,128)(2,1)}, bf16[1,3,256,256]{3,2,1,0:T(8,128)(2,1)S(1)}, u32[]{:S(2)}, u32[]{:S(2)}) collective-permute-start(bf16[1,3,256,256]{3,2,1,0:T(8,128)(2,1)} %collective-permute-done.3.w1_ref.refs_15_), channel_id=1, source_target_pairs={{0,2},{2,0},{4,6},{6,4},{8,10},{10,8},{12,14},{14,12},{16,18},{18,... | collective-permute-start | bytes 1179656 | tf_op jit(solution)/shard_map/ppermute | solution.py:843
  40.1 11.0 %collective-permute-start.8 = (f32[3072]{0:T(1024)S(1)}, f32[3072]{0:T(1024)S(1)}, u32[]{:S(2)}, u32[]{:S(2)}) collective-permute-start(f32[3072]{0:T(1024)S(1)} %pad_maximum_fusion), channel_id=1, source_target_pairs={{0,1},{1,0},{2,3},{3,2},{4,5},{5,4},{6,7},{7,6},{8,9},{9,8},{10,11... | collective-permute-start | bytes 36872 | tf_op jit(solution)/shard_map/ppermute | solution.py:843
  41.7 24.3 %collective-permute-start.11 = (bf16[1,2048,128]{2,1,0:T(8,128)(2,1)}, bf16[1,2048,128]{2,1,0:T(8,128)(2,1)}, u32[]{:S(2)}, u32[]{:S(2)}) collective-permute-start(bf16[1,2048,128]{2,1,0:T(8,128)(2,1)} %get-tuple-element.195), channel_id=1, source_target_pairs={{0,1},{1,0},{2,3},{3,2},{4,5},{5,4},{6,7},{7,6},{8,9},{9,8},{10,11... | collective-permute-start | bytes 1572872 | tf_op jit(solution)/shard_map/ppermute | solution.py:843
  49.1 12.4 %collective-permute-start.2 = (bf16[1,3,256,256]{3,2,1,0:T(8,128)(2,1)}, bf16[1,3,256,256]{3,2,1,0:T(8,128)(2,1)}, u32[]{:S(2)}, u32[]{:S(2)}) collective-permute-start(bf16[1,3,256,256]{3,2,1,0:T(8,128)(2,1)} %collective-permute-done.1.w0_ref.refs_14_), channel_id=1, source_target_pairs={{0,4},{2,6},{4,0},{6,2},{8,12},{10,14},{12,8},{14,10},{16,20},{18,... | collective-permute-start | bytes 1179656 | tf_op jit(solution)/shard_map/ppermute | solution.py:843
  51.1 16.2 %collective-permute-start.9 = (bf16[1,3,256,256]{3,2,1,0:T(8,128)(2,1)}, bf16[1,3,256,256]{3,2,1,0:T(8,128)(2,1)}, u32[]{:S(2)}, u32[]{:S(2)}) collective-permute-start(bf16[1,3,256,256]{3,2,1,0:T(8,128)(2,1)} %collective-permute-done.1.w0_ref.refs_14_), channel_id=1, source_target_pairs={{0,2},{2,0},{4,6},{6,4},{8,10},{10,8},{12,14},{14,12},{16,18},{18,... | collective-permute-start | bytes 1179656 | tf_op jit(solution)/shard_map/ppermute | solution.py:843
  51.8 12.7 %collective-permute-start.12 = (bf16[1,512,256]{2,1,0:T(8,128)(2,1)}, bf16[1,512,256]{2,1,0:T(8,128)(2,1)}, u32[]{:S(2)}, u32[]{:S(2)}) collective-permute-start(bf16[1,512,256]{2,1,0:T(8,128)(2,1)} %collective-permute-done.7.w0.refs_18_), channel_id=1, source_target_pairs={{0,4},{2,6},{4,0},{6,2},{8,12},{10,14},{12,8},{14,10},{16,20},{18,... | collective-permute-start | bytes 786440 | tf_op jit(solution)/shard_map/ppermute | solution.py:843
  62.1 15.4 %collective-permute-start.15 = (bf16[1,128,2048]{2,1,0:T(8,128)(2,1)}, bf16[1,128,2048]{2,1,0:T(8,128)(2,1)}, u32[]{:S(2)}, u32[]{:S(2)}) collective-permute-start(bf16[1,128,2048]{2,1,0:T(8,128)(2,1)} %collective-permute-done.6.piece_ref), channel_id=1, source_target_pairs={{0,4},{2,6},{4,0},{6,2},{8,12},{10,14},{12,8},{14,10},{16,20},{18,... | collective-permute-start | bytes 1572872 | tf_op jit(solution)/shard_map/ppermute | solution.py:843
  64.5 14.4 %collective-permute-start.16 = (bf16[1,128,2048]{2,1,0:T(8,128)(2,1)}, bf16[1,128,2048]{2,1,0:T(8,128)(2,1)}, u32[]{:S(2)}, u32[]{:S(2)}) collective-permute-start(bf16[1,128,2048]{2,1,0:T(8,128)(2,1)} %collective-permute-done.6.piece_ref), channel_id=1, source_target_pairs={{0,8},{2,10},{4,12},{6,14},{8,0},{10,2},{12,4},{14,6},{16,24},{18,... | collective-permute-start | bytes 1572872 | tf_op jit(solution)/shard_map/ppermute | solution.py:843
  66.0 15.7 %collective-permute-start.13 = (bf16[1,512,256]{2,1,0:T(8,128)(2,1)}, bf16[1,512,256]{2,1,0:T(8,128)(2,1)}, u32[]{:S(2)}, u32[]{:S(2)}) collective-permute-start(bf16[1,512,256]{2,1,0:T(8,128)(2,1)} %collective-permute-done.7.w0.refs_18_), channel_id=1, source_target_pairs={{0,2},{2,0},{4,6},{6,4},{8,10},{10,8},{12,14},{14,12},{16,18},{18,... | collective-permute-start | bytes 786440 | tf_op jit(solution)/shard_map/ppermute | solution.py:843
  67.3 15.5 %collective-permute-start.14 = (bf16[1,512,256]{2,1,0:T(8,128)(2,1)}, bf16[1,512,256]{2,1,0:T(8,128)(2,1)}, u32[]{:S(2)}, u32[]{:S(2)}) collective-permute-start(bf16[1,512,256]{2,1,0:T(8,128)(2,1)} %collective-permute-done.12.w1.refs_19_), channel_id=1, source_target_pairs={{0,2},{2,0},{4,6},{6,4},{8,10},{10,8},{12,14},{14,12},{16,18},{18,... | collective-permute-start | bytes 786440 | tf_op jit(solution)/shard_map/ppermute | solution.py:843
  67.8 22.6 %collective-permute-start.17 = (bf16[1,2048,128]{2,1,0:T(8,128)(2,1)}, bf16[1,2048,128]{2,1,0:T(8,128)(2,1)}, u32[]{:S(2)}, u32[]{:S(2)}) collective-permute-start(bf16[1,2048,128]{2,1,0:T(8,128)(2,1)} %collective-permute-done.11.piece_ref), channel_id=1, source_target_pairs={{0,4},{2,6},{4,0},{6,2},{8,12},{10,14},{12,8},{14,10},{16,20},{18,... | collective-permute-start | bytes 1572872 | tf_op jit(solution)/shard_map/ppermute | solution.py:843
  77.5 15.2 %collective-permute-start.18 = (bf16[1,2048,128]{2,1,0:T(8,128)(2,1)}, bf16[1,2048,128]{2,1,0:T(8,128)(2,1)}, u32[]{:S(2)}, u32[]{:S(2)}) collective-permute-start(bf16[1,2048,128]{2,1,0:T(8,128)(2,1)} %collective-permute-done.11.piece_ref), channel_id=1, source_target_pairs={{0,8},{2,10},{4,12},{6,14},{8,0},{10,2},{12,4},{14,6},{16,24},{18,... | collective-permute-start | bytes 1572872 | tf_op jit(solution)/shard_map/ppermute | solution.py:843
  80.8 17.5 %collective-permute-start.19 = (bf16[1,128,1024]{2,1,0:T(8,128)(2,1)}, bf16[1,128,1024]{2,1,0:T(8,128)(2,1)}, u32[]{:S(2)}, u32[]{:S(2)}) collective-permute-start(bf16[1,128,1024]{2,1,0:T(8,128)(2,1)} %get-tuple-element.204), channel_id=1, source_target_pairs={{0,8},{2,10},{4,12},{6,14},{8,0},{10,2},{12,4},{14,6},{16,24},{18,... | collective-permute-start | bytes 786440 | tf_op jit(solution)/shard_map/ppermute | solution.py:843
  81.7 16.7 %collective-permute-start.20 = (bf16[1,128,1024]{2,1,0:T(8,128)(2,1)}, bf16[1,128,1024]{2,1,0:T(8,128)(2,1)}, u32[]{:S(2)}, u32[]{:S(2)}) collective-permute-start(bf16[1,128,1024]{2,1,0:T(8,128)(2,1)} %get-tuple-element.205), channel_id=1, source_target_pairs={{0,4},{2,6},{4,0},{6,2},{8,12},{10,14},{12,8},{14,10},{16,20},{18,... | collective-permute-start | bytes 786440 | tf_op jit(solution)/shard_map/ppermute | solution.py:843
  94.7 20.8 %collective-permute-start.21 = (bf16[1,1024,128]{2,1,0:T(8,128)(2,1)}, bf16[1,1024,128]{2,1,0:T(8,128)(2,1)}, u32[]{:S(2)}, u32[]{:S(2)}) collective-permute-start(bf16[1,1024,128]{2,1,0:T(8,128)(2,1)} %get-tuple-element.209), channel_id=1, source_target_pairs={{0,8},{2,10},{4,12},{6,14},{8,0},{10,2},{12,4},{14,6},{16,24},{18,... | collective-permute-start | bytes 786440 | tf_op jit(solution)/shard_map/ppermute | solution.py:843
  96.0 19.5 %collective-permute-start.22 = (bf16[1,1024,128]{2,1,0:T(8,128)(2,1)}, bf16[1,1024,128]{2,1,0:T(8,128)(2,1)}, u32[]{:S(2)}, u32[]{:S(2)}) collective-permute-start(bf16[1,1024,128]{2,1,0:T(8,128)(2,1)} %get-tuple-element.210), channel_id=1, source_target_pairs={{0,4},{2,6},{4,0},{6,2},{8,12},{10,14},{12,8},{14,10},{16,20},{18,... | collective-permute-start | bytes 786440 | tf_op jit(solution)/shard_map/ppermute | solution.py:843
  101.3 18.5 %collective-permute-start.23 = (bf16[1,512,2048]{2,1,0:T(8,128)(2,1)}, bf16[1,512,2048]{2,1,0:T(8,128)(2,1)}, u32[]{:S(2)}, u32[]{:S(2)}) collective-permute-start(bf16[1,512,2048]{2,1,0:T(8,128)(2,1)} %join_depth.2.up_a.refs_8_), channel_id=1, source_target_pairs={{0,2},{2,0},{4,6},{6,4},{8,10},{10,8},{12,14},{14,12},{16,18},{18,... | collective-permute-start | bytes 6291464 | tf_op jit(solution)/shard_map/ppermute | solution.py:843
  171.8 26.6 %collective-permute-start.25 = (bf16[8,512,512]{2,1,0:T(8,128)(2,1)}, bf16[8,512,512]{2,1,0:T(8,128)(2,1)}, u32[]{:S(2)}, u32[]{:S(2)}) collective-permute-start(bf16[8,512,512]{2,1,0:T(8,128)(2,1)} %get-tuple-element.233), channel_id=1, source_target_pairs={{0,2},{2,0},{4,6},{6,4},{8,10},{10,8},{12,14},{14,12},{16,18},{18,... | collective-permute-start | bytes 12582920 | tf_op jit(solution)/shard_map/ppermute | solution.py:843
  204.8 48.2 %collective-permute-start.27 = (bf16[8,256,512]{2,1,0:T(8,128)(2,1)}, bf16[8,256,512]{2,1,0:T(8,128)(2,1)}, u32[]{:S(2)}, u32[]{:S(2)}) collective-permute-start(bf16[8,256,512]{2,1,0:T(8,128)(2,1)} %get-tuple-element.234), channel_id=1, source_target_pairs={{0,8},{2,10},{4,12},{6,14},{8,0},{10,2},{12,4},{14,6},{16,24},{18,... | collective-permute-start | bytes 6291464 | tf_op jit(solution)/shard_map/ppermute | solution.py:843
  212.2 50.0 %collective-permute-start.29 = (bf16[4,512,512]{2,1,0:T(8,128)(2,1)}, bf16[4,512,512]{2,1,0:T(8,128)(2,1)}, u32[]{:S(2)}, u32[]{:S(2)}) collective-permute-start(bf16[4,512,512]{2,1,0:T(8,128)(2,1)} %combine.21), channel_id=1, source_target_pairs={{0,1},{1,0},{2,3},{3,2},{4,5},{5,4},{6,7},{7,6},{8,9},{9,8},{10,11... | collective-permute-start | bytes 6291464 | tf_op jit(solution)/shard_map/ppermute | solution.py:843
  267.1 35.1 %collective-permute-start.30 = (bf16[4,256,512]{2,1,0:T(8,128)(2,1)}, bf16[4,256,512]{2,1,0:T(8,128)(2,1)}, u32[]{:S(2)}, u32[]{:S(2)}) collective-permute-start(bf16[4,256,512]{2,1,0:T(8,128)(2,1)} %get-tuple-element.256), channel_id=1, source_target_pairs={{0,4},{2,6},{4,0},{6,2},{8,12},{10,14},{12,8},{14,10},{16,20},{18,... | collective-permute-start | bytes 3145736 | tf_op jit(solution)/shard_map/ppermute | solution.py:843
  268.3 49.3 %collective-permute-start.31 = (bf16[8,256,256]{2,1,0:T(8,128)(2,1)}, bf16[8,256,256]{2,1,0:T(8,128)(2,1)}, u32[]{:S(2)}, u32[]{:S(2)}) collective-permute-start(bf16[8,256,256]{2,1,0:T(8,128)(2,1)} %get-tuple-element.254), channel_id=1, source_target_pairs={{0,8},{2,10},{4,12},{6,14},{8,0},{10,2},{12,4},{14,6},{16,24},{18,... | collective-permute-start | bytes 3145736 | tf_op jit(solution)/shard_map/ppermute | solution.py:843
  269.9 50.4 %collective-permute-start.32 = (bf16[8,128,512]{2,1,0:T(8,128)(2,1)}, bf16[8,128,512]{2,1,0:T(8,128)(2,1)}, u32[]{:S(2)}, u32[]{:S(2)}) collective-permute-start(bf16[8,128,512]{2,1,0:T(8,128)(2,1)} %get-tuple-element.251), channel_id=1, source_target_pairs={{0,16},{2,18},{4,20},{6,22},{8,24},{10,26},{12,28},{14,30},{16,0},... | collective-permute-start | bytes 3145736 | tf_op jit(solution)/shard_map/ppermute | solution.py:843
  302.1 23.5 %collective-permute-start.33 = (bf16[8,512,256]{2,1,0:T(8,128)(2,1)}, bf16[8,512,256]{2,1,0:T(8,128)(2,1)}, u32[]{:S(2)}, u32[]{:S(2)}) collective-permute-start(bf16[8,512,256]{2,1,0:T(8,128)(2,1)} %get-tuple-element.273), channel_id=1, source_target_pairs={{0,2},{2,0},{4,6},{6,4},{8,10},{10,8},{12,14},{14,12},{16,18},{18,... | collective-permute-start | bytes 6291464 | tf_op jit(solution)/shard_map/ppermute | solution.py:843
  305.0 24.6 %collective-permute-start.34 = (bf16[4,128,512]{2,1,0:T(8,128)(2,1)}, bf16[4,128,512]{2,1,0:T(8,128)(2,1)}, u32[]{:S(2)}, u32[]{:S(2)}) collective-permute-start(bf16[4,128,512]{2,1,0:T(8,128)(2,1)} %get-tuple-element.262), channel_id=1, source_target_pairs={{0,8},{2,10},{4,12},{6,14},{8,0},{10,2},{12,4},{14,6},{16,24},{18,... | collective-permute-start | bytes 1572872 | tf_op jit(solution)/shard_map/ppermute | solution.py:843
  323.0 18.4 %collective-permute-start.36 = (bf16[8,64,512]{2,1,0:T(8,128)(2,1)}, bf16[8,64,512]{2,1,0:T(8,128)(2,1)}, u32[]{:S(2)}, u32[]{:S(2)}) collective-permute-start(bf16[8,64,512]{2,1,0:T(8,128)(2,1)} %get-tuple-element.271), channel_id=1, source_target_pairs={{0,4},{2,6},{4,0},{6,2},{8,12},{10,14},{12,8},{14,10},{16,20},{18,... | collective-permute-start | bytes 1572872 | tf_op jit(solution)/shard_map/ppermute | solution.py:843
  324.0 12.7 %collective-permute-start.35 = (bf16[4,256,256]{2,1,0:T(8,128)(2,1)S(1)}, bf16[4,256,256]{2,1,0:T(8,128)(2,1)S(1)}, u32[]{:S(2)}, u32[]{:S(2)}) collective-permute-start(bf16[4,256,256]{2,1,0:T(8,128)(2,1)S(1)} %copy-done.38), channel_id=1, source_target_pairs={{0,1},{1,0},{2,3},{3,2},{4,5},{5,4},{6,7},{7,6},{8,9},{9,8},{10,11... | collective-permute-start | bytes 1572872 | tf_op jit(solution)/shard_map/ppermute | solution.py:843
  331.6 17.1 %collective-permute-start.38 = (bf16[4,64,512]{2,1,0:T(8,128)(2,1)}, bf16[4,64,512]{2,1,0:T(8,128)(2,1)}, u32[]{:S(2)}, u32[]{:S(2)}) collective-permute-start(bf16[4,64,512]{2,1,0:T(8,128)(2,1)} %get-tuple-element.276), channel_id=1, source_target_pairs={{0,16},{2,18},{4,20},{6,22},{8,24},{10,26},{12,28},{14,30},{16,0},... | collective-permute-start | bytes 786440 | tf_op jit(solution)/shard_map/ppermute | solution.py:843
  333.3 43.7 %collective-permute-start.40 = (bf16[8,256,256]{2,1,0:T(8,128)(2,1)}, bf16[8,256,256]{2,1,0:T(8,128)(2,1)}, u32[]{:S(2)}, u32[]{:S(2)}) collective-permute-start(bf16[8,256,256]{2,1,0:T(8,128)(2,1)} %get-tuple-element.274), channel_id=1, source_target_pairs={{0,8},{2,10},{4,12},{6,14},{8,0},{10,2},{12,4},{14,6},{16,24},{18,... | collective-permute-start | bytes 3145736 | tf_op jit(solution)/shard_map/ppermute | solution.py:843
  348.8 30.9 %collective-permute-start.41 = (bf16[4,64,256]{2,1,0:T(8,128)(2,1)}, bf16[4,64,256]{2,1,0:T(8,128)(2,1)}, u32[]{:S(2)}, u32[]{:S(2)}) collective-permute-start(bf16[4,64,256]{2,1,0:T(8,128)(2,1)} %get-tuple-element.289), channel_id=1, source_target_pairs={{0,16},{2,18},{4,20},{6,22},{8,24},{10,26},{12,28},{14,30},{16,0},... | collective-permute-start | bytes 393224 | tf_op jit(solution)/shard_map/ppermute | solution.py:843
  350.6 33.7 %collective-permute-start.43 = (bf16[4,64,512]{2,1,0:T(8,128)(2,1)}, bf16[4,64,512]{2,1,0:T(8,128)(2,1)}, u32[]{:S(2)}, u32[]{:S(2)}) collective-permute-start(bf16[4,64,512]{2,1,0:T(8,128)(2,1)} %combine.33.refs_0_), channel_id=1, source_target_pairs={{0,16},{2,18},{4,20},{6,22},{8,24},{10,26},{12,28},{14,30},{16,0},... | collective-permute-start | bytes 786440 | tf_op jit(solution)/shard_map/ppermute | solution.py:843
  356.0 25.7 %collective-permute-start.42 = (bf16[4,64,512]{2,1,0:T(8,128)(2,1)}, bf16[4,64,512]{2,1,0:T(8,128)(2,1)S(1)}, u32[]{:S(2)}, u32[]{:S(2)}) collective-permute-start(bf16[4,64,512]{2,1,0:T(8,128)(2,1)} %combine.34.refs_0_), channel_id=1, source_target_pairs={{0,4},{2,6},{4,0},{6,2},{8,12},{10,14},{12,8},{14,10},{16,20},{18,... | collective-permute-start | bytes 786440 | tf_op jit(solution)/shard_map/ppermute | solution.py:843
  381.3 14.3 %collective-permute-start.45 = (bf16[8,128,256]{2,1,0:T(8,128)(2,1)}, bf16[8,128,256]{2,1,0:T(8,128)(2,1)}, u32[]{:S(2)}, u32[]{:S(2)}) collective-permute-start(bf16[8,128,256]{2,1,0:T(8,128)(2,1)} %get-tuple-element.295), channel_id=1, source_target_pairs={{0,4},{2,6},{4,0},{6,2},{8,12},{10,14},{12,8},{14,10},{16,20},{18,... | collective-permute-start | bytes 1572872 | tf_op jit(solution)/shard_map/ppermute | solution.py:843
  386.1 25.4 %collective-permute-start.47 = (bf16[4,128,512]{2,1,0:T(8,128)(2,1)}, bf16[4,128,512]{2,1,0:T(8,128)(2,1)}, u32[]{:S(2)}, u32[]{:S(2)}) collective-permute-start(bf16[4,128,512]{2,1,0:T(8,128)(2,1)} %join_rows.13.refs_0_), channel_id=1, source_target_pairs={{0,8},{2,10},{4,12},{6,14},{8,0},{10,2},{12,4},{14,6},{16,24},{18,... | collective-permute-start | bytes 1572872 | tf_op jit(solution)/shard_map/ppermute | solution.py:843
  386.9 32.3 %collective-permute-start.49 = (bf16[4,128,512]{2,1,0:T(8,128)(2,1)}, bf16[4,128,512]{2,1,0:T(8,128)(2,1)}, u32[]{:S(2)}, u32[]{:S(2)}) collective-permute-start(bf16[4,128,512]{2,1,0:T(8,128)(2,1)} %join_rows.12.refs_0_), channel_id=1, source_target_pairs={{0,16},{2,18},{4,20},{6,22},{8,24},{10,26},{12,28},{14,30},{16,0},... | collective-permute-start | bytes 1572872 | tf_op jit(solution)/shard_map/ppermute | solution.py:843
  402.3 28.2 %collective-permute-start.50 = (bf16[4,256,256]{2,1,0:T(8,128)(2,1)}, bf16[4,256,256]{2,1,0:T(8,128)(2,1)}, u32[]{:S(2)}, u32[]{:S(2)}) collective-permute-start(bf16[4,256,256]{2,1,0:T(8,128)(2,1)} %join_rows.15.refs_0_), channel_id=1, source_target_pairs={{0,8},{2,10},{4,12},{6,14},{8,0},{10,2},{12,4},{14,6},{16,24},{18,... | collective-permute-start | bytes 1572872 | tf_op jit(solution)/shard_map/ppermute | solution.py:843
  403.2 12.4 %collective-permute-start.48 = (bf16[4,128,256]{2,1,0:T(8,128)(2,1)S(1)}, bf16[4,128,256]{2,1,0:T(8,128)(2,1)S(1)}, u32[]{:S(2)}, u32[]{:S(2)}) collective-permute-start(bf16[4,128,256]{2,1,0:T(8,128)(2,1)S(1)} %copy-done.44), channel_id=1, source_target_pairs={{0,1},{1,0},{2,3},{3,2},{4,5},{5,4},{6,7},{7,6},{8,9},{9,8},{10,11... | collective-permute-start | bytes 786440 | tf_op jit(solution)/shard_map/ppermute | solution.py:843
  413.8 24.4 %collective-permute-start.53 = (bf16[4,256,512]{2,1,0:T(8,128)(2,1)}, bf16[4,256,512]{2,1,0:T(8,128)(2,1)}, u32[]{:S(2)}, u32[]{:S(2)}) collective-permute-start(bf16[4,256,512]{2,1,0:T(8,128)(2,1)} %join_rows.16.refs_0_), channel_id=1, source_target_pairs={{0,4},{2,6},{4,0},{6,2},{8,12},{10,14},{12,8},{14,10},{16,20},{18,... | collective-permute-start | bytes 3145736 | tf_op jit(solution)/shard_map/ppermute | solution.py:843
  421.5 30.3 %collective-permute-start.56 = (bf16[4,256,512]{2,1,0:T(8,128)(2,1)}, bf16[4,256,512]{2,1,0:T(8,128)(2,1)}, u32[]{:S(2)}, u32[]{:S(2)}) collective-permute-start(bf16[4,256,512]{2,1,0:T(8,128)(2,1)} %join_rows.17.refs_0_), channel_id=1, source_target_pairs={{0,8},{2,10},{4,12},{6,14},{8,0},{10,2},{12,4},{14,6},{16,24},{18,... | collective-permute-start | bytes 3145736 | tf_op jit(solution)/shard_map/ppermute | solution.py:843
  427.2 20.4 %collective-permute-start.54 = (bf16[4,64,256]{2,1,0:T(8,128)(2,1)}, bf16[4,64,256]{2,1,0:T(8,128)(2,1)S(1)}, u32[]{:S(2)}, u32[]{:S(2)}) collective-permute-start(bf16[4,64,256]{2,1,0:T(8,128)(2,1)} %combine.39.refs_0_), channel_id=1, source_target_pairs={{0,16},{2,18},{4,20},{6,22},{8,24},{10,26},{12,28},{14,30},{16,0},... | collective-permute-start | bytes 393224 | tf_op jit(solution)/shard_map/ppermute | solution.py:843
  441.2 13.6 %collective-permute-start.55 = (bf16[4,512,512]{2,1,0:T(8,128)(2,1)}, bf16[4,512,512]{2,1,0:T(8,128)(2,1)S(1)}, u32[]{:S(2)}, u32[]{:S(2)}) collective-permute-start(bf16[4,512,512]{2,1,0:T(8,128)(2,1)} %join_rows.19.refs_2_), channel_id=1, source_target_pairs={{0,2},{2,0},{4,6},{6,4},{8,10},{10,8},{12,14},{14,12},{16,18},{18,... | collective-permute-start | bytes 6291464 | tf_op jit(solution)/shard_map/ppermute | solution.py:843
  459.2 15.4 %collective-permute-start.59 = (bf16[4,256,256]{2,1,0:T(8,128)(2,1)}, bf16[4,256,256]{2,1,0:T(8,128)(2,1)}, u32[]{:S(2)}, u32[]{:S(2)}) collective-permute-start(bf16[4,256,256]{2,1,0:T(8,128)(2,1)} %join_rows.22.refs_0_), channel_id=1, source_target_pairs={{0,8},{2,10},{4,12},{6,14},{8,0},{10,2},{12,4},{14,6},{16,24},{18,... | collective-permute-start | bytes 1572872 | tf_op jit(solution)/shard_map/ppermute | solution.py:843
  (66 other events, 671.2 us)
Sparse Core Ops, SparseCore 0:
  302.2 63.0 all-gather.2

commit v4 on v3

--- a/solution.py
+++ b/solution.py
@@ -273,7 +273,7 @@
 
 
 LARGE = 58 * 2**20
-SPEED = 30 * 1.1e9
+SPEED = 400 * 1.1e9
 HEAVY = 1
 UNITS = 512
 GROUP = 256
@@ -382,16 +382,17 @@
     return list(quarters) * (4 // len(quarters))
 
 
-def heads_kernel(order_ref, w0_ref, w1_ref, w2_ref, w3_ref, x_ref, b_ref, *refs):
+def heads_kernel(order_ref, w0_ref, w1_ref, w2_ref, w3_ref, x_ref, bq_ref, bv_ref, *refs):
     three_ref, o_ref, lse_ref, weight = refs[-4:]
 
     @pl.when(pl.program_id(0) == 0)
     def _():
         gather_depth(order_ref, (w0_ref, w1_ref, w2_ref, w3_ref), weight, False)
 
-    scaled = matmul(x_ref[...], weight[...]) + b_ref[...]
-    three_ref[:, :GROUP] = (scaled[:, :GROUP] * 0.125).astype(LOW)
-    three_ref[:, GROUP:] = scaled[:, GROUP:].astype(LOW)
+    product = matmul(x_ref[...], weight[...])
+    three_ref[:, :GROUP] = ((product[:, :GROUP] + bq_ref[...]) * 0.125).astype(LOW)
+    three_ref[:, GROUP : 2 * GROUP] = product[:, GROUP : 2 * GROUP].astype(LOW)
+    three_ref[:, 2 * GROUP :] = (product[:, 2 * GROUP :] + bv_ref[...]).astype(LOW)
     for pair in range(GROUP // LANES):
         queries, key_rows, values = (three_ref[:, entry] for entry in spans(pair))
         values_t = values.T
@@ -421,7 +422,11 @@
         grid=(pages,),
         in_specs=[scalar_spec()]
         + qkv_specs(quarters, part)
-        + [pl.BlockSpec((PAGE, depth), lambda page: (page, 0)), held((1, width))]
+        + [
+            pl.BlockSpec((PAGE, depth), lambda page: (page, 0)),
+            pl.BlockSpec((1, GROUP), lambda page: (0, part)),
+            pl.BlockSpec((1, GROUP), lambda page: (0, parts + part)),
+        ]
         + [pl.BlockSpec(memory_space=pl.ANY)] * len(before),
         out_specs=[
             pl.BlockSpec((PAGE, width), lambda page: (page, part)),
@@ -434,11 +439,11 @@
             shaped(parts, pages, count, PAGE),
         ],
         scratch_shapes=[pltpu.VMEM((depth, width), LOW)],
-        input_output_aliases={7 + number: number for number in range(len(before))},
+        input_output_aliases={8 + number: number for number in range(len(before))},
         compiler_params=pltpu.CompilerParams(vmem_limit_bytes=LARGE),
         cost_estimate=cost_of("heads"),
         name="heads",
-    )(order, *four_times(quarters), x_low, bias, *before)
+    )(order, *four_times(quarters), x_low, bias, bias, *before)
 
 
 def heads_back_kernel(core_ref, order_ref, x_ref, g_ref, before_ref, *refs):
@@ -631,7 +636,8 @@
 
 def units_forward(order, hidden_low, up, bias, down):
     rows, depth = hidden_low.shape
-    units = bias.shape[1]
+    units = down[0].shape[1]
+    skip = (bias.shape[1] - units) // UNITS
     half = depth // 2
     column = pl.BlockSpec((rows, UNITS), lambda step: (0, step))
     return run(
@@ -640,7 +646,7 @@
         (units // UNITS,),
         [scalar_spec(), held((rows, depth))]
         + pair_specs(up, (half, UNITS), 1)
-        + [pl.BlockSpec((1, UNITS), lambda step: (0, step))]
+        + [pl.BlockSpec((1, UNITS), lambda step: (0, step + skip))]
         + pair_specs(down, (UNITS, half), 2),
         [column, column, held((rows, depth))],
         [shaped(rows, units, kind=LOW), shaped(rows, units, kind=LOW), shaped(rows, depth)],
@@ -968,7 +974,8 @@
 
     def last(self):
         self.beside = self.clock.hold(self.beside)
-        self.clock.tick(self.beside)
+        self.core_piece = self.clock.hold(self.core_piece)
+        self.clock.tick(self.beside, self.core_piece)
         self.parts = (self.piece, self.beside, self.core_piece, swap(self.beside, 1))
 
 
@@ -1051,16 +1058,19 @@
     )
 
 
-def join_rows(words, entries, distance):
+def join_rows(words, entries, steps):
     ways = len(entries)
+    outer = steps[1] if ways == 2 else 4
     count, size, columns = entries[0].shape
     shape = (count, ways * size, columns)
 
     def kernel(word_ref, *refs):
         target = refs[-1]
-        place = (word_ref[0] // distance) % 2
-        for relative, ref in enumerate(refs[:-1]):
-            target[:, pl.ds(pl.multiple_of((place ^ relative) * size, size), size), :] = ref[...]
+        for step, ref in zip(steps, refs[:-1]):
+            place = ((word_ref[0] ^ step) // outer) % 2
+            if ways == 4:
+                place = place * 2 + ((word_ref[0] ^ step) // 8) % 2
+            target[:, pl.ds(pl.multiple_of(place * size, size), size), :] = ref[...]
 
     return run(
         kernel,
@@ -1074,10 +1084,13 @@
 
 
 class Piece:
-    def __init__(self, clock, words, order, source, count):
+    def __init__(self, clock, words, order, source, count, direct):
         self.clock, self.words = clock, words
         self.order = list(order)
-        self.back = [ways for ways in reversed(order) if ways != "x"]
+        self.back = [(ways,) for ways in reversed(order) if ways != "x"]
+        if direct:
+            at = self.back.index((8,))
+            self.back[at : at + 2] = [(8, 4, 12)]
         self.source = source
         self.count = count
         self.flight = None
@@ -1101,7 +1114,8 @@
             self.gather()
 
     def gather(self):
-        self.flight = [swap(self.total, self.back[0] if self.back else 1)]
+        steps = self.back[0] if self.back else (1,)
+        self.flight = [swap(self.total, distance) for distance in steps]
 
     def step(self):
         if self.flight is None:
@@ -1120,9 +1134,9 @@
             self.clock.tick(self.flight[0])
             self.complete = True
             return
-        distance = self.back.pop(0)
+        steps = (0,) + self.back.pop(0)
         entries = [self.clock.hold(self.total)] + self.flight
-        self.total = join_rows(self.words, entries, distance)
+        self.total = join_rows(self.words, entries, steps)
         self.clock.tick(self.total)
         self.gather()
 
@@ -1196,14 +1210,16 @@
     )
 
 
+DIRECT = ""
 MLP_ORDERS = ((4, 8, 2, "x"), ("x", 2, 4, 8))
 HEAD_ORDERS = ((4, "x", 2, 8), (4, 2, "x", 8))
 FORWARD = (
     ("own", 0),
     "a",
     ("own", 1),
+    "a",
+    "biases",
     "b",
-    "a",
     "out",
     "up",
     ("other", 0),
@@ -1310,8 +1326,8 @@
     fetch["out"] = FetchQuarters(clock, pieces_now[0])
     fetch["up"] = FetchHalves(clock, words, pieces_now[1], 1)
     fetch["down"] = FetchHalves(clock, words, pieces_now[2], 2)
-    biases = jnp.concatenate([qv_bias[0].reshape(-1), up_bias[0]])
-    biases = {"own": biases, "other": swap(biases, 1, "mp")}
+    biases = jnp.concatenate([qv_bias[:, 0], qv_bias[:, 1], up_bias], 1)
+    biases = {"own": biases}
     gains, shifts = norm_gain[0], norm_shift[0]
     saved = {"own": (), "other": ()}
     qkv_w = {("own", part): (qkv_weight,) for part in range(parts)}
@@ -1319,18 +1335,14 @@
     units = {}
 
     def run_heads(side, part):
-        values = biases[side] if side == "own" else clock.hold(biases[side])
-        span = slice(part * GROUP, (part + 1) * GROUP)
-        bias = jnp.concatenate(
-            [values[:width][span], jnp.zeros((GROUP,), F32), values[width : 2 * width][span]]
-        )
+        bias = biases[side] if side == "own" else clock.hold(biases[side])
         if side == "other":
             qkv_w[side, part] = fetch["ab"[part]].parts
         saved[side] = heads_forward(
             quarter_order[side],
             qkv_w[side, part],
             clock.hold(inputs),
-            bias[None],
+            bias,
             part,
             parts,
             saved[side],
@@ -1338,14 +1350,16 @@
         clock.tick(saved[side][1])
 
     def run_units(side):
-        bias = up_bias if side == "own" else clock.hold(biases[side])[None, 2 * width :]
+        bias = biases[side] if side == "own" else clock.hold(biases[side])
         units[side] = units_forward(
             half_order[side], clock.hold(hidden_low), up_w[side], bias, down_w[side]
         )
         clock.tick(units[side][2])
 
     for action in FORWARD:
-        if action == "project":
+        if action == "biases":
+            biases["other"] = swap(clock.hold(biases["own"]), 1, "mp")
+        elif action == "project":
             out_w["other"] = fetch["out"].parts
             pre_first, hidden, hidden_low = project(
                 quarter_word,
@@ -1433,11 +1447,14 @@
         state["every"], state["split"] = every, split[0].shape[0]
 
     def add_small():
-        every = clock.hold(state["every"]).reshape(lax.axis_size("dp"), 2, -1)
+        every = clock.hold(state["every"])
         split_width = state["split"]
-        same = jnp.sum(every, axis=0)
-        straight = same[0, :split_width] + same[1, split_width : 2 * split_width]
-        turned = same[1, :split_width] + same[0, split_width : 2 * split_width]
+        odd = (lax.broadcasted_iota(jnp.int32, (every.shape[0], 1), 0) % 2) == 1
+        same = [
+            jnp.sum(jnp.where(odd == (number == 1), every, 0.0), axis=0) for number in range(2)
+        ]
+        straight = same[0][:split_width] + same[1][split_width : 2 * split_width]
+        turned = same[1][:split_width] + same[0][split_width : 2 * split_width]
         split_sum = jnp.where(lax.axis_index("mp") == 0, straight, turned)
         shared = (same[0] + same[1])[2 * split_width :].reshape(6, -1)
         clock.tick(split_sum, shared)
@@ -1458,7 +1475,7 @@
             def source(side):
                 return [(keep[key], side), (received[key], side)]
 
-            pieces[key] = Piece(clock, words, orders[number], source, 4)
+            pieces[key] = Piece(clock, words, orders[number], source, 4, kind in DIRECT)
         pieces[key].step()
         both = [pieces.get((kind, other)) for other in range(2)]
         if kind not in outcome and all(piece and piece.complete for piece in both):

time: 504 us -> 498 us (0.988)
  the two profiles are of different devices: /device:TPU:0 before, /device:TPU:19 now
where the time goes in v4:
time: 498 us; the launch traced here: 488 us
  Pallas kernels  305 us (61%)
  waiting for transfers between devices  84.5 us (17%)
  starting transfers between devices  64.4 us (13%)
  local copies, waits for them, and re-layouts  16.6 us (3%)
  between operations  15.1 us (3%)
    pallas_call x47, Pallas kernels, run(): pl.pallas_call(kernel, grid=grid, in_specs=in_specs, out_specs=out_specs,...  266 us
    ppermute x61, waiting for transfers between devices, swap(): lax.ppermute(value, axis, [(place, place ^ distance) for place in range(c...  67.5 us
    ppermute x61, starting transfers between devices, swap(): lax.ppermute(value, axis, [(place, place ^ distance) for place in range(c...  64.4 us
    pallas_call x4, Pallas kernels, heads_forward(): pl.pallas_call(heads_kernel, grid=(pages,), in_specs=[scalar_spec()] + qk...  32.8 us
    all_gather x1, waiting for transfers between devices, gather_small(): lax.all_gather(jnp.concatenate(split + [entry[0] for entry in sums]), ('d...  16.9 us
  transfers between devices with their start and end apart: 62, of which 18 were waited for; matrix products, arithmetic and copies ran while one was open for 3% of the time, Pallas kernels for 50%

profile of v4, /device:TPU:19, one launch (start us, length us, event | category | flops | bytes accessed | tf_op | source)
XLA Modules:
  0.0 488.3 jit_solution(10778197636289625486)
XLA Ops:
  7.8 2.7 take_blocks.2
  12.0 3.2 take_blocks.3
  16.1 8.2 %heads.4 = (bf16[832,1536]{1,0:T(8,128)(2,1)}, bf16[832,512]{1,0:T(8,128)(2,1)}, f32[2,2,4,416]{3,2,1,0:T(4,128)}) custom-call(s32[1]{0:T(128)} %constant.12.clone.1.order_ref, bf16[1,3,1024,512]{3,2,1,0:T(8,128)(2,1)} %refs_6_.3, bf16[1,3,1024,512]{3,2,1,0:T(8,128)(2,1)} %refs_6_.3, bf16[1,3,1024,512]{3,2,1,0:T(8,128)(2,1)} %refs_6_.3, ...), custom_call_target="tpu_custom_call" | custom-call | flops 3519999901696 | bytes 1 | tf_op jit(solution)/shard_map/heads/pallas_call | solution.py:420
  27.1 8.3 %heads.5 = (bf16[832,1536]{1,0:T(8,128)(2,1)}, bf16[832,512]{1,0:T(8,128)(2,1)}, f32[2,2,4,416]{3,2,1,0:T(4,128)}) custom-call(s32[1]{0:T(128)} %constant.12.clone.1.order_ref, bf16[1,3,1024,512]{3,2,1,0:T(8,128)(2,1)} %refs_6_.3, bf16[1,3,1024,512]{3,2,1,0:T(8,128)(2,1)} %refs_6_.3, ...), custom_call_target="tpu_custom_call", output_to_operand_aliasing={{0}: (8, {}), {1}: (9, {}), {2}: (10, {})} | custom-call | flops 3519999901696 | bytes 1 | tf_op jit(solution)/shard_map/heads/pallas_call | solution.py:420
  40.4 5.7 %collective-permute-done.7.w0.refs_18_ = bf16[1,512,256]{2,1,0:T(8,128)(2,1)S(1)} collective-permute-done((bf16[1,512,256]{2,1,0:T(8,128)(2,1)S(1)}, bf16[1,512,256]{2,1,0:T(8,128)(2,1)S(1)}, u32[]{:S(2)}, u32[]{:S(2)}) %collective-permute-start.7) | collective-permute-done | bytes 262176 | tf_op jit(solution)/shard_map/ppermute | solution.py:849
  51.3 8.2 %heads.6 = (bf16[832,1536]{1,0:T(8,128)(2,1)}, bf16[832,512]{1,0:T(8,128)(2,1)}, f32[2,2,4,416]{3,2,1,0:T(4,128)}) custom-call(s32[1]{0:T(128)} %bitcast.order_ref, bf16[1,3,256,256]{3,2,1,0:T(8,128)(2,1)} %collective-permute-done.w0_ref.refs_14_, bf16[1,3,256,256]{3,2,1,0:T(8,128)(2,1)} %collective-permute-done.2.w1_ref.refs_15_, ...), custom_call_target="tpu_custom_call" | custom-call | flops 3519999901696 | bytes 1 | tf_op jit(solution)/shard_map/heads/pallas_call | solution.py:420
  63.9 4.1 collective-permute-done.12.w1.refs_19_
  72.9 8.2 %heads.7 = (bf16[832,1536]{1,0:T(8,128)(2,1)}, bf16[832,512]{1,0:T(8,128)(2,1)}, f32[2,2,4,416]{3,2,1,0:T(4,128)}) custom-call(s32[1]{0:T(128)} %bitcast.order_ref, bf16[1,3,256,256]{3,2,1,0:T(8,128)(2,1)} %collective-permute-done.1.w0_ref.refs_14_, ...), custom_call_target="tpu_custom_call", output_to_operand_aliasing={{0}: (8, {}), {1}: (9, {}), {2}: (10, {})} | custom-call | flops 3519999901696 | bytes 1 | tf_op jit(solution)/shard_map/heads/pallas_call | solution.py:420
  84.0 7.6 %project.1 = (f32[832,1024]{1,0:T(8,128)}, f32[832,1024]{1,0:T(8,128)}, bf16[832,1024]{1,0:T(8,128)(2,1)}) custom-call(s32[1]{0:T(128)} %bitcast.order_ref, bf16[832,512]{1,0:T(8,128)(2,1)} %get-tuple-element.189.a_ref.refs_2_, bf16[832,512]{1,0:T(8,128)(2,1)} %get-tuple-element.211.b_ref.refs_13_, bf16[1,512,1024]{2,1,0:T(8,128)(2,1)} %refs_10_.3, ...), custom_call_target="tpu_custom_call" | custom-call | flops 3080000110592 | bytes 1 | tf_op jit(solution)/shard_map/project/pallas_call | solution.py:334
  96.0 3.0 join_depth.2.up_a.refs_8_
  100.8 14.4 %units.2 = (bf16[832,2048]{1,0:T(8,128)(2,1)}, bf16[832,2048]{1,0:T(8,128)(2,1)}, f32[832,1024]{1,0:T(8,128)}) custom-call(s32[1]{0:T(128)} %constant.12.clone.1.order_ref, bf16[832,1024]{1,0:T(8,128)(2,1)} %get-tuple-element.224.h_ref, bf16[1,1024,2048]{2,1,0:T(8,128)(2,1)} %refs_3_.5, bf16[1,1024,2048]{2,1,0:T(8,128)(2,1)} %refs_3_.5, ...), custom_call_target="tpu_custom_call" | custom-call | flops 6160000221184 | bytes 1 | tf_op jit(solution)/shard_map/units/pallas_call | solution.py:334
  115.3 3.3 join_depth.3.down_a.refs_10_
  119.1 3.8 collective-permute-done.24.down_b.refs_11_
  124.2 14.1 %units.3 = (bf16[832,2048]{1,0:T(8,128)(2,1)}, bf16[832,2048]{1,0:T(8,128)(2,1)}, f32[832,1024]{1,0:T(8,128)}) custom-call(s32[1]{0:T(128)} %bitcast.3.order_ref.core_ref, bf16[832,1024]{1,0:T(8,128)(2,1)} %get-tuple-element.224.h_ref, bf16[1,512,2048]{2,1,0:T(8,128)(2,1)} %join_depth.2.up_a.refs_8_, ...), custom_call_target="tpu_custom_call" | custom-call | flops 6160000221184 | bytes 1 | tf_op jit(solution)/shard_map/units/pallas_call | solution.py:334
  138.4 8.7 %turn.1 = (f32[832,1024]{1,0:T(8,128)}, f32[832,1024]{1,0:T(8,128)}, bf16[832,1024]{1,0:T(8,128)(2,1)}, f32[1,1024]{1,0:T(1,128)}, f32[1,1024]{1,0:T(1,128)}, /*index=5*/f32[1,1024]{1,0:T(1,128)}) custom-call(f32[832,1024]{1,0:T(8,128)} %get-tuple-element.222.a_ref, f32[832,1024]{1,0:T(8,128)} %get-tuple-element.226.b_ref, ...), custom_call_target="tpu_custom_call" | custom-call | flops 3959999954944 | bytes 1 | tf_op jit(solution)/shard_map/turn/pallas_call | solution.py:334
  147.1 24.5 %units_back.2 = (bf16[8,512,512]{2,1,0:T(8,128)(2,1)}, bf16[8,512,512]{2,1,0:T(8,128)(2,1)}, f32[832,1024]{1,0:T(8,128)}, f32[4,1,512]{2,1,0:T(1,128)}) custom-call(s32[1]{0:T(128)} %bitcast.3.order_ref.core_ref, s32[1]{0:T(128)} %bitcast.3.order_ref.core_ref, bf16[832,1024]{1,0:T(8,128)(2,1)} %get-tuple-element.236.g_ref, ...), custom_call_target="tpu_custom_call" | custom-call | flops 9679999598592 | bytes 1 | tf_op jit(solution)/shard_map/units_back/pallas_call | solution.py:334
  171.7 24.1 %units_back.3 = (bf16[8,512,512]{2,1,0:T(8,128)(2,1)}, bf16[8,512,512]{2,1,0:T(8,128)(2,1)}, f32[832,1024]{1,0:T(8,128)}, f32[4,1,512]{2,1,0:T(1,128)}) custom-call(s32[1]{0:T(128)} %bitcast.3.order_ref.core_ref, s32[1]{0:T(128)} %bitcast.3.order_ref.core_ref, bf16[832,1024]{1,0:T(8,128)(2,1)} %get-tuple-element.236.g_ref, ...), custom_call_target="tpu_custom_call" | custom-call | flops 9679999598592 | bytes 1 | tf_op jit(solution)/shard_map/units_back/pallas_call | solution.py:334
  198.2 6.4 %combine.20 = (bf16[8,256,512]{2,1,0:T(8,128)(2,1)}, bf16[4,256,512]{2,1,0:T(8,128)(2,1)}, bf16[4,256,512]{2,1,0:T(8,128)(2,1)}) custom-call(s32[4]{0:T(128)} %pad_add_fusion.word_ref, bf16[8,512,512]{2,1,0:T(8,128)(2,1)} %get-tuple-element.241.refs_0_.refs_2_, bf16[8,512,512]{2,1,0:T(8,128)(2,1)} %collective-permute-done.25.refs_1_.refs_3_, ...), custom_call_target="tpu_custom_call" | custom-call | flops 879999975424 | bytes 1 | tf_op jit(solution)/shard_map/combine/pallas_call | solution.py:334
  205.6 4.1 combine.21
  209.7 8.6 %first_back.1 = (f32[832,1024]{1,0:T(8,128)}, bf16[832,1024]{1,0:T(8,128)(2,1)}, f32[1,1024]{1,0:T(1,128)}, f32[1,1024]{1,0:T(1,128)}, f32[1,1024]{1,0:T(1,128)}) custom-call(f32[832,1024]{1,0:T(8,128)} %get-tuple-element.235.refs_0_, f32[832,1024]{1,0:T(8,128)} %get-tuple-element.237.refs_1_, f32[832,1024]{1,0:T(8,128)} %get-tuple-element.246.refs_2_, ...), custom_call_target="tpu_custom_call" | custom-call | flops 4400000008192 | bytes 1 | tf_op jit(solution)/shard_map/first_back/pallas_call | solution.py:334
  218.3 27.5 %heads_back.2 = (bf16[8,512,256]{2,1,0:T(8,128)(2,1)}, bf16[8,512,256]{2,1,0:T(8,128)(2,1)}, f32[832,1024]{1,0:T(8,128)}, f32[2,1,768]{2,1,0:T(1,128)}) custom-call(s32[1]{0:T(128)} %bitcast.3.order_ref.core_ref, s32[1]{0:T(128)} %bitcast.order_ref, bf16[832,1024]{1,0:T(8,128)(2,1)} %x_ref.8, bf16[832,1024]{1,0:T(8,128)(2,1)} %get-tuple-element.266.g_ref, ...), custom_call_target="tpu_custom_call" | custom-call | flops 11439999811584 | bytes 1 | tf_op jit(solution)/shard_map/heads_back/pallas_call | solution.py:334
  248.9 3.1 collective-permute-done.27.refs_1_.refs_3_
  252.0 4.0 combine.22
  256.0 3.9 combine.23
  259.9 4.9 %combine.24 = (bf16[4,256,512]{2,1,0:T(8,128)(2,1)}, bf16[4,256,512]{2,1,0:T(8,128)(2,1)}) custom-call(s32[4]{0:T(128)} %pad_add_fusion.word_ref, bf16[8,512,512]{2,1,0:T(8,128)(2,1)} %get-tuple-element.264.refs_0_, bf16[8,512,512]{2,1,0:T(8,128)(2,1)} %collective-permute-done.26.refs_1_, bf16[4,512,512]{2,1,0:T(8,128)(2,1)} %collective-permute-done.29.refs_2_), custom_call_target="tpu_custom_call" | custom-call | flops 879999975424 | bytes 1 | tf_op jit(solution)/shard_map/combine/pallas_call | solution.py:334
  267.3 27.8 %heads_back.3 = (bf16[8,512,256]{2,1,0:T(8,128)(2,1)}, bf16[8,512,256]{2,1,0:T(8,128)(2,1)}, f32[832,1024]{1,0:T(8,128)}, f32[2,1,768]{2,1,0:T(1,128)}) custom-call(s32[1]{0:T(128)} %bitcast.3.order_ref.core_ref, s32[1]{0:T(128)} %bitcast.order_ref, bf16[832,1024]{1,0:T(8,128)(2,1)} %x_ref.8, bf16[832,1024]{1,0:T(8,128)(2,1)} %get-tuple-element.266.g_ref, ...), custom_call_target="tpu_custom_call" | custom-call | flops 11439999811584 | bytes 1 | tf_op jit(solution)/shard_map/heads_back/pallas_call | solution.py:334
  298.7 2.7 combine.25
  301.4 9.7 %collective-permute-done.31.refs_1_.refs_3_ = bf16[8,256,256]{2,1,0:T(8,128)(2,1)} collective-permute-done((bf16[8,256,256]{2,1,0:T(8,128)(2,1)}, bf16[8,256,256]{2,1,0:T(8,128)(2,1)}, u32[]{:S(2)}, u32[]{:S(2)}) %collective-permute-start.31) | collective-permute-done | bytes 1048608 | tf_op jit(solution)/shard_map/ppermute | solution.py:849
  313.8 2.7 combine.27
  316.5 3.9 combine.28
  320.4 3.8 collective-permute-done.34.refs_1_
  332.6 3.8 collective-permute-done.37.refs_1_
  346.7 16.9 %all-gather.3.cloned.1.call-done = f32[393216]{0:T(1024)} async-done(((f32[12288]{0:T(1024)}), f32[393216]{0:T(1024)}) %all-gather.3.cloned.1.call-update) | async-done | bytes 1572880 | tf_op jit(solution)/shard_map/all_gather | solution.py:1444
  363.7 2.6 reshape.125
  366.3 3.1 collective-permute-done.40.refs_1_.refs_3_
  369.4 2.7 combine.35
  388.2 4.3 collective-permute-done.46.refs_1_
  395.4 8.2 %collective-permute-done.47.refs_1_ = bf16[4,128,512]{2,1,0:T(8,128)(2,1)} collective-permute-done((bf16[4,128,512]{2,1,0:T(8,128)(2,1)}, bf16[4,128,512]{2,1,0:T(8,128)(2,1)}, u32[]{:S(2)}, u32[]{:S(2)}) %collective-permute-start.47) | collective-permute-done | bytes 524320 | tf_op jit(solution)/shard_map/ppermute | solution.py:849
  412.1 5.4 %collective-permute-done.50.refs_1_ = bf16[4,256,256]{2,1,0:T(8,128)(2,1)} collective-permute-done((bf16[4,256,256]{2,1,0:T(8,128)(2,1)}, bf16[4,256,256]{2,1,0:T(8,128)(2,1)}, u32[]{:S(2)}, u32[]{:S(2)}) %collective-permute-start.50) | collective-permute-done | bytes 524320 | tf_op jit(solution)/shard_map/ppermute | solution.py:849
  419.9 3.1 collective-permute-start.52
  428.9 3.0 join_rows.19.refs_2_
  431.9 2.9 collective-permute-start.55
  434.7 7.3 %collective-permute-done.54.refs_1_ = bf16[4,64,256]{2,1,0:T(8,128)(2,1)} collective-permute-done((bf16[4,64,256]{2,1,0:T(8,128)(2,1)}, bf16[4,64,256]{2,1,0:T(8,128)(2,1)}, u32[]{:S(2)}, u32[]{:S(2)}) %collective-permute-start.54) | collective-permute-done | bytes 131104 | tf_op jit(solution)/shard_map/ppermute | solution.py:849
  445.1 3.0 join_rows.21.refs_0_
  448.1 4.2 collective-permute-start.58
  456.4 9.8 %finish.2 = (f32[2048,1024]{1,0:T(8,128)}, f32[1024,2048]{1,0:T(8,128)}) custom-call(s32[1]{0:T(128)} %bitcast.3.order_ref.core_ref, bf16[4,512,512]{2,1,0:T(8,128)(2,1)} %join_rows.21.refs_0_, bf16[4,512,512]{2,1,0:T(8,128)(2,1)} %collective-permute-done.58.refs_1_, bf16[4,512,512]{2,1,0:T(8,128)(2,1)} %join_rows.19.refs_2_, ...), custom_call_target="tpu_custom_call" | custom-call | flops 2640000057344 | bytes 1 | tf_op jit(solution)/shard_map/finish/pallas_call | solution.py:334
  468.5 2.6 collective-permute-start.60
  475.2 5.8 %finish.3 = (f32[3,1024,512]{2,1,0:T(8,128)}, f32[512,1024]{1,0:T(8,128)}) custom-call(s32[1]{0:T(128)} %bitcast.3.order_ref.core_ref, bf16[4,512,256]{2,1,0:T(8,128)(2,1)} %join_rows.18.refs_0_, bf16[4,512,256]{2,1,0:T(8,128)(2,1)} %collective-permute-done.52.refs_1_, bf16[4,512,256]{2,1,0:T(8,128)(2,1)} %join_rows.23.refs_2_, bf16[4,512,256]{2,1,0:T(8,128)(2,1)} %copy-done.30), custom_call_target="tpu_custom_call" | custom-call | flops 2640000057344 | bytes 1 | tf_op jit(solution)/shard_map/finish/pallas_call | solution.py:334
  (246 shorter events, 119.5 us)
Async XLA Ops:
  7.2 356.5 %all-gather.3.cloned.1.call-start = ((), (), s32[]{:S(2)}) async-start(), calls=%async_computation | async-start | bytes 1622016 | tf_op jit(solution)/shard_map/all_gather | solution.py:1444
  10.5 13.7 %collective-permute-start = (bf16[1,3,256,256]{3,2,1,0:T(8,128)(2,1)}, bf16[1,3,256,256]{3,2,1,0:T(8,128)(2,1)}, u32[]{:S(2)}, u32[]{:S(2)}) collective-permute-start(bf16[1,3,256,256]{3,2,1,0:T(8,128)(2,1)} %get-tuple-element.180), channel_id=1, source_target_pairs={{0,1},{1,0},{2,3},{3,2},{4,5},{5,4},{6,7},{7,6},{8,9},{9,8},{10,11... | collective-permute-start | bytes 1179656 | tf_op jit(solution)/shard_map/ppermute | solution.py:849
  10.8 28.4 %collective-permute-start.1 = (bf16[1,3,256,256]{3,2,1,0:T(8,128)(2,1)}, bf16[1,3,256,256]{3,2,1,0:T(8,128)(2,1)}, u32[]{:S(2)}, u32[]{:S(2)}) collective-permute-start(bf16[1,3,256,256]{3,2,1,0:T(8,128)(2,1)} %get-tuple-element.190), channel_id=1, source_target_pairs={{0,1},{1,0},{2,3},{3,2},{4,5},{5,4},{6,7},{7,6},{8,9},{9,8},{10,11... | collective-permute-start | bytes 1179656 | tf_op jit(solution)/shard_map/ppermute | solution.py:849
  15.2 33.5 %collective-permute-start.6 = (bf16[1,128,2048]{2,1,0:T(8,128)(2,1)}, bf16[1,128,2048]{2,1,0:T(8,128)(2,1)}, u32[]{:S(2)}, u32[]{:S(2)}) collective-permute-start(bf16[1,128,2048]{2,1,0:T(8,128)(2,1)} %get-tuple-element.194), channel_id=1, source_target_pairs={{0,1},{1,0},{2,3},{3,2},{4,5},{5,4},{6,7},{7,6},{8,9},{9,8},{10,11... | collective-permute-start | bytes 1572872 | tf_op jit(solution)/shard_map/ppermute | solution.py:849
  24.2 14.7 %collective-permute-start.3 = (bf16[1,3,256,256]{3,2,1,0:T(8,128)(2,1)}, bf16[1,3,256,256]{3,2,1,0:T(8,128)(2,1)}, u32[]{:S(2)}, u32[]{:S(2)}) collective-permute-start(bf16[1,3,256,256]{3,2,1,0:T(8,128)(2,1)} %collective-permute-done.w0_ref.refs_14_), channel_id=1, source_target_pairs={{0,2},{2,0},{4,6},{6,4},{8,10},{10,8},{12,14},{14,12},{16,18},{18,... | collective-permute-start | bytes 1179656 | tf_op jit(solution)/shard_map/ppermute | solution.py:849
  25.8 11.0 %collective-permute-start.2 = (bf16[1,3,256,256]{3,2,1,0:T(8,128)(2,1)}, bf16[1,3,256,256]{3,2,1,0:T(8,128)(2,1)}, u32[]{:S(2)}, u32[]{:S(2)}) collective-permute-start(bf16[1,3,256,256]{3,2,1,0:T(8,128)(2,1)} %collective-permute-done.w0_ref.refs_14_), channel_id=1, source_target_pairs={{0,4},{2,6},{4,0},{6,2},{8,12},{10,14},{12,8},{14,10},{16,20},{18,... | collective-permute-start | bytes 1179656 | tf_op jit(solution)/shard_map/ppermute | solution.py:849
  36.8 13.0 %collective-permute-start.5 = (bf16[1,3,256,256]{3,2,1,0:T(8,128)(2,1)}, bf16[1,3,256,256]{3,2,1,0:T(8,128)(2,1)S(1)}, u32[]{:S(2)}, u32[]{:S(2)}) collective-permute-start(bf16[1,3,256,256]{3,2,1,0:T(8,128)(2,1)} %collective-permute-done.2.w1_ref.refs_15_), channel_id=1, source_target_pairs={{0,2},{2,0},{4,6},{6,4},{8,10},{10,8},{12,14},{14,12},{16,18},{18,... | collective-permute-start | bytes 1179656 | tf_op jit(solution)/shard_map/ppermute | solution.py:849
  38.9 11.0 %collective-permute-start.8 = (f32[1,3072]{1,0:T(1,128)S(1)}, f32[1,3072]{1,0:T(1,128)S(1)}, u32[]{:S(2)}, u32[]{:S(2)}) collective-permute-start(f32[1,3072]{1,0:T(1,128)S(1)} %copy-done.12), channel_id=1, source_target_pairs={{0,1},{1,0},{2,3},{3,2},{4,5},{5,4},{6,7},{7,6},{8,9},{9,8},{10,11... | collective-permute-start | bytes 36872 | tf_op jit(solution)/shard_map/ppermute | solution.py:849
  39.2 31.1 %collective-permute-start.11 = (bf16[1,2048,128]{2,1,0:T(8,128)(2,1)}, bf16[1,2048,128]{2,1,0:T(8,128)(2,1)}, u32[]{:S(2)}, u32[]{:S(2)}) collective-permute-start(bf16[1,2048,128]{2,1,0:T(8,128)(2,1)} %get-tuple-element.203), channel_id=1, source_target_pairs={{0,1},{1,0},{2,3},{3,2},{4,5},{5,4},{6,7},{7,6},{8,9},{9,8},{10,11... | collective-permute-start | bytes 1572872 | tf_op jit(solution)/shard_map/ppermute | solution.py:849
  46.1 16.3 %collective-permute-start.9 = (bf16[1,3,256,256]{3,2,1,0:T(8,128)(2,1)}, bf16[1,3,256,256]{3,2,1,0:T(8,128)(2,1)}, u32[]{:S(2)}, u32[]{:S(2)}) collective-permute-start(bf16[1,3,256,256]{3,2,1,0:T(8,128)(2,1)} %collective-permute-done.1.w0_ref.refs_14_), channel_id=1, source_target_pairs={{0,2},{2,0},{4,6},{6,4},{8,10},{10,8},{12,14},{14,12},{16,18},{18,... | collective-permute-start | bytes 1179656 | tf_op jit(solution)/shard_map/ppermute | solution.py:849
  48.6 11.0 %collective-permute-start.4 = (bf16[1,3,256,256]{3,2,1,0:T(8,128)(2,1)}, bf16[1,3,256,256]{3,2,1,0:T(8,128)(2,1)}, u32[]{:S(2)}, u32[]{:S(2)}) collective-permute-start(bf16[1,3,256,256]{3,2,1,0:T(8,128)(2,1)} %collective-permute-done.1.w0_ref.refs_14_), channel_id=1, source_target_pairs={{0,4},{2,6},{4,0},{6,2},{8,12},{10,14},{12,8},{14,10},{16,20},{18,... | collective-permute-start | bytes 1179656 | tf_op jit(solution)/shard_map/ppermute | solution.py:849
  59.6 11.9 %collective-permute-start.10 = (bf16[1,3,256,256]{3,2,1,0:T(8,128)(2,1)}, bf16[1,3,256,256]{3,2,1,0:T(8,128)(2,1)S(1)}, u32[]{:S(2)}, u32[]{:S(2)}) collective-permute-start(bf16[1,3,256,256]{3,2,1,0:T(8,128)(2,1)} %collective-permute-done.4.w1_ref.refs_15_), channel_id=1, source_target_pairs={{0,2},{2,0},{4,6},{6,4},{8,10},{10,8},{12,14},{14,12},{16,18},{18,... | collective-permute-start | bytes 1179656 | tf_op jit(solution)/shard_map/ppermute | solution.py:849
  62.4 18.7 %collective-permute-start.15 = (bf16[1,128,2048]{2,1,0:T(8,128)(2,1)}, bf16[1,128,2048]{2,1,0:T(8,128)(2,1)}, u32[]{:S(2)}, u32[]{:S(2)}) collective-permute-start(bf16[1,128,2048]{2,1,0:T(8,128)(2,1)} %collective-permute-done.6.piece_ref), channel_id=1, source_target_pairs={{0,4},{2,6},{4,0},{6,2},{8,12},{10,14},{12,8},{14,10},{16,20},{18,... | collective-permute-start | bytes 1572872 | tf_op jit(solution)/shard_map/ppermute | solution.py:849
  62.6 18.5 %collective-permute-start.16 = (bf16[1,128,2048]{2,1,0:T(8,128)(2,1)}, bf16[1,128,2048]{2,1,0:T(8,128)(2,1)}, u32[]{:S(2)}, u32[]{:S(2)}) collective-permute-start(bf16[1,128,2048]{2,1,0:T(8,128)(2,1)} %collective-permute-done.6.piece_ref), channel_id=1, source_target_pairs={{0,8},{2,10},{4,12},{6,14},{8,0},{10,2},{12,4},{14,6},{16,24},{18,... | collective-permute-start | bytes 1572872 | tf_op jit(solution)/shard_map/ppermute | solution.py:849
  68.0 16.0 %collective-permute-start.14 = (bf16[1,512,256]{2,1,0:T(8,128)(2,1)}, bf16[1,512,256]{2,1,0:T(8,128)(2,1)}, u32[]{:S(2)}, u32[]{:S(2)}) collective-permute-start(bf16[1,512,256]{2,1,0:T(8,128)(2,1)} %collective-permute-done.12.w1.refs_19_), channel_id=1, source_target_pairs={{0,2},{2,0},{4,6},{6,4},{8,10},{10,8},{12,14},{14,12},{16,18},{18,... | collective-permute-start | bytes 786440 | tf_op jit(solution)/shard_map/ppermute | solution.py:849
  70.3 21.3 %collective-permute-start.17 = (bf16[1,2048,128]{2,1,0:T(8,128)(2,1)}, bf16[1,2048,128]{2,1,0:T(8,128)(2,1)}, u32[]{:S(2)}, u32[]{:S(2)}) collective-permute-start(bf16[1,2048,128]{2,1,0:T(8,128)(2,1)} %collective-permute-done.11.piece_ref), channel_id=1, source_target_pairs={{0,4},{2,6},{4,0},{6,2},{8,12},{10,14},{12,8},{14,10},{16,20},{18,... | collective-permute-start | bytes 1572872 | tf_op jit(solution)/shard_map/ppermute | solution.py:849
  71.5 20.0 %collective-permute-start.18 = (bf16[1,2048,128]{2,1,0:T(8,128)(2,1)}, bf16[1,2048,128]{2,1,0:T(8,128)(2,1)}, u32[]{:S(2)}, u32[]{:S(2)}) collective-permute-start(bf16[1,2048,128]{2,1,0:T(8,128)(2,1)} %collective-permute-done.11.piece_ref), channel_id=1, source_target_pairs={{0,8},{2,10},{4,12},{6,14},{8,0},{10,2},{12,4},{14,6},{16,24},{18,... | collective-permute-start | bytes 1572872 | tf_op jit(solution)/shard_map/ppermute | solution.py:849
  83.1 12.5 %collective-permute-start.19 = (bf16[1,128,1024]{2,1,0:T(8,128)(2,1)}, bf16[1,128,1024]{2,1,0:T(8,128)(2,1)}, u32[]{:S(2)}, u32[]{:S(2)}) collective-permute-start(bf16[1,128,1024]{2,1,0:T(8,128)(2,1)} %get-tuple-element.213), channel_id=1, source_target_pairs={{0,8},{2,10},{4,12},{6,14},{8,0},{10,2},{12,4},{14,6},{16,24},{18,... | collective-permute-start | bytes 786440 | tf_op jit(solution)/shard_map/ppermute | solution.py:849
  83.7 12.3 %collective-permute-start.20 = (bf16[1,128,1024]{2,1,0:T(8,128)(2,1)}, bf16[1,128,1024]{2,1,0:T(8,128)(2,1)}, u32[]{:S(2)}, u32[]{:S(2)}) collective-permute-start(bf16[1,128,1024]{2,1,0:T(8,128)(2,1)} %get-tuple-element.214), channel_id=1, source_target_pairs={{0,4},{2,6},{4,0},{6,2},{8,12},{10,14},{12,8},{14,10},{16,20},{18,... | collective-permute-start | bytes 786440 | tf_op jit(solution)/shard_map/ppermute | solution.py:849
  93.6 21.7 %collective-permute-start.21 = (bf16[1,1024,128]{2,1,0:T(8,128)(2,1)}, bf16[1,1024,128]{2,1,0:T(8,128)(2,1)}, u32[]{:S(2)}, u32[]{:S(2)}) collective-permute-start(bf16[1,1024,128]{2,1,0:T(8,128)(2,1)} %get-tuple-element.218), channel_id=1, source_target_pairs={{0,8},{2,10},{4,12},{6,14},{8,0},{10,2},{12,4},{14,6},{16,24},{18,... | collective-permute-start | bytes 786440 | tf_op jit(solution)/shard_map/ppermute | solution.py:849
  94.4 20.9 %collective-permute-start.22 = (bf16[1,1024,128]{2,1,0:T(8,128)(2,1)}, bf16[1,1024,128]{2,1,0:T(8,128)(2,1)}, u32[]{:S(2)}, u32[]{:S(2)}) collective-permute-start(bf16[1,1024,128]{2,1,0:T(8,128)(2,1)} %get-tuple-element.219), channel_id=1, source_target_pairs={{0,4},{2,6},{4,0},{6,2},{8,12},{10,14},{12,8},{14,10},{16,20},{18,... | collective-permute-start | bytes 786440 | tf_op jit(solution)/shard_map/ppermute | solution.py:849
  99.0 20.1 %collective-permute-start.23 = (bf16[1,512,2048]{2,1,0:T(8,128)(2,1)}, bf16[1,512,2048]{2,1,0:T(8,128)(2,1)}, u32[]{:S(2)}, u32[]{:S(2)}) collective-permute-start(bf16[1,512,2048]{2,1,0:T(8,128)(2,1)} %join_depth.2.up_a.refs_8_), channel_id=1, source_target_pairs={{0,2},{2,0},{4,6},{6,4},{8,10},{10,8},{12,14},{14,12},{16,18},{18,... | collective-permute-start | bytes 6291464 | tf_op jit(solution)/shard_map/ppermute | solution.py:849
  171.6 26.6 %collective-permute-start.25 = (bf16[8,512,512]{2,1,0:T(8,128)(2,1)}, bf16[8,512,512]{2,1,0:T(8,128)(2,1)}, u32[]{:S(2)}, u32[]{:S(2)}) collective-permute-start(bf16[8,512,512]{2,1,0:T(8,128)(2,1)} %get-tuple-element.242), channel_id=1, source_target_pairs={{0,2},{2,0},{4,6},{6,4},{8,10},{10,8},{12,14},{14,12},{16,18},{18,... | collective-permute-start | bytes 12582920 | tf_op jit(solution)/shard_map/ppermute | solution.py:849
  204.6 47.4 %collective-permute-start.27 = (bf16[8,256,512]{2,1,0:T(8,128)(2,1)}, bf16[8,256,512]{2,1,0:T(8,128)(2,1)}, u32[]{:S(2)}, u32[]{:S(2)}) collective-permute-start(bf16[8,256,512]{2,1,0:T(8,128)(2,1)} %get-tuple-element.243), channel_id=1, source_target_pairs={{0,8},{2,10},{4,12},{6,14},{8,0},{10,2},{12,4},{14,6},{16,24},{18,... | collective-permute-start | bytes 6291464 | tf_op jit(solution)/shard_map/ppermute | solution.py:849
  209.7 50.2 %collective-permute-start.29 = (bf16[4,512,512]{2,1,0:T(8,128)(2,1)}, bf16[4,512,512]{2,1,0:T(8,128)(2,1)}, u32[]{:S(2)}, u32[]{:S(2)}) collective-permute-start(bf16[4,512,512]{2,1,0:T(8,128)(2,1)} %combine.21), channel_id=1, source_target_pairs={{0,1},{1,0},{2,3},{3,2},{4,5},{5,4},{6,7},{7,6},{8,9},{9,8},{10,11... | collective-permute-start | bytes 6291464 | tf_op jit(solution)/shard_map/ppermute | solution.py:849
  264.9 33.8 %collective-permute-start.30 = (bf16[4,256,512]{2,1,0:T(8,128)(2,1)}, bf16[4,256,512]{2,1,0:T(8,128)(2,1)}, u32[]{:S(2)}, u32[]{:S(2)}) collective-permute-start(bf16[4,256,512]{2,1,0:T(8,128)(2,1)} %get-tuple-element.265), channel_id=1, source_target_pairs={{0,4},{2,6},{4,0},{6,2},{8,12},{10,14},{12,8},{14,10},{16,20},{18,... | collective-permute-start | bytes 3145736 | tf_op jit(solution)/shard_map/ppermute | solution.py:849
  265.7 45.4 %collective-permute-start.31 = (bf16[8,256,256]{2,1,0:T(8,128)(2,1)}, bf16[8,256,256]{2,1,0:T(8,128)(2,1)}, u32[]{:S(2)}, u32[]{:S(2)}) collective-permute-start(bf16[8,256,256]{2,1,0:T(8,128)(2,1)} %get-tuple-element.263), channel_id=1, source_target_pairs={{0,8},{2,10},{4,12},{6,14},{8,0},{10,2},{12,4},{14,6},{16,24},{18,... | collective-permute-start | bytes 3145736 | tf_op jit(solution)/shard_map/ppermute | solution.py:849
  267.2 46.6 %collective-permute-start.32 = (bf16[8,128,512]{2,1,0:T(8,128)(2,1)}, bf16[8,128,512]{2,1,0:T(8,128)(2,1)}, u32[]{:S(2)}, u32[]{:S(2)}) collective-permute-start(bf16[8,128,512]{2,1,0:T(8,128)(2,1)} %get-tuple-element.260), channel_id=1, source_target_pairs={{0,16},{2,18},{4,20},{6,22},{8,24},{10,26},{12,28},{14,30},{16,0},... | collective-permute-start | bytes 3145736 | tf_op jit(solution)/shard_map/ppermute | solution.py:849
  296.8 19.7 %collective-permute-start.33 = (bf16[8,512,256]{2,1,0:T(8,128)(2,1)}, bf16[8,512,256]{2,1,0:T(8,128)(2,1)}, u32[]{:S(2)}, u32[]{:S(2)}) collective-permute-start(bf16[8,512,256]{2,1,0:T(8,128)(2,1)} %get-tuple-element.282), channel_id=1, source_target_pairs={{0,2},{2,0},{4,6},{6,4},{8,10},{10,8},{12,14},{14,12},{16,18},{18,... | collective-permute-start | bytes 6291464 | tf_op jit(solution)/shard_map/ppermute | solution.py:849
  301.4 22.8 %collective-permute-start.34 = (bf16[4,128,512]{2,1,0:T(8,128)(2,1)}, bf16[4,128,512]{2,1,0:T(8,128)(2,1)}, u32[]{:S(2)}, u32[]{:S(2)}) collective-permute-start(bf16[4,128,512]{2,1,0:T(8,128)(2,1)} %get-tuple-element.271), channel_id=1, source_target_pairs={{0,8},{2,10},{4,12},{6,14},{8,0},{10,2},{12,4},{14,6},{16,24},{18,... | collective-permute-start | bytes 1572872 | tf_op jit(solution)/shard_map/ppermute | solution.py:849
  316.5 14.1 %collective-permute-start.36 = (bf16[8,64,512]{2,1,0:T(8,128)(2,1)}, bf16[8,64,512]{2,1,0:T(8,128)(2,1)}, u32[]{:S(2)}, u32[]{:S(2)}) collective-permute-start(bf16[8,64,512]{2,1,0:T(8,128)(2,1)} %get-tuple-element.280), channel_id=1, source_target_pairs={{0,4},{2,6},{4,0},{6,2},{8,12},{10,14},{12,8},{14,10},{16,20},{18,... | collective-permute-start | bytes 1572872 | tf_op jit(solution)/shard_map/ppermute | solution.py:849
  316.5 11.9 %collective-permute-start.35 = (bf16[4,256,256]{2,1,0:T(8,128)(2,1)}, bf16[4,256,256]{2,1,0:T(8,128)(2,1)}, u32[]{:S(2)}, u32[]{:S(2)}) collective-permute-start(bf16[4,256,256]{2,1,0:T(8,128)(2,1)} %get-tuple-element.287), channel_id=1, source_target_pairs={{0,1},{1,0},{2,3},{3,2},{4,5},{5,4},{6,7},{7,6},{8,9},{9,8},{10,11... | collective-permute-start | bytes 1572872 | tf_op jit(solution)/shard_map/ppermute | solution.py:849
  326.3 14.2 %collective-permute-start.38 = (bf16[4,64,512]{2,1,0:T(8,128)(2,1)}, bf16[4,64,512]{2,1,0:T(8,128)(2,1)}, u32[]{:S(2)}, u32[]{:S(2)}) collective-permute-start(bf16[4,64,512]{2,1,0:T(8,128)(2,1)} %get-tuple-element.285), channel_id=1, source_target_pairs={{0,16},{2,18},{4,20},{6,22},{8,24},{10,26},{12,28},{14,30},{16,0},... | collective-permute-start | bytes 786440 | tf_op jit(solution)/shard_map/ppermute | solution.py:849
  326.3 43.1 %collective-permute-start.40 = (bf16[8,256,256]{2,1,0:T(8,128)(2,1)}, bf16[8,256,256]{2,1,0:T(8,128)(2,1)}, u32[]{:S(2)}, u32[]{:S(2)}) collective-permute-start(bf16[8,256,256]{2,1,0:T(8,128)(2,1)} %get-tuple-element.283), channel_id=1, source_target_pairs={{0,8},{2,10},{4,12},{6,14},{8,0},{10,2},{12,4},{14,6},{16,24},{18,... | collective-permute-start | bytes 3145736 | tf_op jit(solution)/shard_map/ppermute | solution.py:849
  338.2 33.9 %collective-permute-start.41 = (bf16[4,64,256]{2,1,0:T(8,128)(2,1)}, bf16[4,64,256]{2,1,0:T(8,128)(2,1)}, u32[]{:S(2)}, u32[]{:S(2)}) collective-permute-start(bf16[4,64,256]{2,1,0:T(8,128)(2,1)} %get-tuple-element.298), channel_id=1, source_target_pairs={{0,16},{2,18},{4,20},{6,22},{8,24},{10,26},{12,28},{14,30},{16,0},... | collective-permute-start | bytes 393224 | tf_op jit(solution)/shard_map/ppermute | solution.py:849
  342.4 35.4 %collective-permute-start.43 = (bf16[4,64,512]{2,1,0:T(8,128)(2,1)}, bf16[4,64,512]{2,1,0:T(8,128)(2,1)}, u32[]{:S(2)}, u32[]{:S(2)}) collective-permute-start(bf16[4,64,512]{2,1,0:T(8,128)(2,1)} %combine.33.refs_0_), channel_id=1, source_target_pairs={{0,16},{2,18},{4,20},{6,22},{8,24},{10,26},{12,28},{14,30},{16,0},... | collective-permute-start | bytes 786440 | tf_op jit(solution)/shard_map/ppermute | solution.py:849
  344.8 31.1 %collective-permute-start.42 = (bf16[4,64,512]{2,1,0:T(8,128)(2,1)}, bf16[4,64,512]{2,1,0:T(8,128)(2,1)}, u32[]{:S(2)}, u32[]{:S(2)}) collective-permute-start(bf16[4,64,512]{2,1,0:T(8,128)(2,1)} %combine.34.refs_0_), channel_id=1, source_target_pairs={{0,4},{2,6},{4,0},{6,2},{8,12},{10,14},{12,8},{14,10},{16,20},{18,... | collective-permute-start | bytes 786440 | tf_op jit(solution)/shard_map/ppermute | solution.py:849
  374.9 11.2 %collective-permute-start.45 = (bf16[8,128,256]{2,1,0:T(8,128)(2,1)}, bf16[8,128,256]{2,1,0:T(8,128)(2,1)}, u32[]{:S(2)}, u32[]{:S(2)}) collective-permute-start(bf16[8,128,256]{2,1,0:T(8,128)(2,1)} %get-tuple-element.304), channel_id=1, source_target_pairs={{0,4},{2,6},{4,0},{6,2},{8,12},{10,14},{12,8},{14,10},{16,20},{18,... | collective-permute-start | bytes 1572872 | tf_op jit(solution)/shard_map/ppermute | solution.py:849
  379.7 23.9 %collective-permute-start.47 = (bf16[4,128,512]{2,1,0:T(8,128)(2,1)}, bf16[4,128,512]{2,1,0:T(8,128)(2,1)}, u32[]{:S(2)}, u32[]{:S(2)}) collective-permute-start(bf16[4,128,512]{2,1,0:T(8,128)(2,1)} %join_rows.13.refs_0_), channel_id=1, source_target_pairs={{0,8},{2,10},{4,12},{6,14},{8,0},{10,2},{12,4},{14,6},{16,24},{18,... | collective-permute-start | bytes 1572872 | tf_op jit(solution)/shard_map/ppermute | solution.py:849
  379.7 28.6 %collective-permute-start.49 = (bf16[4,128,512]{2,1,0:T(8,128)(2,1)}, bf16[4,128,512]{2,1,0:T(8,128)(2,1)}, u32[]{:S(2)}, u32[]{:S(2)}) collective-permute-start(bf16[4,128,512]{2,1,0:T(8,128)(2,1)} %join_rows.12.refs_0_), channel_id=1, source_target_pairs={{0,16},{2,18},{4,20},{6,22},{8,24},{10,26},{12,28},{14,30},{16,0},... | collective-permute-start | bytes 1572872 | tf_op jit(solution)/shard_map/ppermute | solution.py:849
  394.4 23.1 %collective-permute-start.50 = (bf16[4,256,256]{2,1,0:T(8,128)(2,1)}, bf16[4,256,256]{2,1,0:T(8,128)(2,1)}, u32[]{:S(2)}, u32[]{:S(2)}) collective-permute-start(bf16[4,256,256]{2,1,0:T(8,128)(2,1)} %join_rows.15.refs_0_), channel_id=1, source_target_pairs={{0,8},{2,10},{4,12},{6,14},{8,0},{10,2},{12,4},{14,6},{16,24},{18,... | collective-permute-start | bytes 1572872 | tf_op jit(solution)/shard_map/ppermute | solution.py:849
  395.4 10.5 %collective-permute-start.48 = (bf16[4,128,256]{2,1,0:T(8,128)(2,1)}, bf16[4,128,256]{2,1,0:T(8,128)(2,1)}, u32[]{:S(2)}, u32[]{:S(2)}) collective-permute-start(bf16[4,128,256]{2,1,0:T(8,128)(2,1)} %get-tuple-element.316), channel_id=1, source_target_pairs={{0,1},{1,0},{2,3},{3,2},{4,5},{5,4},{6,7},{7,6},{8,9},{9,8},{10,11... | collective-permute-start | bytes 786440 | tf_op jit(solution)/shard_map/ppermute | solution.py:849
  405.8 23.0 %collective-permute-start.53 = (bf16[4,256,512]{2,1,0:T(8,128)(2,1)}, bf16[4,256,512]{2,1,0:T(8,128)(2,1)}, u32[]{:S(2)}, u32[]{:S(2)}) collective-permute-start(bf16[4,256,512]{2,1,0:T(8,128)(2,1)} %join_rows.16.refs_0_), channel_id=1, source_target_pairs={{0,4},{2,6},{4,0},{6,2},{8,12},{10,14},{12,8},{14,10},{16,20},{18,... | collective-permute-start | bytes 3145736 | tf_op jit(solution)/shard_map/ppermute | solution.py:849
  407.6 17.0 %collective-permute-start.51 = (bf16[4,64,256]{2,1,0:T(8,128)(2,1)}, bf16[4,64,256]{2,1,0:T(8,128)(2,1)}, u32[]{:S(2)}, u32[]{:S(2)}) collective-permute-start(bf16[4,64,256]{2,1,0:T(8,128)(2,1)} %get-tuple-element.317), channel_id=1, source_target_pairs={{0,16},{2,18},{4,20},{6,22},{8,24},{10,26},{12,28},{14,30},{16,0},... | collective-permute-start | bytes 393224 | tf_op jit(solution)/shard_map/ppermute | solution.py:849
  410.6 34.5 %collective-permute-start.56 = (bf16[4,256,512]{2,1,0:T(8,128)(2,1)}, bf16[4,256,512]{2,1,0:T(8,128)(2,1)}, u32[]{:S(2)}, u32[]{:S(2)}) collective-permute-start(bf16[4,256,512]{2,1,0:T(8,128)(2,1)} %join_rows.17.refs_0_), channel_id=1, source_target_pairs={{0,8},{2,10},{4,12},{6,14},{8,0},{10,2},{12,4},{14,6},{16,24},{18,... | collective-permute-start | bytes 3145736 | tf_op jit(solution)/shard_map/ppermute | solution.py:849
  426.3 15.7 %collective-permute-start.54 = (bf16[4,64,256]{2,1,0:T(8,128)(2,1)}, bf16[4,64,256]{2,1,0:T(8,128)(2,1)}, u32[]{:S(2)}, u32[]{:S(2)}) collective-permute-start(bf16[4,64,256]{2,1,0:T(8,128)(2,1)} %combine.39.refs_0_), channel_id=1, source_target_pairs={{0,16},{2,18},{4,20},{6,22},{8,24},{10,26},{12,28},{14,30},{16,0},... | collective-permute-start | bytes 393224 | tf_op jit(solution)/shard_map/ppermute | solution.py:849
  431.9 20.4 %collective-permute-start.55 = (bf16[4,512,512]{2,1,0:T(8,128)(2,1)}, bf16[4,512,512]{2,1,0:T(8,128)(2,1)}, u32[]{:S(2)}, u32[]{:S(2)}) collective-permute-start(bf16[4,512,512]{2,1,0:T(8,128)(2,1)} %join_rows.19.refs_2_), channel_id=1, source_target_pairs={{0,2},{2,0},{4,6},{6,4},{8,10},{10,8},{12,14},{14,12},{16,18},{18,... | collective-permute-start | bytes 6291464 | tf_op jit(solution)/shard_map/ppermute | solution.py:849
  454.2 12.0 %collective-permute-start.59 = (bf16[4,256,256]{2,1,0:T(8,128)(2,1)}, bf16[4,256,256]{2,1,0:T(8,128)(2,1)}, u32[]{:S(2)}, u32[]{:S(2)}) collective-permute-start(bf16[4,256,256]{2,1,0:T(8,128)(2,1)} %join_rows.22.refs_0_), channel_id=1, source_target_pairs={{0,8},{2,10},{4,12},{6,14},{8,0},{10,2},{12,4},{14,6},{16,24},{18,... | collective-permute-start | bytes 1572872 | tf_op jit(solution)/shard_map/ppermute | solution.py:849
  (53 other events, 652.2 us)
Sparse Core Ops, SparseCore 0:
  296.9 66.6 all-gather.2

commit v5 on v4

--- a/solution.py
+++ b/solution.py
@@ -1220,13 +1220,13 @@
     "a",
     "biases",
     "b",
-    "out",
     "up",
     ("other", 0),
+    "out",
     "b",
-    "out",
     "down",
     ("other", 1),
+    "out",
     "up",
     "project",
     "down",

time: 498 us -> 492 us (0.988)
  transfers between devices with their start and end apart: 62 -> 62, of which waited for: 18 -> 20; matrix products, arithmetic and copies ran while one was open for 3% -> 3% of each run, Pallas kernels for 50% -> 50%
where the time goes in v5:
time: 492 us; the launch traced here: 482 us
  Pallas kernels  305 us (62%)
  waiting for transfers between devices  81 us (16%)
  starting transfers between devices  62.1 us (13%)
  local copies, waits for them, and re-layouts  16.5 us (3%)
  between operations  15.1 us (3%)
    pallas_call x47, Pallas kernels, run(): pl.pallas_call(kernel, grid=grid, in_specs=in_specs, out_specs=out_specs,...  266 us
    ppermute x61, waiting for transfers between devices, swap(): lax.ppermute(value, axis, [(place, place ^ distance) for place in range(c...  63.1 us
    ppermute x61, starting transfers between devices, swap(): lax.ppermute(value, axis, [(place, place ^ distance) for place in range(c...  62.1 us
    pallas_call x4, Pallas kernels, heads_forward(): pl.pallas_call(heads_kernel, grid=(pages,), in_specs=[scalar_spec()] + qk...  32.7 us
    all_gather x1, waiting for transfers between devices, gather_small(): lax.all_gather(jnp.concatenate(split + [entry[0] for entry in sums]), ('d...  17.9 us
  transfers between devices with their start and end apart: 62, of which 20 were waited for; matrix products, arithmetic and copies ran while one was open for 3% of the time, Pallas kernels for 50%

profile of v5, /device:TPU:19, one launch (start us, length us, event | category | flops | bytes accessed | tf_op | source)
XLA Modules:
  0.0 482.3 jit_solution(9448766049236878427)
XLA Ops:
  7.9 2.7 take_blocks.2
  12.1 3.2 take_blocks.3
  16.1 8.2 %heads.4 = (bf16[832,1536]{1,0:T(8,128)(2,1)}, bf16[832,512]{1,0:T(8,128)(2,1)}, f32[2,2,4,416]{3,2,1,0:T(4,128)}) custom-call(s32[1]{0:T(128)} %constant.12.clone.1.order_ref, bf16[1,3,1024,512]{3,2,1,0:T(8,128)(2,1)} %refs_6_.3, bf16[1,3,1024,512]{3,2,1,0:T(8,128)(2,1)} %refs_6_.3, bf16[1,3,1024,512]{3,2,1,0:T(8,128)(2,1)} %refs_6_.3, ...), custom_call_target="tpu_custom_call" | custom-call | flops 3519999901696 | bytes 1 | tf_op jit(solution)/shard_map/heads/pallas_call | solution.py:420
  27.1 8.2 %heads.5 = (bf16[832,1536]{1,0:T(8,128)(2,1)}, bf16[832,512]{1,0:T(8,128)(2,1)}, f32[2,2,4,416]{3,2,1,0:T(4,128)}) custom-call(s32[1]{0:T(128)} %constant.12.clone.1.order_ref, bf16[1,3,1024,512]{3,2,1,0:T(8,128)(2,1)} %refs_6_.3, bf16[1,3,1024,512]{3,2,1,0:T(8,128)(2,1)} %refs_6_.3, ...), custom_call_target="tpu_custom_call", output_to_operand_aliasing={{0}: (8, {}), {1}: (9, {}), {2}: (10, {})} | custom-call | flops 3519999901696 | bytes 1 | tf_op jit(solution)/shard_map/heads/pallas_call | solution.py:420
  44.2 8.2 %heads.6 = (bf16[832,1536]{1,0:T(8,128)(2,1)}, bf16[832,512]{1,0:T(8,128)(2,1)}, f32[2,2,4,416]{3,2,1,0:T(4,128)}) custom-call(s32[1]{0:T(128)} %bitcast.order_ref, bf16[1,3,256,256]{3,2,1,0:T(8,128)(2,1)} %collective-permute-done.w0_ref.refs_14_, bf16[1,3,256,256]{3,2,1,0:T(8,128)(2,1)} %collective-permute-done.2.w1_ref.refs_15_, ...), custom_call_target="tpu_custom_call" | custom-call | flops 3519999901696 | bytes 1 | tf_op jit(solution)/shard_map/heads/pallas_call | solution.py:420
  60.1 8.1 %heads.7 = (bf16[832,1536]{1,0:T(8,128)(2,1)}, bf16[832,512]{1,0:T(8,128)(2,1)}, f32[2,2,4,416]{3,2,1,0:T(4,128)}) custom-call(s32[1]{0:T(128)} %bitcast.order_ref, bf16[1,3,256,256]{3,2,1,0:T(8,128)(2,1)} %collective-permute-done.1.w0_ref.refs_14_, ...), custom_call_target="tpu_custom_call", output_to_operand_aliasing={{0}: (8, {}), {1}: (9, {}), {2}: (10, {})} | custom-call | flops 3519999901696 | bytes 1 | tf_op jit(solution)/shard_map/heads/pallas_call | solution.py:420
  69.6 4.6 collective-permute-done.12.w1.refs_19_
  79.9 7.6 %project.1 = (f32[832,1024]{1,0:T(8,128)}, f32[832,1024]{1,0:T(8,128)}, bf16[832,1024]{1,0:T(8,128)(2,1)}) custom-call(s32[1]{0:T(128)} %bitcast.order_ref, bf16[832,512]{1,0:T(8,128)(2,1)} %get-tuple-element.189.a_ref.refs_2_, bf16[832,512]{1,0:T(8,128)(2,1)} %get-tuple-element.209.b_ref.refs_13_, bf16[1,512,1024]{2,1,0:T(8,128)(2,1)} %refs_10_.3, ...), custom_call_target="tpu_custom_call" | custom-call | flops 3080000110592 | bytes 1 | tf_op jit(solution)/shard_map/project/pallas_call | solution.py:334
  91.0 3.0 join_depth.2.up_a.refs_8_
  94.8 14.4 %units.2 = (bf16[832,2048]{1,0:T(8,128)(2,1)}, bf16[832,2048]{1,0:T(8,128)(2,1)}, f32[832,1024]{1,0:T(8,128)}) custom-call(s32[1]{0:T(128)} %constant.12.clone.1.order_ref, bf16[832,1024]{1,0:T(8,128)(2,1)} %get-tuple-element.224.h_ref, bf16[1,1024,2048]{2,1,0:T(8,128)(2,1)} %refs_3_.5, bf16[1,1024,2048]{2,1,0:T(8,128)(2,1)} %refs_3_.5, ...), custom_call_target="tpu_custom_call" | custom-call | flops 6160000221184 | bytes 1 | tf_op jit(solution)/shard_map/units/pallas_call | solution.py:334
  109.2 3.2 join_depth.3.down_a.refs_10_
  113.1 3.8 collective-permute-done.24.down_b.refs_11_
  118.2 14.1 %units.3 = (bf16[832,2048]{1,0:T(8,128)(2,1)}, bf16[832,2048]{1,0:T(8,128)(2,1)}, f32[832,1024]{1,0:T(8,128)}) custom-call(s32[1]{0:T(128)} %bitcast.3.order_ref.core_ref, bf16[832,1024]{1,0:T(8,128)(2,1)} %get-tuple-element.224.h_ref, bf16[1,512,2048]{2,1,0:T(8,128)(2,1)} %join_depth.2.up_a.refs_8_, ...), custom_call_target="tpu_custom_call" | custom-call | flops 6160000221184 | bytes 1 | tf_op jit(solution)/shard_map/units/pallas_call | solution.py:334
  132.3 8.7 %turn.1 = (f32[832,1024]{1,0:T(8,128)}, f32[832,1024]{1,0:T(8,128)}, bf16[832,1024]{1,0:T(8,128)(2,1)}, f32[1,1024]{1,0:T(1,128)}, f32[1,1024]{1,0:T(1,128)}, /*index=5*/f32[1,1024]{1,0:T(1,128)}) custom-call(f32[832,1024]{1,0:T(8,128)} %get-tuple-element.222.a_ref, f32[832,1024]{1,0:T(8,128)} %get-tuple-element.226.b_ref, ...), custom_call_target="tpu_custom_call" | custom-call | flops 3959999954944 | bytes 1 | tf_op jit(solution)/shard_map/turn/pallas_call | solution.py:334
  141.0 24.5 %units_back.2 = (bf16[8,512,512]{2,1,0:T(8,128)(2,1)}, bf16[8,512,512]{2,1,0:T(8,128)(2,1)}, f32[832,1024]{1,0:T(8,128)}, f32[4,1,512]{2,1,0:T(1,128)}) custom-call(s32[1]{0:T(128)} %bitcast.3.order_ref.core_ref, s32[1]{0:T(128)} %bitcast.3.order_ref.core_ref, bf16[832,1024]{1,0:T(8,128)(2,1)} %get-tuple-element.236.g_ref, ...), custom_call_target="tpu_custom_call" | custom-call | flops 9679999598592 | bytes 1 | tf_op jit(solution)/shard_map/units_back/pallas_call | solution.py:334
  165.7 24.1 %units_back.3 = (bf16[8,512,512]{2,1,0:T(8,128)(2,1)}, bf16[8,512,512]{2,1,0:T(8,128)(2,1)}, f32[832,1024]{1,0:T(8,128)}, f32[4,1,512]{2,1,0:T(1,128)}) custom-call(s32[1]{0:T(128)} %bitcast.3.order_ref.core_ref, s32[1]{0:T(128)} %bitcast.3.order_ref.core_ref, bf16[832,1024]{1,0:T(8,128)(2,1)} %get-tuple-element.236.g_ref, ...), custom_call_target="tpu_custom_call" | custom-call | flops 9679999598592 | bytes 1 | tf_op jit(solution)/shard_map/units_back/pallas_call | solution.py:334
  192.2 6.4 %combine.20 = (bf16[8,256,512]{2,1,0:T(8,128)(2,1)}, bf16[4,256,512]{2,1,0:T(8,128)(2,1)}, bf16[4,256,512]{2,1,0:T(8,128)(2,1)}) custom-call(s32[4]{0:T(128)} %pad_add_fusion.word_ref, bf16[8,512,512]{2,1,0:T(8,128)(2,1)} %get-tuple-element.241.refs_0_.refs_2_, bf16[8,512,512]{2,1,0:T(8,128)(2,1)} %collective-permute-done.25.refs_1_.refs_3_, ...), custom_call_target="tpu_custom_call" | custom-call | flops 879999975424 | bytes 1 | tf_op jit(solution)/shard_map/combine/pallas_call | solution.py:334
  199.9 4.1 combine.21
  204.1 8.7 %first_back.1 = (f32[832,1024]{1,0:T(8,128)}, bf16[832,1024]{1,0:T(8,128)(2,1)}, f32[1,1024]{1,0:T(1,128)}, f32[1,1024]{1,0:T(1,128)}, f32[1,1024]{1,0:T(1,128)}) custom-call(f32[832,1024]{1,0:T(8,128)} %get-tuple-element.235.refs_0_, f32[832,1024]{1,0:T(8,128)} %get-tuple-element.237.refs_1_, f32[832,1024]{1,0:T(8,128)} %get-tuple-element.246.refs_2_, ...), custom_call_target="tpu_custom_call" | custom-call | flops 4400000008192 | bytes 1 | tf_op jit(solution)/shard_map/first_back/pallas_call | solution.py:334
  212.8 27.5 %heads_back.2 = (bf16[8,512,256]{2,1,0:T(8,128)(2,1)}, bf16[8,512,256]{2,1,0:T(8,128)(2,1)}, f32[832,1024]{1,0:T(8,128)}, f32[2,1,768]{2,1,0:T(1,128)}) custom-call(s32[1]{0:T(128)} %bitcast.3.order_ref.core_ref, s32[1]{0:T(128)} %bitcast.order_ref, bf16[832,1024]{1,0:T(8,128)(2,1)} %x_ref.8, bf16[832,1024]{1,0:T(8,128)(2,1)} %get-tuple-element.266.g_ref, ...), custom_call_target="tpu_custom_call" | custom-call | flops 11439999811584 | bytes 1 | tf_op jit(solution)/shard_map/heads_back/pallas_call | solution.py:334
  245.9 4.0 combine.22
  249.9 3.9 combine.23
  253.8 4.9 %combine.24 = (bf16[4,256,512]{2,1,0:T(8,128)(2,1)}, bf16[4,256,512]{2,1,0:T(8,128)(2,1)}) custom-call(s32[4]{0:T(128)} %pad_add_fusion.word_ref, bf16[8,512,512]{2,1,0:T(8,128)(2,1)} %get-tuple-element.264.refs_0_, bf16[8,512,512]{2,1,0:T(8,128)(2,1)} %collective-permute-done.26.refs_1_, bf16[4,512,512]{2,1,0:T(8,128)(2,1)} %collective-permute-done.29.refs_2_), custom_call_target="tpu_custom_call" | custom-call | flops 879999975424 | bytes 1 | tf_op jit(solution)/shard_map/combine/pallas_call | solution.py:334
  261.5 27.8 %heads_back.3 = (bf16[8,512,256]{2,1,0:T(8,128)(2,1)}, bf16[8,512,256]{2,1,0:T(8,128)(2,1)}, f32[832,1024]{1,0:T(8,128)}, f32[2,1,768]{2,1,0:T(1,128)}) custom-call(s32[1]{0:T(128)} %bitcast.3.order_ref.core_ref, s32[1]{0:T(128)} %bitcast.order_ref, bf16[832,1024]{1,0:T(8,128)(2,1)} %x_ref.8, bf16[832,1024]{1,0:T(8,128)(2,1)} %get-tuple-element.266.g_ref, ...), custom_call_target="tpu_custom_call" | custom-call | flops 11439999811584 | bytes 1 | tf_op jit(solution)/shard_map/heads_back/pallas_call | solution.py:334
  292.8 2.8 combine.25
  295.8 9.2 %collective-permute-done.31.refs_1_.refs_3_ = bf16[8,256,256]{2,1,0:T(8,128)(2,1)} collective-permute-done((bf16[8,256,256]{2,1,0:T(8,128)(2,1)}, bf16[8,256,256]{2,1,0:T(8,128)(2,1)}, u32[]{:S(2)}, u32[]{:S(2)}) %collective-permute-start.31) | collective-permute-done | bytes 1048608 | tf_op jit(solution)/shard_map/ppermute | solution.py:849
  304.9 2.6 combine.26
  307.6 2.7 combine.27
  310.7 3.9 combine.28
  314.6 3.9 collective-permute-done.34.refs_1_
  327.0 3.4 collective-permute-done.37.refs_1_
  332.1 2.4 collective-permute-start.41
  340.1 17.9 %all-gather.3.cloned.1.call-done = f32[393216]{0:T(1024)} async-done(((f32[12288]{0:T(1024)}), f32[393216]{0:T(1024)}) %all-gather.3.cloned.1.call-update) | async-done | bytes 1572880 | tf_op jit(solution)/shard_map/all_gather | solution.py:1444
  358.0 2.6 reshape.125
  360.6 2.8 collective-permute-done.40.refs_1_.refs_3_
  363.4 2.7 combine.35
  382.0 4.5 collective-permute-done.46.refs_1_
  388.9 9.0 %collective-permute-done.47.refs_1_ = bf16[4,128,512]{2,1,0:T(8,128)(2,1)} collective-permute-done((bf16[4,128,512]{2,1,0:T(8,128)(2,1)}, bf16[4,128,512]{2,1,0:T(8,128)(2,1)}, u32[]{:S(2)}, u32[]{:S(2)}) %collective-permute-start.47) | collective-permute-done | bytes 524320 | tf_op jit(solution)/shard_map/ppermute | solution.py:849
  406.5 5.5 %collective-permute-done.50.refs_1_ = bf16[4,256,256]{2,1,0:T(8,128)(2,1)} collective-permute-done((bf16[4,256,256]{2,1,0:T(8,128)(2,1)}, bf16[4,256,256]{2,1,0:T(8,128)(2,1)}, u32[]{:S(2)}, u32[]{:S(2)}) %collective-permute-start.50) | collective-permute-done | bytes 524320 | tf_op jit(solution)/shard_map/ppermute | solution.py:849
  412.0 2.4 join_rows.18.refs_0_
  420.0 2.9 collective-permute-start.54
  423.8 3.0 join_rows.19.refs_2_
  429.1 6.4 %collective-permute-done.54.refs_1_ = bf16[4,64,256]{2,1,0:T(8,128)(2,1)} collective-permute-done((bf16[4,64,256]{2,1,0:T(8,128)(2,1)}, bf16[4,64,256]{2,1,0:T(8,128)(2,1)}, u32[]{:S(2)}, u32[]{:S(2)}) %collective-permute-start.54) | collective-permute-done | bytes 131104 | tf_op jit(solution)/shard_map/ppermute | solution.py:849
  439.0 3.0 join_rows.21.refs_0_
  442.0 4.3 collective-permute-start.58
  450.4 9.8 %finish.2 = (f32[2048,1024]{1,0:T(8,128)}, f32[1024,2048]{1,0:T(8,128)}) custom-call(s32[1]{0:T(128)} %bitcast.3.order_ref.core_ref, bf16[4,512,512]{2,1,0:T(8,128)(2,1)} %join_rows.21.refs_0_, bf16[4,512,512]{2,1,0:T(8,128)(2,1)} %collective-permute-done.58.refs_1_, bf16[4,512,512]{2,1,0:T(8,128)(2,1)} %join_rows.19.refs_2_, ...), custom_call_target="tpu_custom_call" | custom-call | flops 2640000057344 | bytes 1 | tf_op jit(solution)/shard_map/finish/pallas_call | solution.py:334
  462.6 2.7 collective-permute-start.60
  469.3 5.8 %finish.3 = (f32[3,1024,512]{2,1,0:T(8,128)}, f32[512,1024]{1,0:T(8,128)}) custom-call(s32[1]{0:T(128)} %bitcast.3.order_ref.core_ref, bf16[4,512,256]{2,1,0:T(8,128)(2,1)} %join_rows.18.refs_0_, bf16[4,512,256]{2,1,0:T(8,128)(2,1)} %collective-permute-done.52.refs_1_, bf16[4,512,256]{2,1,0:T(8,128)(2,1)} %join_rows.23.refs_2_, bf16[4,512,256]{2,1,0:T(8,128)(2,1)} %copy-done.30), custom_call_target="tpu_custom_call" | custom-call | flops 2640000057344 | bytes 1 | tf_op jit(solution)/shard_map/finish/pallas_call | solution.py:334
  (238 shorter events, 117.3 us)
Async XLA Ops:
  7.2 350.8 %all-gather.3.cloned.1.call-start = ((), (), s32[]{:S(2)}) async-start(), calls=%async_computation | async-start | bytes 1622016 | tf_op jit(solution)/shard_map/all_gather | solution.py:1444
  10.6 13.7 %collective-permute-start = (bf16[1,3,256,256]{3,2,1,0:T(8,128)(2,1)}, bf16[1,3,256,256]{3,2,1,0:T(8,128)(2,1)}, u32[]{:S(2)}, u32[]{:S(2)}) collective-permute-start(bf16[1,3,256,256]{3,2,1,0:T(8,128)(2,1)} %get-tuple-element.180), channel_id=1, source_target_pairs={{0,1},{1,0},{2,3},{3,2},{4,5},{5,4},{6,7},{7,6},{8,9},{9,8},{10,11... | collective-permute-start | bytes 1179656 | tf_op jit(solution)/shard_map/ppermute | solution.py:849
  10.8 28.4 %collective-permute-start.1 = (bf16[1,3,256,256]{3,2,1,0:T(8,128)(2,1)}, bf16[1,3,256,256]{3,2,1,0:T(8,128)(2,1)}, u32[]{:S(2)}, u32[]{:S(2)}) collective-permute-start(bf16[1,3,256,256]{3,2,1,0:T(8,128)(2,1)} %get-tuple-element.190), channel_id=1, source_target_pairs={{0,1},{1,0},{2,3},{3,2},{4,5},{5,4},{6,7},{7,6},{8,9},{9,8},{10,11... | collective-permute-start | bytes 1179656 | tf_op jit(solution)/shard_map/ppermute | solution.py:849
  15.2 25.3 %collective-permute-start.7 = (bf16[1,128,2048]{2,1,0:T(8,128)(2,1)}, bf16[1,128,2048]{2,1,0:T(8,128)(2,1)}, u32[]{:S(2)}, u32[]{:S(2)}) collective-permute-start(bf16[1,128,2048]{2,1,0:T(8,128)(2,1)} %get-tuple-element.194), channel_id=1, source_target_pairs={{0,1},{1,0},{2,3},{3,2},{4,5},{5,4},{6,7},{7,6},{8,9},{9,8},{10,11... | collective-permute-start | bytes 1572872 | tf_op jit(solution)/shard_map/ppermute | solution.py:849
  24.3 13.4 %collective-permute-start.3 = (bf16[1,3,256,256]{3,2,1,0:T(8,128)(2,1)}, bf16[1,3,256,256]{3,2,1,0:T(8,128)(2,1)}, u32[]{:S(2)}, u32[]{:S(2)}) collective-permute-start(bf16[1,3,256,256]{3,2,1,0:T(8,128)(2,1)} %collective-permute-done.w0_ref.refs_14_), channel_id=1, source_target_pairs={{0,2},{2,0},{4,6},{6,4},{8,10},{10,8},{12,14},{14,12},{16,18},{18,... | collective-permute-start | bytes 1179656 | tf_op jit(solution)/shard_map/ppermute | solution.py:849
  25.9 11.0 %collective-permute-start.2 = (bf16[1,3,256,256]{3,2,1,0:T(8,128)(2,1)}, bf16[1,3,256,256]{3,2,1,0:T(8,128)(2,1)}, u32[]{:S(2)}, u32[]{:S(2)}) collective-permute-start(bf16[1,3,256,256]{3,2,1,0:T(8,128)(2,1)} %collective-permute-done.w0_ref.refs_14_), channel_id=1, source_target_pairs={{0,4},{2,6},{4,0},{6,2},{8,12},{10,14},{12,8},{14,10},{16,20},{18,... | collective-permute-start | bytes 1179656 | tf_op jit(solution)/shard_map/ppermute | solution.py:849
  39.0 13.4 %collective-permute-start.5 = (bf16[1,512,256]{2,1,0:T(8,128)(2,1)}, bf16[1,512,256]{2,1,0:T(8,128)(2,1)}, u32[]{:S(2)}, u32[]{:S(2)}) collective-permute-start(bf16[1,512,256]{2,1,0:T(8,128)(2,1)} %get-tuple-element.182), channel_id=1, source_target_pairs={{0,1},{1,0},{2,3},{3,2},{4,5},{5,4},{6,7},{7,6},{8,9},{9,8},{10,11... | collective-permute-start | bytes 786440 | tf_op jit(solution)/shard_map/ppermute | solution.py:849
  39.2 18.8 %collective-permute-start.11 = (bf16[1,2048,128]{2,1,0:T(8,128)(2,1)}, bf16[1,2048,128]{2,1,0:T(8,128)(2,1)}, u32[]{:S(2)}, u32[]{:S(2)}) collective-permute-start(bf16[1,2048,128]{2,1,0:T(8,128)(2,1)} %get-tuple-element.203), channel_id=1, source_target_pairs={{0,1},{1,0},{2,3},{3,2},{4,5},{5,4},{6,7},{7,6},{8,9},{9,8},{10,11... | collective-permute-start | bytes 1572872 | tf_op jit(solution)/shard_map/ppermute | solution.py:849
  40.6 16.7 %collective-permute-start.9 = (bf16[1,3,256,256]{3,2,1,0:T(8,128)(2,1)}, bf16[1,3,256,256]{3,2,1,0:T(8,128)(2,1)}, u32[]{:S(2)}, u32[]{:S(2)}) collective-permute-start(bf16[1,3,256,256]{3,2,1,0:T(8,128)(2,1)} %collective-permute-done.1.w0_ref.refs_14_), channel_id=1, source_target_pairs={{0,2},{2,0},{4,6},{6,4},{8,10},{10,8},{12,14},{14,12},{16,18},{18,... | collective-permute-start | bytes 1179656 | tf_op jit(solution)/shard_map/ppermute | solution.py:849
  42.2 11.0 %collective-permute-start.4 = (bf16[1,3,256,256]{3,2,1,0:T(8,128)(2,1)}, bf16[1,3,256,256]{3,2,1,0:T(8,128)(2,1)}, u32[]{:S(2)}, u32[]{:S(2)}) collective-permute-start(bf16[1,3,256,256]{3,2,1,0:T(8,128)(2,1)} %collective-permute-done.1.w0_ref.refs_14_), channel_id=1, source_target_pairs={{0,4},{2,6},{4,0},{6,2},{8,12},{10,14},{12,8},{14,10},{16,20},{18,... | collective-permute-start | bytes 1179656 | tf_op jit(solution)/shard_map/ppermute | solution.py:849
  54.7 20.7 %collective-permute-start.15 = (bf16[1,128,2048]{2,1,0:T(8,128)(2,1)}, bf16[1,128,2048]{2,1,0:T(8,128)(2,1)}, u32[]{:S(2)}, u32[]{:S(2)}) collective-permute-start(bf16[1,128,2048]{2,1,0:T(8,128)(2,1)} %collective-permute-done.7.piece_ref), channel_id=1, source_target_pairs={{0,4},{2,6},{4,0},{6,2},{8,12},{10,14},{12,8},{14,10},{16,20},{18,... | collective-permute-start | bytes 1572872 | tf_op jit(solution)/shard_map/ppermute | solution.py:849
  55.9 19.4 %collective-permute-start.16 = (bf16[1,128,2048]{2,1,0:T(8,128)(2,1)}, bf16[1,128,2048]{2,1,0:T(8,128)(2,1)}, u32[]{:S(2)}, u32[]{:S(2)}) collective-permute-start(bf16[1,128,2048]{2,1,0:T(8,128)(2,1)} %collective-permute-done.7.piece_ref), channel_id=1, source_target_pairs={{0,8},{2,10},{4,12},{6,14},{8,0},{10,2},{12,4},{14,6},{16,24},{18,... | collective-permute-start | bytes 1572872 | tf_op jit(solution)/shard_map/ppermute | solution.py:849
  57.2 10.9 %collective-permute-start.13 = (bf16[1,512,256]{2,1,0:T(8,128)(2,1)}, bf16[1,512,256]{2,1,0:T(8,128)(2,1)}, u32[]{:S(2)}, u32[]{:S(2)}) collective-permute-start(bf16[1,512,256]{2,1,0:T(8,128)(2,1)} %collective-permute-done.5.w0.refs_18_), channel_id=1, source_target_pairs={{0,2},{2,0},{4,6},{6,4},{8,10},{10,8},{12,14},{14,12},{16,18},{18,... | collective-permute-start | bytes 786440 | tf_op jit(solution)/shard_map/ppermute | solution.py:849
  58.1 16.1 %collective-permute-start.12 = (bf16[1,512,256]{2,1,0:T(8,128)(2,1)}, bf16[1,512,256]{2,1,0:T(8,128)(2,1)}, u32[]{:S(2)}, u32[]{:S(2)}) collective-permute-start(bf16[1,512,256]{2,1,0:T(8,128)(2,1)} %collective-permute-done.5.w0.refs_18_), channel_id=1, source_target_pairs={{0,4},{2,6},{4,0},{6,2},{8,12},{10,14},{12,8},{14,10},{16,20},{18,... | collective-permute-start | bytes 786440 | tf_op jit(solution)/shard_map/ppermute | solution.py:849
  59.3 28.2 %collective-permute-start.17 = (bf16[1,2048,128]{2,1,0:T(8,128)(2,1)}, bf16[1,2048,128]{2,1,0:T(8,128)(2,1)}, u32[]{:S(2)}, u32[]{:S(2)}) collective-permute-start(bf16[1,2048,128]{2,1,0:T(8,128)(2,1)} %collective-permute-done.11.piece_ref), channel_id=1, source_target_pairs={{0,4},{2,6},{4,0},{6,2},{8,12},{10,14},{12,8},{14,10},{16,20},{18,... | collective-permute-start | bytes 1572872 | tf_op jit(solution)/shard_map/ppermute | solution.py:849
  68.2 19.3 %collective-permute-start.18 = (bf16[1,2048,128]{2,1,0:T(8,128)(2,1)}, bf16[1,2048,128]{2,1,0:T(8,128)(2,1)}, u32[]{:S(2)}, u32[]{:S(2)}) collective-permute-start(bf16[1,2048,128]{2,1,0:T(8,128)(2,1)} %collective-permute-done.11.piece_ref), channel_id=1, source_target_pairs={{0,8},{2,10},{4,12},{6,14},{8,0},{10,2},{12,4},{14,6},{16,24},{18,... | collective-permute-start | bytes 1572872 | tf_op jit(solution)/shard_map/ppermute | solution.py:849
  77.4 12.6 %collective-permute-start.19 = (bf16[1,128,1024]{2,1,0:T(8,128)(2,1)}, bf16[1,128,1024]{2,1,0:T(8,128)(2,1)}, u32[]{:S(2)}, u32[]{:S(2)}) collective-permute-start(bf16[1,128,1024]{2,1,0:T(8,128)(2,1)} %get-tuple-element.213), channel_id=1, source_target_pairs={{0,8},{2,10},{4,12},{6,14},{8,0},{10,2},{12,4},{14,6},{16,24},{18,... | collective-permute-start | bytes 786440 | tf_op jit(solution)/shard_map/ppermute | solution.py:849
  78.7 12.4 %collective-permute-start.20 = (bf16[1,128,1024]{2,1,0:T(8,128)(2,1)}, bf16[1,128,1024]{2,1,0:T(8,128)(2,1)}, u32[]{:S(2)}, u32[]{:S(2)}) collective-permute-start(bf16[1,128,1024]{2,1,0:T(8,128)(2,1)} %get-tuple-element.214), channel_id=1, source_target_pairs={{0,4},{2,6},{4,0},{6,2},{8,12},{10,14},{12,8},{14,10},{16,20},{18,... | collective-permute-start | bytes 786440 | tf_op jit(solution)/shard_map/ppermute | solution.py:849
  89.5 19.7 %collective-permute-start.21 = (bf16[1,1024,128]{2,1,0:T(8,128)(2,1)}, bf16[1,1024,128]{2,1,0:T(8,128)(2,1)}, u32[]{:S(2)}, u32[]{:S(2)}) collective-permute-start(bf16[1,1024,128]{2,1,0:T(8,128)(2,1)} %get-tuple-element.218), channel_id=1, source_target_pairs={{0,8},{2,10},{4,12},{6,14},{8,0},{10,2},{12,4},{14,6},{16,24},{18,... | collective-permute-start | bytes 786440 | tf_op jit(solution)/shard_map/ppermute | solution.py:849
  89.7 19.5 %collective-permute-start.22 = (bf16[1,1024,128]{2,1,0:T(8,128)(2,1)}, bf16[1,1024,128]{2,1,0:T(8,128)(2,1)}, u32[]{:S(2)}, u32[]{:S(2)}) collective-permute-start(bf16[1,1024,128]{2,1,0:T(8,128)(2,1)} %get-tuple-element.219), channel_id=1, source_target_pairs={{0,4},{2,6},{4,0},{6,2},{8,12},{10,14},{12,8},{14,10},{16,20},{18,... | collective-permute-start | bytes 786440 | tf_op jit(solution)/shard_map/ppermute | solution.py:849
  94.0 19.1 %collective-permute-start.23 = (bf16[1,512,2048]{2,1,0:T(8,128)(2,1)}, bf16[1,512,2048]{2,1,0:T(8,128)(2,1)}, u32[]{:S(2)}, u32[]{:S(2)}) collective-permute-start(bf16[1,512,2048]{2,1,0:T(8,128)(2,1)} %join_depth.2.up_a.refs_8_), channel_id=1, source_target_pairs={{0,2},{2,0},{4,6},{6,4},{8,10},{10,8},{12,14},{14,12},{16,18},{18,... | collective-permute-start | bytes 6291464 | tf_op jit(solution)/shard_map/ppermute | solution.py:849
  165.5 26.6 %collective-permute-start.25 = (bf16[8,512,512]{2,1,0:T(8,128)(2,1)}, bf16[8,512,512]{2,1,0:T(8,128)(2,1)}, u32[]{:S(2)}, u32[]{:S(2)}) collective-permute-start(bf16[8,512,512]{2,1,0:T(8,128)(2,1)} %get-tuple-element.242), channel_id=1, source_target_pairs={{0,2},{2,0},{4,6},{6,4},{8,10},{10,8},{12,14},{14,12},{16,18},{18,... | collective-permute-start | bytes 12582920 | tf_op jit(solution)/shard_map/ppermute | solution.py:849
  198.5 47.4 %collective-permute-start.27 = (bf16[8,256,512]{2,1,0:T(8,128)(2,1)}, bf16[8,256,512]{2,1,0:T(8,128)(2,1)}, u32[]{:S(2)}, u32[]{:S(2)}) collective-permute-start(bf16[8,256,512]{2,1,0:T(8,128)(2,1)} %get-tuple-element.243), channel_id=1, source_target_pairs={{0,8},{2,10},{4,12},{6,14},{8,0},{10,2},{12,4},{14,6},{16,24},{18,... | collective-permute-start | bytes 6291464 | tf_op jit(solution)/shard_map/ppermute | solution.py:849
  203.9 49.9 %collective-permute-start.29 = (bf16[4,512,512]{2,1,0:T(8,128)(2,1)}, bf16[4,512,512]{2,1,0:T(8,128)(2,1)}, u32[]{:S(2)}, u32[]{:S(2)}) collective-permute-start(bf16[4,512,512]{2,1,0:T(8,128)(2,1)} %combine.21), channel_id=1, source_target_pairs={{0,1},{1,0},{2,3},{3,2},{4,5},{5,4},{6,7},{7,6},{8,9},{9,8},{10,11... | collective-permute-start | bytes 6291464 | tf_op jit(solution)/shard_map/ppermute | solution.py:849
  258.7 34.1 %collective-permute-start.30 = (bf16[4,256,512]{2,1,0:T(8,128)(2,1)}, bf16[4,256,512]{2,1,0:T(8,128)(2,1)}, u32[]{:S(2)}, u32[]{:S(2)}) collective-permute-start(bf16[4,256,512]{2,1,0:T(8,128)(2,1)} %get-tuple-element.265), channel_id=1, source_target_pairs={{0,4},{2,6},{4,0},{6,2},{8,12},{10,14},{12,8},{14,10},{16,20},{18,... | collective-permute-start | bytes 3145736 | tf_op jit(solution)/shard_map/ppermute | solution.py:849
  260.0 45.0 %collective-permute-start.31 = (bf16[8,256,256]{2,1,0:T(8,128)(2,1)}, bf16[8,256,256]{2,1,0:T(8,128)(2,1)}, u32[]{:S(2)}, u32[]{:S(2)}) collective-permute-start(bf16[8,256,256]{2,1,0:T(8,128)(2,1)} %get-tuple-element.263), channel_id=1, source_target_pairs={{0,8},{2,10},{4,12},{6,14},{8,0},{10,2},{12,4},{14,6},{16,24},{18,... | collective-permute-start | bytes 3145736 | tf_op jit(solution)/shard_map/ppermute | solution.py:849
  261.3 46.3 %collective-permute-start.32 = (bf16[8,128,512]{2,1,0:T(8,128)(2,1)}, bf16[8,128,512]{2,1,0:T(8,128)(2,1)}, u32[]{:S(2)}, u32[]{:S(2)}) collective-permute-start(bf16[8,128,512]{2,1,0:T(8,128)(2,1)} %get-tuple-element.260), channel_id=1, source_target_pairs={{0,16},{2,18},{4,20},{6,22},{8,24},{10,26},{12,28},{14,30},{16,0},... | collective-permute-start | bytes 3145736 | tf_op jit(solution)/shard_map/ppermute | solution.py:849
  290.9 19.7 %collective-permute-start.33 = (bf16[8,512,256]{2,1,0:T(8,128)(2,1)}, bf16[8,512,256]{2,1,0:T(8,128)(2,1)}, u32[]{:S(2)}, u32[]{:S(2)}) collective-permute-start(bf16[8,512,256]{2,1,0:T(8,128)(2,1)} %get-tuple-element.282), channel_id=1, source_target_pairs={{0,2},{2,0},{4,6},{6,4},{8,10},{10,8},{12,14},{14,12},{16,18},{18,... | collective-permute-start | bytes 6291464 | tf_op jit(solution)/shard_map/ppermute | solution.py:849
  295.6 22.9 %collective-permute-start.34 = (bf16[4,128,512]{2,1,0:T(8,128)(2,1)}, bf16[4,128,512]{2,1,0:T(8,128)(2,1)}, u32[]{:S(2)}, u32[]{:S(2)}) collective-permute-start(bf16[4,128,512]{2,1,0:T(8,128)(2,1)} %get-tuple-element.271), channel_id=1, source_target_pairs={{0,8},{2,10},{4,12},{6,14},{8,0},{10,2},{12,4},{14,6},{16,24},{18,... | collective-permute-start | bytes 1572872 | tf_op jit(solution)/shard_map/ppermute | solution.py:849
  310.3 14.4 %collective-permute-start.36 = (bf16[8,64,512]{2,1,0:T(8,128)(2,1)}, bf16[8,64,512]{2,1,0:T(8,128)(2,1)}, u32[]{:S(2)}, u32[]{:S(2)}) collective-permute-start(bf16[8,64,512]{2,1,0:T(8,128)(2,1)} %get-tuple-element.280), channel_id=1, source_target_pairs={{0,4},{2,6},{4,0},{6,2},{8,12},{10,14},{12,8},{14,10},{16,20},{18,... | collective-permute-start | bytes 1572872 | tf_op jit(solution)/shard_map/ppermute | solution.py:849
  310.5 12.0 %collective-permute-start.35 = (bf16[4,256,256]{2,1,0:T(8,128)(2,1)}, bf16[4,256,256]{2,1,0:T(8,128)(2,1)}, u32[]{:S(2)}, u32[]{:S(2)}) collective-permute-start(bf16[4,256,256]{2,1,0:T(8,128)(2,1)} %get-tuple-element.287), channel_id=1, source_target_pairs={{0,1},{1,0},{2,3},{3,2},{4,5},{5,4},{6,7},{7,6},{8,9},{9,8},{10,11... | collective-permute-start | bytes 1572872 | tf_op jit(solution)/shard_map/ppermute | solution.py:849
  320.6 13.9 %collective-permute-start.38 = (bf16[4,64,512]{2,1,0:T(8,128)(2,1)}, bf16[4,64,512]{2,1,0:T(8,128)(2,1)}, u32[]{:S(2)}, u32[]{:S(2)}) collective-permute-start(bf16[4,64,512]{2,1,0:T(8,128)(2,1)} %get-tuple-element.285), channel_id=1, source_target_pairs={{0,16},{2,18},{4,20},{6,22},{8,24},{10,26},{12,28},{14,30},{16,0},... | collective-permute-start | bytes 786440 | tf_op jit(solution)/shard_map/ppermute | solution.py:849
  320.6 42.8 %collective-permute-start.40 = (bf16[8,256,256]{2,1,0:T(8,128)(2,1)}, bf16[8,256,256]{2,1,0:T(8,128)(2,1)}, u32[]{:S(2)}, u32[]{:S(2)}) collective-permute-start(bf16[8,256,256]{2,1,0:T(8,128)(2,1)} %get-tuple-element.283), channel_id=1, source_target_pairs={{0,8},{2,10},{4,12},{6,14},{8,0},{10,2},{12,4},{14,6},{16,24},{18,... | collective-permute-start | bytes 3145736 | tf_op jit(solution)/shard_map/ppermute | solution.py:849
  326.8 10.6 %collective-permute-start.39 = (bf16[4,64,512]{2,1,0:T(8,128)(2,1)}, bf16[4,64,512]{2,1,0:T(8,128)(2,1)}, u32[]{:S(2)}, u32[]{:S(2)}) collective-permute-start(bf16[4,64,512]{2,1,0:T(8,128)(2,1)} %get-tuple-element.301), channel_id=1, source_target_pairs={{0,1},{1,0},{2,3},{3,2},{4,5},{5,4},{6,7},{7,6},{8,9},{9,8},{10,11... | collective-permute-start | bytes 786440 | tf_op jit(solution)/shard_map/ppermute | solution.py:849
  332.1 33.9 %collective-permute-start.41 = (bf16[4,64,256]{2,1,0:T(8,128)(2,1)}, bf16[4,64,256]{2,1,0:T(8,128)(2,1)}, u32[]{:S(2)}, u32[]{:S(2)}) collective-permute-start(bf16[4,64,256]{2,1,0:T(8,128)(2,1)} %get-tuple-element.298), channel_id=1, source_target_pairs={{0,16},{2,18},{4,20},{6,22},{8,24},{10,26},{12,28},{14,30},{16,0},... | collective-permute-start | bytes 393224 | tf_op jit(solution)/shard_map/ppermute | solution.py:849
  336.3 34.9 %collective-permute-start.43 = (bf16[4,64,512]{2,1,0:T(8,128)(2,1)}, bf16[4,64,512]{2,1,0:T(8,128)(2,1)}, u32[]{:S(2)}, u32[]{:S(2)}) collective-permute-start(bf16[4,64,512]{2,1,0:T(8,128)(2,1)} %combine.33.refs_0_), channel_id=1, source_target_pairs={{0,16},{2,18},{4,20},{6,22},{8,24},{10,26},{12,28},{14,30},{16,0},... | collective-permute-start | bytes 786440 | tf_op jit(solution)/shard_map/ppermute | solution.py:849
  339.1 30.2 %collective-permute-start.42 = (bf16[4,64,512]{2,1,0:T(8,128)(2,1)}, bf16[4,64,512]{2,1,0:T(8,128)(2,1)}, u32[]{:S(2)}, u32[]{:S(2)}) collective-permute-start(bf16[4,64,512]{2,1,0:T(8,128)(2,1)} %combine.34.refs_0_), channel_id=1, source_target_pairs={{0,4},{2,6},{4,0},{6,2},{8,12},{10,14},{12,8},{14,10},{16,20},{18,... | collective-permute-start | bytes 786440 | tf_op jit(solution)/shard_map/ppermute | solution.py:849
  368.9 11.0 %collective-permute-start.45 = (bf16[8,128,256]{2,1,0:T(8,128)(2,1)}, bf16[8,128,256]{2,1,0:T(8,128)(2,1)}, u32[]{:S(2)}, u32[]{:S(2)}) collective-permute-start(bf16[8,128,256]{2,1,0:T(8,128)(2,1)} %get-tuple-element.304), channel_id=1, source_target_pairs={{0,4},{2,6},{4,0},{6,2},{8,12},{10,14},{12,8},{14,10},{16,20},{18,... | collective-permute-start | bytes 1572872 | tf_op jit(solution)/shard_map/ppermute | solution.py:849
  373.1 24.8 %collective-permute-start.47 = (bf16[4,128,512]{2,1,0:T(8,128)(2,1)}, bf16[4,128,512]{2,1,0:T(8,128)(2,1)}, u32[]{:S(2)}, u32[]{:S(2)}) collective-permute-start(bf16[4,128,512]{2,1,0:T(8,128)(2,1)} %join_rows.13.refs_0_), channel_id=1, source_target_pairs={{0,8},{2,10},{4,12},{6,14},{8,0},{10,2},{12,4},{14,6},{16,24},{18,... | collective-permute-start | bytes 1572872 | tf_op jit(solution)/shard_map/ppermute | solution.py:849
  373.7 29.0 %collective-permute-start.49 = (bf16[4,128,512]{2,1,0:T(8,128)(2,1)}, bf16[4,128,512]{2,1,0:T(8,128)(2,1)}, u32[]{:S(2)}, u32[]{:S(2)}) collective-permute-start(bf16[4,128,512]{2,1,0:T(8,128)(2,1)} %join_rows.12.refs_0_), channel_id=1, source_target_pairs={{0,16},{2,18},{4,20},{6,22},{8,24},{10,26},{12,28},{14,30},{16,0},... | collective-permute-start | bytes 1572872 | tf_op jit(solution)/shard_map/ppermute | solution.py:849
  388.4 23.6 %collective-permute-start.50 = (bf16[4,256,256]{2,1,0:T(8,128)(2,1)}, bf16[4,256,256]{2,1,0:T(8,128)(2,1)}, u32[]{:S(2)}, u32[]{:S(2)}) collective-permute-start(bf16[4,256,256]{2,1,0:T(8,128)(2,1)} %join_rows.15.refs_0_), channel_id=1, source_target_pairs={{0,8},{2,10},{4,12},{6,14},{8,0},{10,2},{12,4},{14,6},{16,24},{18,... | collective-permute-start | bytes 1572872 | tf_op jit(solution)/shard_map/ppermute | solution.py:849
  388.9 11.3 %collective-permute-start.48 = (bf16[4,128,256]{2,1,0:T(8,128)(2,1)}, bf16[4,128,256]{2,1,0:T(8,128)(2,1)}, u32[]{:S(2)}, u32[]{:S(2)}) collective-permute-start(bf16[4,128,256]{2,1,0:T(8,128)(2,1)} %get-tuple-element.316), channel_id=1, source_target_pairs={{0,1},{1,0},{2,3},{3,2},{4,5},{5,4},{6,7},{7,6},{8,9},{9,8},{10,11... | collective-permute-start | bytes 786440 | tf_op jit(solution)/shard_map/ppermute | solution.py:849
  400.2 23.6 %collective-permute-start.53 = (bf16[4,256,512]{2,1,0:T(8,128)(2,1)}, bf16[4,256,512]{2,1,0:T(8,128)(2,1)}, u32[]{:S(2)}, u32[]{:S(2)}) collective-permute-start(bf16[4,256,512]{2,1,0:T(8,128)(2,1)} %join_rows.16.refs_0_), channel_id=1, source_target_pairs={{0,4},{2,6},{4,0},{6,2},{8,12},{10,14},{12,8},{14,10},{16,20},{18,... | collective-permute-start | bytes 3145736 | tf_op jit(solution)/shard_map/ppermute | solution.py:849
  402.0 16.3 %collective-permute-start.51 = (bf16[4,64,256]{2,1,0:T(8,128)(2,1)}, bf16[4,64,256]{2,1,0:T(8,128)(2,1)}, u32[]{:S(2)}, u32[]{:S(2)}) collective-permute-start(bf16[4,64,256]{2,1,0:T(8,128)(2,1)} %get-tuple-element.317), channel_id=1, source_target_pairs={{0,16},{2,18},{4,20},{6,22},{8,24},{10,26},{12,28},{14,30},{16,0},... | collective-permute-start | bytes 393224 | tf_op jit(solution)/shard_map/ppermute | solution.py:849
  405.0 34.0 %collective-permute-start.56 = (bf16[4,256,512]{2,1,0:T(8,128)(2,1)}, bf16[4,256,512]{2,1,0:T(8,128)(2,1)}, u32[]{:S(2)}, u32[]{:S(2)}) collective-permute-start(bf16[4,256,512]{2,1,0:T(8,128)(2,1)} %join_rows.17.refs_0_), channel_id=1, source_target_pairs={{0,8},{2,10},{4,12},{6,14},{8,0},{10,2},{12,4},{14,6},{16,24},{18,... | collective-permute-start | bytes 3145736 | tf_op jit(solution)/shard_map/ppermute | solution.py:849
  420.0 15.5 %collective-permute-start.54 = (bf16[4,64,256]{2,1,0:T(8,128)(2,1)}, bf16[4,64,256]{2,1,0:T(8,128)(2,1)}, u32[]{:S(2)}, u32[]{:S(2)}) collective-permute-start(bf16[4,64,256]{2,1,0:T(8,128)(2,1)} %combine.39.refs_0_), channel_id=1, source_target_pairs={{0,16},{2,18},{4,20},{6,22},{8,24},{10,26},{12,28},{14,30},{16,0},... | collective-permute-start | bytes 393224 | tf_op jit(solution)/shard_map/ppermute | solution.py:849
  426.8 19.5 %collective-permute-start.55 = (bf16[4,512,512]{2,1,0:T(8,128)(2,1)}, bf16[4,512,512]{2,1,0:T(8,128)(2,1)}, u32[]{:S(2)}, u32[]{:S(2)}) collective-permute-start(bf16[4,512,512]{2,1,0:T(8,128)(2,1)} %join_rows.19.refs_2_), channel_id=1, source_target_pairs={{0,2},{2,0},{4,6},{6,4},{8,10},{10,8},{12,14},{14,12},{16,18},{18,... | collective-permute-start | bytes 6291464 | tf_op jit(solution)/shard_map/ppermute | solution.py:849
  448.2 12.0 %collective-permute-start.59 = (bf16[4,256,256]{2,1,0:T(8,128)(2,1)}, bf16[4,256,256]{2,1,0:T(8,128)(2,1)}, u32[]{:S(2)}, u32[]{:S(2)}) collective-permute-start(bf16[4,256,256]{2,1,0:T(8,128)(2,1)} %join_rows.22.refs_0_), channel_id=1, source_target_pairs={{0,8},{2,10},{4,12},{6,14},{8,0},{10,2},{12,4},{14,6},{16,24},{18,... | collective-permute-start | bytes 1572872 | tf_op jit(solution)/shard_map/ppermute | solution.py:849
  (49 other events, 609.0 us)
Sparse Core Ops, SparseCore 0:
  291.1 66.8 all-gather.2
